TPU v7x, 512 devices: a whole 4x4x16 slice. The times are simulated.
512 devices in a mesh: seq: 256 (over y, x_hi, z, core), head: 2 (over x_lo).
Axes of the slice: x: 4 (x_hi: 2, x_lo: 2; x = x_hi * 2 + x_lo), y: 4, z: 16, core: 2. Of those that a mesh axis runs over, the one named last changes fastest.
Arguments:
- query: bfloat16 [131072, 8, 128], P('seq', 'head'), may hold values from -190 to 190
- key: bfloat16 [131072, 8, 128], P('seq', 'head'), may hold values from -7 to 7
- value: bfloat16 [131072, 8, 128], P('seq', 'head'), may hold values from -6 to 6
- dout: bfloat16 [131072, 8, 128], P('seq', 'head'), may hold values from -6 to 6
Outputs:
- attended: bfloat16 [131072, 8, 128], P('seq', 'head')
- grad_query: bfloat16 [131072, 8, 128], P('seq', 'head')
- grad_key: bfloat16 [131072, 8, 128], P('seq', 'head')
- grad_value: bfloat16 [131072, 8, 128], P('seq', 'head')
All inputs are finite; a program needn't handle non-finite values.
Results may differ from a plain program's by a relative error of at most 0.012.
The roundings to bfloat16 on the way count: a program that leaves them out, or rounds other values in their place, can miss the bound.
Values may be sent and summed in bfloat16 or wider, within the bound.
No kernel may reach another device: no remote copies, remote signals or barrier semaphores. Data moves between devices by JAX's collectives and lax.ppermute only.
A program may use at most 128 MiB of HBM per device.

v0:
```python
import functools
import math

import jax
import jax.numpy as jnp
from jax import lax
from jax.experimental import pallas as pl
from jax.experimental.pallas import tpu as pltpu
from jax.sharding import PartitionSpec as P

BLOCK = 256
LEVELS = 3
CHUNKS = 2
LOG2E = math.log2(math.e)

BF = jnp.bfloat16
F32 = jnp.float32


def passed_along(value, steps):
    count = lax.axis_size("seq")
    initial, last = max(0, -steps), min(count, count - steps)
    return lax.ppermute(value, "seq", [(source, source + steps) for source in range(initial, last)])


def nt(left, right):
    return lax.dot_general(left, right, (((1,), (1,)), ((), ())), preferred_element_type=F32)


def nn(left, right):
    return jnp.dot(left, right, preferred_element_type=F32)


def shape(dims, dtype=BF):
    return jax.ShapeDtypeStruct(dims, dtype)


def params():
    return pltpu.CompilerParams(vmem_limit_bytes=48 * 2**20)


def split_kv_kernel(heads, base, k_ref, v_ref, first, last, *rest):
    coarse, (wide, sums) = rest[:LEVELS], rest[LEVELS:]
    per = first.shape[1]
    span = 2 * first.shape[2]
    for at, ref in enumerate((k_ref, v_ref)):
        wide[...] = ref[...].astype(F32)
        for head in range(per):
            row = base + head
            block = span // 2
            first[at, head] = wide[pl.ds(row, block, stride=heads), :].astype(BF)
            last[at, head] = wide[pl.ds(row + heads * block, block, stride=heads), :].astype(BF)
            size = span // 2
            total = (
                wide[pl.ds(row, size, stride=2 * heads), :]
                + wide[pl.ds(row + heads, size, stride=2 * heads), :]
            )
            for level in range(LEVELS):
                coarse[level][at, head] = (total * (1.0 / 2 ** (level + 1))).astype(BF)
                if level + 1 < LEVELS:
                    sums[pl.ds(0, size), :] = total
                    size //= 2
                    total = sums[pl.ds(0, size, stride=2), :] + sums[pl.ds(1, size, stride=2), :]


def split_kv(k2, v2, heads, base, per, span):
    block = span // 2
    outs = [shape((2, per, block, 128)), shape((2, per, block, 128))]
    outs += [shape((2, per, span // 2 ** (level + 1), 128)) for level in range(LEVELS)]
    return pl.pallas_call(
        functools.partial(split_kv_kernel, heads, base),
        out_shape=outs,
        scratch_shapes=[
            pltpu.VMEM((heads * span, 128), F32),
            pltpu.VMEM((span // 2, 128), F32),
        ],
        compiler_params=params(),
        name="split_kv",
        cost_estimate=pl.CostEstimate(flops=0, bytes_accessed=4 * 2**20, transcendentals=0),
    )(k2, v2)


def split_qd_kernel(heads, q_ref, d_ref, q_out, d_out, rep_out, wide, sums, spread):
    span = q_out.shape[1]
    wide[...] = d_ref[...].astype(F32)
    for head in range(heads):
        d_out[head] = wide[pl.ds(head, span, stride=heads), :].astype(BF)
    wide[...] = q_ref[...].astype(F32)
    for head in range(heads):
        q_out[head] = wide[pl.ds(head, span, stride=heads), :].astype(BF)
        size = span // 2
        total = (
            wide[pl.ds(head, size, stride=2 * heads), :]
            + wide[pl.ds(head + heads, size, stride=2 * heads), :]
        )
        for level in range(LEVELS):
            factor = 2 ** (level + 1)
            mean = (total * (1.0 / factor)).astype(BF).astype(F32)
            for row in range(factor):
                spread[pl.ds(row, size, stride=factor), :] = mean
            rep_out[level, head] = spread[...].astype(BF)
            if level + 1 < LEVELS:
                sums[pl.ds(0, size), :] = total
                size //= 2
                total = sums[pl.ds(0, size, stride=2), :] + sums[pl.ds(1, size, stride=2), :]


def split_qd(q2, d2, heads, span):
    return pl.pallas_call(
        functools.partial(split_qd_kernel, heads),
        out_shape=[
            shape((heads, span, 128)),
            shape((heads, span, 128)),
            shape((LEVELS, heads, span, 128)),
        ],
        scratch_shapes=[
            pltpu.VMEM((heads * span, 128), F32),
            pltpu.VMEM((span // 2, 128), F32),
            pltpu.VMEM((span, 128), F32),
        ],
        compiler_params=params(),
        name="split_qd",
        cost_estimate=pl.CostEstimate(flops=0, bytes_accessed=8 * 2**20, transcendentals=0),
    )(q2, d2)


def attend_kernel(
    count, place_ref, q_ref, d_ref, rep_ref, first, last, before, after, *rest
):
    lows, highs = rest[:LEVELS], rest[LEVELS : 2 * LEVELS]
    (att, gq, own, g_before, g_after) = rest[2 * LEVELS : 2 * LEVELS + 5]
    rest = rest[2 * LEVELS + 5 :]
    g_lows, g_highs = rest[:LEVELS], rest[LEVELS : 2 * LEVELS]
    keys, vals, keys_t, vals_t, scores, grads, probs, dscores, rows, total_q = rest[2 * LEVELS :]
    place = place_ref[0]
    block = first.shape[2]
    scale = 1.0 / math.sqrt(128)
    scale2 = scale * LOG2E

    parts = [(before, place > 0, 0), (first, None, 0), (last, None, 0)]
    for level in range(LEVELS):
        factor = 2 ** (level + 1)
        parts.append((lows[level], place >= factor, level + 1))
        parts.append((highs[level], place < count - factor, level + 1))
    parts.append((after, place < count - 1, 0))
    at = 0
    segments = []
    for ref, ok, level in parts:
        size = ref.shape[2]
        keys[pl.ds(at, size), :] = ref[0, 0]
        vals[pl.ds(at, size), :] = ref[1, 0]
        bias = float(level)
        if ok is not None:
            bias = jnp.where(ok, bias, -jnp.inf).astype(F32)
        segments.append((at, size, bias, level))
        at += size
    keys_t[...] = keys[...].T
    vals_t[...] = vals[...].T

    held = None
    for turn in range(2):
        own_rows = pl.ds(turn * block, block)
        q_blk = q_ref[0, own_rows, :]
        d_blk = d_ref[0, own_rows, :]
        using = [q_blk] + [rep_ref[level, 0, own_rows, :] for level in range(LEVELS)]
        mine = segments[:-1] if turn == 0 else segments[1:]
        base = mine[0][0]
        width = mine[-1][0] + mine[-1][1] - base
        top = None
        for start, size, bias, level in mine:
            s = nt(keys[pl.ds(start, size), :], using[level])
            scores[pl.ds(start - base, size), :] = s
            high = jnp.max(s, axis=0, keepdims=True) * scale2 + bias
            top = high if top is None else jnp.maximum(top, high)
        total = jnp.zeros((1, block), F32)
        acc = jnp.zeros((1, block), F32)
        for start, size, bias, level in mine:
            here = pl.ds(start - base, size)
            e = jnp.exp2(scores[here, :] * scale2 - (top - bias))
            scores[here, :] = e
            total = total + jnp.sum(e, axis=0, keepdims=True)
            dp = nt(vals[pl.ds(start, size), :], d_blk)
            grads[here, :] = dp
            acc = acc + jnp.sum(e * dp, axis=0, keepdims=True)
        inverse = 1.0 / total
        delta = acc * inverse
        for start, size, bias, level in mine:
            here = pl.ds(start - base, size)
            p = scores[here, :] * inverse
            probs[here, :] = p.astype(BF)
            dscores[here, :] = (p * (grads[here, :] - delta)).astype(BF)
        att[0, own_rows, :] = nn(vals_t[:, base : base + width], probs[...]).T.astype(BF)
        gv = nn(probs[...], d_blk)
        pieces = {}
        fine = jnp.zeros((128, block), F32)
        for start, size, bias, level in mine:
            here = pl.ds(start - base, size)
            ds = dscores[here, :]
            gk = nn(ds, using[level]) * scale
            pieces[start] = (gk, gv[start - base : start - base + size])
        fine_at = [(s, z) for s, z, _, level in mine if level == 0]
        for start, size in fine_at:
            fine = fine + nn(keys_t[:, start : start + size], dscores[pl.ds(start - base, size), :])
        total_q[...] = fine.T
        for level in range(1, LEVELS + 1):
            spots = [(s, z) for s, z, _, lev in mine if lev == level]
            start, size = spots[0][0], spots[0][1] + spots[1][1]
            up = nn(keys_t[:, start : start + size], dscores[pl.ds(start - base, size), :])
            rows[...] = up.T
            factor = 2**level
            groups = block // factor
            mean = rows[pl.ds(0, groups, stride=factor), :]
            for row in range(1, factor):
                mean = mean + rows[pl.ds(row, groups, stride=factor), :]
            mean = mean * (1.0 / factor)
            for row in range(factor):
                spot = pl.ds(row, groups, stride=factor)
                total_q[spot, :] = total_q[spot, :] + mean
        gq[0, own_rows, :] = (total_q[...] * scale).astype(BF)
        if turn == 0:
            held = pieces
        else:
            for key, pair in pieces.items():
                if key in held:
                    held[key] = (held[key][0] + pair[0], held[key][1] + pair[1])
                else:
                    held[key] = pair

    places = [(g_before, None), (own, 0), (own, block)]
    for level in range(LEVELS):
        places += [(g_lows[level], None), (g_highs[level], None)]
    places.append((g_after, None))
    for (ref, offset), (start, size, bias, level) in zip(places, segments):
        for which in range(2):
            value = held[start][which]
            if offset is None:
                ref[which, 0] = value.astype(ref.dtype)
            else:
                ref[which, 0, pl.ds(offset, size), :] = value


def attend(place, count, q, d, rep, base, first, last, before, after, lows, highs):
    per, block = first.shape[1], first.shape[2]
    span = 2 * block
    sizes = [x.shape[2] for x in lows]
    columns = 4 * block + 2 * sum(sizes)
    width = columns - block

    def pair(size):
        return pl.BlockSpec((2, 1, size, 128), lambda h: (0, h, 0, 0))

    head_in = pl.BlockSpec((1, span, 128), lambda h: (base + h, 0, 0))
    head_out = pl.BlockSpec((1, span, 128), lambda h: (h, 0, 0))
    flops = 2 * per * span * width * 128 * 6
    return pl.pallas_call(
        functools.partial(attend_kernel, count),
        grid=(per,),
        in_specs=[
            pl.BlockSpec(memory_space=pltpu.SMEM),
            head_in,
            head_in,
            pl.BlockSpec((LEVELS, 1, span, 128), lambda h: (0, base + h, 0, 0)),
        ]
        + [pair(block)] * 4
        + [pair(size) for size in sizes] * 2,
        out_specs=[head_out, head_out, pair(span), pair(block), pair(block)]
        + [pair(size) for size in sizes] * 2,
        out_shape=[
            shape((per, span, 128)),
            shape((per, span, 128)),
            shape((2, per, span, 128), F32),
            shape((2, per, block, 128)),
            shape((2, per, block, 128)),
        ]
        + [shape((2, per, size, 128)) for size in sizes] * 2,
        scratch_shapes=[
            pltpu.VMEM((columns, 128), BF),
            pltpu.VMEM((columns, 128), BF),
            pltpu.VMEM((128, columns), BF),
            pltpu.VMEM((128, columns), BF),
            pltpu.VMEM((width, block), F32),
            pltpu.VMEM((width, block), F32),
            pltpu.VMEM((width, block), BF),
            pltpu.VMEM((width, block), BF),
            pltpu.VMEM((block, 128), F32),
            pltpu.VMEM((block, 128), F32),
        ],
        compiler_params=params(),
        name="attend",
        cost_estimate=pl.CostEstimate(
            flops=flops, bytes_accessed=8 * 2**20, transcendentals=per * span * width
        ),
    )(place, q, d, rep, first, last, before, after, *lows, *highs)


def join_kernel(heads, *refs):
    ins, (wide,) = refs[: 2 * CHUNKS], refs[-1:]
    outs = refs[2 * CHUNKS : 2 * CHUNKS + 2]
    per, span = ins[0].shape[0], ins[0].shape[1]
    for which in range(2):
        for chunk in range(CHUNKS):
            for head in range(per):
                wide[pl.ds(chunk * per + head, span, stride=heads), :] = ins[
                    which * CHUNKS + chunk
                ][head].astype(F32)
        outs[which][...] = wide[...].astype(BF)


def join(atts, gqs, heads, span):
    return pl.pallas_call(
        functools.partial(join_kernel, heads),
        out_shape=[shape((heads * span, 128))] * 2,
        scratch_shapes=[pltpu.VMEM((heads * span, 128), F32)],
        compiler_params=params(),
        name="join",
        cost_estimate=pl.CostEstimate(flops=0, bytes_accessed=4 * 2**20, transcendentals=0),
    )(*atts, *gqs)


def gather_kernel(heads, *refs):
    width = 3 + 2 * LEVELS
    groups = [refs[chunk * width : (chunk + 1) * width] for chunk in range(CHUNKS)]
    outs = refs[CHUNKS * width : CHUNKS * width + 2]
    wide, part, mine = refs[CHUNKS * width + 2 :]
    for which in range(2):
        for chunk, group in enumerate(groups):
            own, right, left = group[:3]
            downs, ups = group[3 : 3 + LEVELS], group[3 + LEVELS :]
            per, span = own.shape[1], own.shape[2]
            block = span // 2
            for head in range(per):
                carry = None
                for level in reversed(range(LEVELS)):
                    size = span // 2 ** (level + 1)
                    value = (
                        downs[level][which, head].astype(F32) + ups[level][which, head].astype(F32)
                    ) * (1.0 / 2 ** (level + 1))
                    if carry is not None:
                        half = size // 2
                        part[pl.ds(0, half, stride=2), :] = carry
                        part[pl.ds(1, half, stride=2), :] = carry
                        value = value + part[pl.ds(0, size), :]
                    carry = value
                mine[pl.ds(0, block), :] = own[which, head, :block] + left[which, head].astype(F32)
                mine[pl.ds(block, block), :] = own[which, head, block:] + right[which, head].astype(
                    F32
                )
                row = chunk * per + head
                for odd in range(2):
                    wide[pl.ds(row + heads * odd, block, stride=2 * heads), :] = (
                        mine[pl.ds(odd, block, stride=2), :] + carry
                    )
        outs[which][...] = wide[...].astype(BF)


def gather(groups, heads, span):
    return pl.pallas_call(
        functools.partial(gather_kernel, heads),
        out_shape=[shape((heads * span, 128))] * 2,
        scratch_shapes=[
            pltpu.VMEM((heads * span, 128), F32),
            pltpu.VMEM((span // 2, 128), F32),
            pltpu.VMEM((span, 128), F32),
        ],
        compiler_params=params(),
        name="gather",
        cost_estimate=pl.CostEstimate(flops=0, bytes_accessed=8 * 2**20, transcendentals=0),
    )(*[x for group in groups for x in group])


def local(query, key, value, dout):
    span, heads, width = query.shape
    per = heads // CHUNKS
    count = lax.axis_size("seq")
    place = jnp.reshape(lax.axis_index("seq"), (1,)).astype(jnp.int32)
    flat = (heads * span, width)
    q2, k2, v2, d2 = (x.reshape(flat) for x in (query, key, value, dout))
    sent = []
    for chunk in range(CHUNKS):
        first, last, *coarse = split_kv(k2, v2, heads, chunk * per, per, span)
        before = passed_along(last, 1)
        after = passed_along(first, -1)
        lows = [passed_along(x, 2 ** (level + 1)) for level, x in enumerate(coarse)]
        highs = [passed_along(x, -(2 ** (level + 1))) for level, x in enumerate(coarse)]
        sent.append((first, last, before, after, lows, highs))
    qh, dh, rep = split_qd(q2, d2, heads, span)
    atts, gqs, groups = [], [], []
    for chunk in range(CHUNKS):
        att, gq, own, g_before, g_after, *grads = attend(
            place, count, qh, dh, rep, chunk * per, *sent[chunk]
        )
        atts.append(att)
        gqs.append(gq)
        right = passed_along(g_before, -1)
        left = passed_along(g_after, 1)
        downs = [passed_along(x, -(2 ** (level + 1))) for level, x in enumerate(grads[:LEVELS])]
        ups = [passed_along(x, 2 ** (level + 1)) for level, x in enumerate(grads[LEVELS:])]
        groups.append([own, right, left, *downs, *ups])
    attended, grad_query = join(atts, gqs, heads, span)
    grad_key, grad_value = gather(groups, heads, span)
    return tuple(
        x.reshape(span, heads, width) for x in (attended, grad_query, grad_key, grad_value)
    )


def solution(mesh):
    placed = P("seq", "head", None)
    return jax.shard_map(
        local,
        mesh=mesh,
        in_specs=(placed,) * 4,
        out_specs=(placed,) * 4,
        check_vma=False,
    )
```

profile of v0, /device:TPU:25, one launch (start us, length us, event | category | flops | bytes accessed | tf_op | source)
XLA Modules:
  0.0 218.9 jit_solution(16559802987344582562)
XLA Ops:
  3.2 14.2 %collective-permute-start.14 = (bf16[2,2,128,128]{3,2,1,0:T(8,128)(2,1)S(1)}, bf16[2,2,128,128]{3,2,1,0:T(8,128)(2,1)S(1)}, u32[]{:S(2)}, u32[]{:S(2)}) collective-permute-start(bf16[2,2,128,128]{3,2,1,0:T(8,128)(2,1)S(1)} %get-tuple-element.55), channel_id=1, source_target_pairs={{8,0},{10,2},{12,4},{14,6},{16,8},{18,10},{20,12},{22,14},{24,16},... | collective-permute-start | bytes 393224 | tf_op jit(solution)/shard_map/ppermute | solution.py:23
  17.4 5.2 %collective-permute-start.15 = (bf16[2,2,64,128]{3,2,1,0:T(8,128)(2,1)S(1)}, bf16[2,2,64,128]{3,2,1,0:T(8,128)(2,1)S(1)}, u32[]{:S(2)}, u32[]{:S(2)}) collective-permute-start(bf16[2,2,64,128]{3,2,1,0:T(8,128)(2,1)S(1)} %get-tuple-element.56), channel_id=1, source_target_pairs={{16,0},{18,2},{20,4},{22,6},{24,8},{26,10},{28,12},{30,14},{32,16}... | collective-permute-start | bytes 196616 | tf_op jit(solution)/shard_map/ppermute | solution.py:23
  22.6 4.0 %collective-permute-start.12 = (bf16[2,2,64,128]{3,2,1,0:T(8,128)(2,1)S(1)}, bf16[2,2,64,128]{3,2,1,0:T(8,128)(2,1)S(1)}, u32[]{:S(2)}, u32[]{:S(2)}) collective-permute-start(bf16[2,2,64,128]{3,2,1,0:T(8,128)(2,1)S(1)} %get-tuple-element.56), channel_id=1, source_target_pairs={{0,16},{2,18},{4,20},{6,22},{8,24},{10,26},{12,28},{14,30},{16,32}... | collective-permute-start | bytes 196616 | tf_op jit(solution)/shard_map/ppermute | solution.py:23
  27.7 8.5 %collective-permute-start.7 = (bf16[2,2,64,128]{3,2,1,0:T(8,128)(2,1)S(1)}, bf16[2,2,64,128]{3,2,1,0:T(8,128)(2,1)S(1)}, u32[]{:S(2)}, u32[]{:S(2)}) collective-permute-start(bf16[2,2,64,128]{3,2,1,0:T(8,128)(2,1)S(1)} %get-tuple-element.50), channel_id=1, source_target_pairs={{16,0},{18,2},{20,4},{22,6},{24,8},{26,10},{28,12},{30,14},{32,16}... | collective-permute-start | bytes 196616 | tf_op jit(solution)/shard_map/ppermute | solution.py:23
  36.2 1.9 collective-permute-start.4
  41.3 3.9 %collective-permute-start.9 = (bf16[2,2,256,128]{3,2,1,0:T(8,128)(2,1)S(1)}, bf16[2,2,256,128]{3,2,1,0:T(8,128)(2,1)S(1)}, u32[]{:S(2)}, u32[]{:S(2)}) collective-permute-start(bf16[2,2,256,128]{3,2,1,0:T(8,128)(2,1)S(1)} %get-tuple-element.52.first), channel_id=1, source_target_pairs={{2,0},{4,2},{6,4},{8,6},{10,8},{12,10},{14,12},{16,14},{18,16},{20... | collective-permute-start | bytes 786440 | tf_op jit(solution)/shard_map/ppermute | solution.py:23
  45.9 2.5 %collective-permute-start.8 = (bf16[2,2,256,128]{3,2,1,0:T(8,128)(2,1)S(1)}, bf16[2,2,256,128]{3,2,1,0:T(8,128)(2,1)S(1)}, u32[]{:S(2)}, u32[]{:S(2)}) collective-permute-start(bf16[2,2,256,128]{3,2,1,0:T(8,128)(2,1)S(1)} %get-tuple-element.53.last), channel_id=1, source_target_pairs={{0,2},{2,4},{4,6},{6,8},{8,10},{10,12},{12,14},{14,16},{16,18},{18... | collective-permute-start | bytes 786440 | tf_op jit(solution)/shard_map/ppermute | solution.py:23
  49.3 11.6 %collective-permute-start.13 = (bf16[2,2,256,128]{3,2,1,0:T(8,128)(2,1)S(1)}, bf16[2,2,256,128]{3,2,1,0:T(8,128)(2,1)S(1)}, u32[]{:S(2)}, u32[]{:S(2)}) collective-permute-start(bf16[2,2,256,128]{3,2,1,0:T(8,128)(2,1)S(1)} %get-tuple-element.54), channel_id=1, source_target_pairs={{4,0},{6,2},{8,4},{10,6},{12,8},{14,10},{16,12},{18,14},{20,16},{2... | collective-permute-start | bytes 786440 | tf_op jit(solution)/shard_map/ppermute | solution.py:23
  61.0 1.9 collective-permute-start.10
  63.6 3.1 %collective-permute-start.6 = (bf16[2,2,128,128]{3,2,1,0:T(8,128)(2,1)}, bf16[2,2,128,128]{3,2,1,0:T(8,128)(2,1)S(1)}, u32[]{:S(2)}, u32[]{:S(2)}) collective-permute-start(bf16[2,2,128,128]{3,2,1,0:T(8,128)(2,1)} %get-tuple-element.49), channel_id=1, source_target_pairs={{8,0},{10,2},{12,4},{14,6},{16,8},{18,10},{20,12},{22,14},{24,16},... | collective-permute-start | bytes 393224 | tf_op jit(solution)/shard_map/ppermute | solution.py:23
  66.6 4.7 %collective-permute-done.6.rest_4_ = bf16[2,2,128,128]{3,2,1,0:T(8,128)(2,1)S(1)} collective-permute-done((bf16[2,2,128,128]{3,2,1,0:T(8,128)(2,1)}, bf16[2,2,128,128]{3,2,1,0:T(8,128)(2,1)S(1)}, u32[]{:S(2)}, u32[]{:S(2)}) %collective-permute-start.6) | collective-permute-done | bytes 131104 | tf_op jit(solution)/shard_map/ppermute | solution.py:23
  74.0 3.6 %collective-permute-start = (bf16[2,2,256,128]{3,2,1,0:T(8,128)(2,1)S(1)}, bf16[2,2,256,128]{3,2,1,0:T(8,128)(2,1)S(1)}, u32[]{:S(2)}, u32[]{:S(2)}) collective-permute-start(bf16[2,2,256,128]{3,2,1,0:T(8,128)(2,1)S(1)} %get-tuple-element.47.last), channel_id=1, source_target_pairs={{0,2},{2,4},{4,6},{6,8},{8,10},{10,12},{12,14},{14,16},{16,18},{18... | collective-permute-start | bytes 786440 | tf_op jit(solution)/shard_map/ppermute | solution.py:23
  78.3 15.9 %collective-permute-start.5 = (bf16[2,2,256,128]{3,2,1,0:T(8,128)(2,1)S(1)}, bf16[2,2,256,128]{3,2,1,0:T(8,128)(2,1)}, u32[]{:S(2)}, u32[]{:S(2)}) collective-permute-start(bf16[2,2,256,128]{3,2,1,0:T(8,128)(2,1)S(1)} %get-tuple-element.48), channel_id=1, source_target_pairs={{4,0},{6,2},{8,4},{10,6},{12,8},{14,10},{16,12},{18,14},{20,16},{2... | collective-permute-start | bytes 786440 | tf_op jit(solution)/shard_map/ppermute | solution.py:23
  105.4 9.3 %attend.3 = (bf16[2,512,128]{2,1,0:T(8,128)(2,1)S(1)}, bf16[2,512,128]{2,1,0:T(8,128)(2,1)S(1)}, f32[2,2,512,128]{3,2,1,0:T(8,128)S(1)}, bf16[2,2,256,128]{3,2,1...) custom-call(s32[1]{0:T(128)} %bitcast.place_ref, ...), custom_call_target="tpu_custom_call" | custom-call | flops 2617245696 | bytes 8388608 | tf_op jit(solution)/shard_map/attend/pallas_call | solution.py:255
  114.7 5.2 %collective-permute-start.28 = (bf16[2,2,64,128]{3,2,1,0:T(8,128)(2,1)S(1)}, bf16[2,2,64,128]{3,2,1,0:T(8,128)(2,1)S(1)}, u32[]{:S(2)}, u32[]{:S(2)}) collective-permute-start(bf16[2,2,64,128]{3,2,1,0:T(8,128)(2,1)S(1)} %get-tuple-element.76), channel_id=1, source_target_pairs={{16,0},{18,2},{20,4},{22,6},{24,8},{26,10},{28,12},{30,14},{32,16}... | collective-permute-start | bytes 196616 | tf_op jit(solution)/shard_map/ppermute | solution.py:23
  119.9 4.0 %collective-permute-start.31 = (bf16[2,2,64,128]{3,2,1,0:T(8,128)(2,1)S(1)}, bf16[2,2,64,128]{3,2,1,0:T(8,128)(2,1)S(1)}, u32[]{:S(2)}, u32[]{:S(2)}) collective-permute-start(bf16[2,2,64,128]{3,2,1,0:T(8,128)(2,1)S(1)} %get-tuple-element.79), channel_id=1, source_target_pairs={{0,16},{2,18},{4,20},{6,22},{8,24},{10,26},{12,28},{14,30},{16,32}... | collective-permute-start | bytes 196616 | tf_op jit(solution)/shard_map/ppermute | solution.py:23
  124.0 9.4 %attend.2 = (bf16[2,512,128]{2,1,0:T(8,128)(2,1)S(1)}, bf16[2,512,128]{2,1,0:T(8,128)(2,1)S(1)}, f32[2,2,512,128]{3,2,1,0:T(8,128)S(1)}, bf16[2,2,256,128]{3,2,1...) custom-call(s32[1]{0:T(128)} %bitcast.place_ref, ...), custom_call_target="tpu_custom_call" | custom-call | flops 2617245696 | bytes 8388608 | tf_op jit(solution)/shard_map/attend/pallas_call | solution.py:255
  133.4 8.4 %collective-permute-start.20 = (bf16[2,2,64,128]{3,2,1,0:T(8,128)(2,1)S(1)}, bf16[2,2,64,128]{3,2,1,0:T(8,128)(2,1)S(1)}, u32[]{:S(2)}, u32[]{:S(2)}) collective-permute-start(bf16[2,2,64,128]{3,2,1,0:T(8,128)(2,1)S(1)} %get-tuple-element.67), channel_id=1, source_target_pairs={{16,0},{18,2},{20,4},{22,6},{24,8},{26,10},{28,12},{30,14},{32,16}... | collective-permute-start | bytes 196616 | tf_op jit(solution)/shard_map/ppermute | solution.py:23
  141.8 1.9 collective-permute-start.23
  143.7 14.2 %collective-permute-start.27 = (bf16[2,2,128,128]{3,2,1,0:T(8,128)(2,1)S(1)}, bf16[2,2,128,128]{3,2,1,0:T(8,128)(2,1)S(1)}, u32[]{:S(2)}, u32[]{:S(2)}) collective-permute-start(bf16[2,2,128,128]{3,2,1,0:T(8,128)(2,1)S(1)} %get-tuple-element.75), channel_id=1, source_target_pairs={{8,0},{10,2},{12,4},{14,6},{16,8},{18,10},{20,12},{22,14},{24,16},... | collective-permute-start | bytes 393224 | tf_op jit(solution)/shard_map/ppermute | solution.py:23
  158.0 1.9 collective-permute-start.30
  159.9 1.9 collective-permute-start.24
  161.8 3.6 %collective-permute-start.25 = (bf16[2,2,256,128]{3,2,1,0:T(8,128)(2,1)S(1)}, bf16[2,2,256,128]{3,2,1,0:T(8,128)(2,1)S(1)}, u32[]{:S(2)}, u32[]{:S(2)}) collective-permute-start(bf16[2,2,256,128]{3,2,1,0:T(8,128)(2,1)S(1)} %get-tuple-element.73), channel_id=1, source_target_pairs={{0,2},{2,4},{4,6},{6,8},{8,10},{10,12},{12,14},{14,16},{16,18},{18... | collective-permute-start | bytes 786440 | tf_op jit(solution)/shard_map/ppermute | solution.py:23
  165.5 12.4 %collective-permute-start.26 = (bf16[2,2,256,128]{3,2,1,0:T(8,128)(2,1)S(1)}, bf16[2,2,256,128]{3,2,1,0:T(8,128)(2,1)S(1)}, u32[]{:S(2)}, u32[]{:S(2)}) collective-permute-start(bf16[2,2,256,128]{3,2,1,0:T(8,128)(2,1)S(1)} %get-tuple-element.74), channel_id=1, source_target_pairs={{4,0},{6,2},{8,4},{10,6},{12,8},{14,10},{16,12},{18,14},{20,16},{2... | collective-permute-start | bytes 786440 | tf_op jit(solution)/shard_map/ppermute | solution.py:23
  177.9 1.9 collective-permute-start.19
  179.8 4.3 %collective-permute-start.22 = (bf16[2,2,128,128]{3,2,1,0:T(8,128)(2,1)S(1)}, bf16[2,2,128,128]{3,2,1,0:T(8,128)(2,1)S(1)}, u32[]{:S(2)}, u32[]{:S(2)}) collective-permute-start(bf16[2,2,128,128]{3,2,1,0:T(8,128)(2,1)S(1)} %get-tuple-element.69), channel_id=1, source_target_pairs={{0,8},{2,10},{4,12},{6,14},{8,16},{10,18},{12,20},{14,22},{16,24},... | collective-permute-start | bytes 393224 | tf_op jit(solution)/shard_map/ppermute | solution.py:23
  187.3 3.7 %collective-permute-done.22.refs_7_ = bf16[2,2,128,128]{3,2,1,0:T(8,128)(2,1)S(1)} collective-permute-done((bf16[2,2,128,128]{3,2,1,0:T(8,128)(2,1)S(1)}, bf16[2,2,128,128]{3,2,1,0:T(8,128)(2,1)S(1)}, u32[]{:S(2)}, u32[]{:S(2)}) %collective-permute-start.22) | collective-permute-done | bytes 131104 | tf_op jit(solution)/shard_map/ppermute | solution.py:23
  193.0 3.6 %collective-permute-start.17 = (bf16[2,2,256,128]{3,2,1,0:T(8,128)(2,1)S(1)}, bf16[2,2,256,128]{3,2,1,0:T(8,128)(2,1)S(1)}, u32[]{:S(2)}, u32[]{:S(2)}) collective-permute-start(bf16[2,2,256,128]{3,2,1,0:T(8,128)(2,1)S(1)} %get-tuple-element.64), channel_id=1, source_target_pairs={{0,2},{2,4},{4,6},{6,8},{8,10},{10,12},{12,14},{14,16},{16,18},{18... | collective-permute-start | bytes 786440 | tf_op jit(solution)/shard_map/ppermute | solution.py:23
  196.6 8.7 %collective-permute-start.18 = (bf16[2,2,256,128]{3,2,1,0:T(8,128)(2,1)S(1)}, bf16[2,2,256,128]{3,2,1,0:T(8,128)(2,1)S(1)}, u32[]{:S(2)}, u32[]{:S(2)}) collective-permute-start(bf16[2,2,256,128]{3,2,1,0:T(8,128)(2,1)S(1)} %get-tuple-element.65), channel_id=1, source_target_pairs={{4,0},{6,2},{8,4},{10,6},{12,8},{14,10},{16,12},{18,14},{20,16},{2... | collective-permute-start | bytes 786440 | tf_op jit(solution)/shard_map/ppermute | solution.py:23
  205.3 1.9 collective-permute-start.21
  208.6 8.3 %collective-permute-done.21.refs_6_ = bf16[2,2,256,128]{3,2,1,0:T(8,128)(2,1)S(1)} collective-permute-done((bf16[2,2,256,128]{3,2,1,0:T(8,128)(2,1)S(1)}, bf16[2,2,256,128]{3,2,1,0:T(8,128)(2,1)S(1)}, u32[]{:S(2)}, u32[]{:S(2)}) %collective-permute-start.21) | collective-permute-done | bytes 262176 | tf_op jit(solution)/shard_map/ppermute | solution.py:23
  217.0 1.9 gather.1
  (81 shorter events, 29.8 us)
Async XLA Ops:
  3.2 57.8 %collective-permute-start.14 = (bf16[2,2,128,128]{3,2,1,0:T(8,128)(2,1)S(1)}, bf16[2,2,128,128]{3,2,1,0:T(8,128)(2,1)S(1)}, u32[]{:S(2)}, u32[]{:S(2)}) collective-permute-start(bf16[2,2,128,128]{3,2,1,0:T(8,128)(2,1)S(1)} %get-tuple-element.55), channel_id=1, source_target_pairs={{8,0},{10,2},{12,4},{14,6},{16,8},{18,10},{20,12},{22,14},{24,16},... | collective-permute-start | bytes 393224 | tf_op jit(solution)/shard_map/ppermute | solution.py:23
  17.4 20.7 %collective-permute-start.15 = (bf16[2,2,64,128]{3,2,1,0:T(8,128)(2,1)S(1)}, bf16[2,2,64,128]{3,2,1,0:T(8,128)(2,1)S(1)}, u32[]{:S(2)}, u32[]{:S(2)}) collective-permute-start(bf16[2,2,64,128]{3,2,1,0:T(8,128)(2,1)S(1)} %get-tuple-element.56), channel_id=1, source_target_pairs={{16,0},{18,2},{20,4},{22,6},{24,8},{26,10},{28,12},{30,14},{32,16}... | collective-permute-start | bytes 196616 | tf_op jit(solution)/shard_map/ppermute | solution.py:23
  22.6 18.1 %collective-permute-start.12 = (bf16[2,2,64,128]{3,2,1,0:T(8,128)(2,1)S(1)}, bf16[2,2,64,128]{3,2,1,0:T(8,128)(2,1)S(1)}, u32[]{:S(2)}, u32[]{:S(2)}) collective-permute-start(bf16[2,2,64,128]{3,2,1,0:T(8,128)(2,1)S(1)} %get-tuple-element.56), channel_id=1, source_target_pairs={{0,16},{2,18},{4,20},{6,22},{8,24},{10,26},{12,28},{14,30},{16,32}... | collective-permute-start | bytes 196616 | tf_op jit(solution)/shard_map/ppermute | solution.py:23
  27.7 17.5 %collective-permute-start.7 = (bf16[2,2,64,128]{3,2,1,0:T(8,128)(2,1)S(1)}, bf16[2,2,64,128]{3,2,1,0:T(8,128)(2,1)S(1)}, u32[]{:S(2)}, u32[]{:S(2)}) collective-permute-start(bf16[2,2,64,128]{3,2,1,0:T(8,128)(2,1)S(1)} %get-tuple-element.50), channel_id=1, source_target_pairs={{16,0},{18,2},{20,4},{22,6},{24,8},{26,10},{28,12},{30,14},{32,16}... | collective-permute-start | bytes 196616 | tf_op jit(solution)/shard_map/ppermute | solution.py:23
  36.2 12.5 %collective-permute-start.4 = (bf16[2,2,64,128]{3,2,1,0:T(8,128)(2,1)S(1)}, bf16[2,2,64,128]{3,2,1,0:T(8,128)(2,1)S(1)}, u32[]{:S(2)}, u32[]{:S(2)}) collective-permute-start(bf16[2,2,64,128]{3,2,1,0:T(8,128)(2,1)S(1)} %get-tuple-element.50), channel_id=1, source_target_pairs={{0,16},{2,18},{4,20},{6,22},{8,24},{10,26},{12,28},{14,30},{16,32}... | collective-permute-start | bytes 196616 | tf_op jit(solution)/shard_map/ppermute | solution.py:23
  38.8 24.1 %collective-permute-start.11 = (bf16[2,2,128,128]{3,2,1,0:T(8,128)(2,1)S(1)}, bf16[2,2,128,128]{3,2,1,0:T(8,128)(2,1)S(1)}, u32[]{:S(2)}, u32[]{:S(2)}) collective-permute-start(bf16[2,2,128,128]{3,2,1,0:T(8,128)(2,1)S(1)} %get-tuple-element.55), channel_id=1, source_target_pairs={{0,8},{2,10},{4,12},{6,14},{8,16},{10,18},{12,20},{14,22},{16,24},... | collective-permute-start | bytes 393224 | tf_op jit(solution)/shard_map/ppermute | solution.py:23
  41.3 32.6 %collective-permute-start.9 = (bf16[2,2,256,128]{3,2,1,0:T(8,128)(2,1)S(1)}, bf16[2,2,256,128]{3,2,1,0:T(8,128)(2,1)S(1)}, u32[]{:S(2)}, u32[]{:S(2)}) collective-permute-start(bf16[2,2,256,128]{3,2,1,0:T(8,128)(2,1)S(1)} %get-tuple-element.52.first), channel_id=1, source_target_pairs={{2,0},{4,2},{6,4},{8,6},{10,8},{12,10},{14,12},{16,14},{18,16},{20... | collective-permute-start | bytes 786440 | tf_op jit(solution)/shard_map/ppermute | solution.py:23
  45.9 31.7 %collective-permute-start.8 = (bf16[2,2,256,128]{3,2,1,0:T(8,128)(2,1)S(1)}, bf16[2,2,256,128]{3,2,1,0:T(8,128)(2,1)S(1)}, u32[]{:S(2)}, u32[]{:S(2)}) collective-permute-start(bf16[2,2,256,128]{3,2,1,0:T(8,128)(2,1)S(1)} %get-tuple-element.53.last), channel_id=1, source_target_pairs={{0,2},{2,4},{4,6},{6,8},{8,10},{10,12},{12,14},{14,16},{16,18},{18... | collective-permute-start | bytes 786440 | tf_op jit(solution)/shard_map/ppermute | solution.py:23
  49.3 44.9 %collective-permute-start.13 = (bf16[2,2,256,128]{3,2,1,0:T(8,128)(2,1)S(1)}, bf16[2,2,256,128]{3,2,1,0:T(8,128)(2,1)S(1)}, u32[]{:S(2)}, u32[]{:S(2)}) collective-permute-start(bf16[2,2,256,128]{3,2,1,0:T(8,128)(2,1)S(1)} %get-tuple-element.54), channel_id=1, source_target_pairs={{4,0},{6,2},{8,4},{10,6},{12,8},{14,10},{16,12},{18,14},{20,16},{2... | collective-permute-start | bytes 786440 | tf_op jit(solution)/shard_map/ppermute | solution.py:23
  61.0 38.0 %collective-permute-start.10 = (bf16[2,2,256,128]{3,2,1,0:T(8,128)(2,1)S(1)}, bf16[2,2,256,128]{3,2,1,0:T(8,128)(2,1)}, u32[]{:S(2)}, u32[]{:S(2)}) collective-permute-start(bf16[2,2,256,128]{3,2,1,0:T(8,128)(2,1)S(1)} %get-tuple-element.54), channel_id=1, source_target_pairs={{0,4},{2,6},{4,8},{6,10},{8,12},{10,14},{12,16},{14,18},{16,20},{1... | collective-permute-start | bytes 786440 | tf_op jit(solution)/shard_map/ppermute | solution.py:23
  63.6 7.8 %collective-permute-start.6 = (bf16[2,2,128,128]{3,2,1,0:T(8,128)(2,1)}, bf16[2,2,128,128]{3,2,1,0:T(8,128)(2,1)S(1)}, u32[]{:S(2)}, u32[]{:S(2)}) collective-permute-start(bf16[2,2,128,128]{3,2,1,0:T(8,128)(2,1)} %get-tuple-element.49), channel_id=1, source_target_pairs={{8,0},{10,2},{12,4},{14,6},{16,8},{18,10},{20,12},{22,14},{24,16},... | collective-permute-start | bytes 393224 | tf_op jit(solution)/shard_map/ppermute | solution.py:23
  72.0 47.8 %collective-permute-start.1 = (bf16[2,2,256,128]{3,2,1,0:T(8,128)(2,1)S(1)}, bf16[2,2,256,128]{3,2,1,0:T(8,128)(2,1)S(1)}, u32[]{:S(2)}, u32[]{:S(2)}) collective-permute-start(bf16[2,2,256,128]{3,2,1,0:T(8,128)(2,1)S(1)} %get-tuple-element.46.first), channel_id=1, source_target_pairs={{2,0},{4,2},{6,4},{8,6},{10,8},{12,10},{14,12},{16,14},{18,16},{20... | collective-permute-start | bytes 786440 | tf_op jit(solution)/shard_map/ppermute | solution.py:23
  74.0 50.0 %collective-permute-start = (bf16[2,2,256,128]{3,2,1,0:T(8,128)(2,1)S(1)}, bf16[2,2,256,128]{3,2,1,0:T(8,128)(2,1)S(1)}, u32[]{:S(2)}, u32[]{:S(2)}) collective-permute-start(bf16[2,2,256,128]{3,2,1,0:T(8,128)(2,1)S(1)} %get-tuple-element.47.last), channel_id=1, source_target_pairs={{0,2},{2,4},{4,6},{6,8},{8,10},{10,12},{12,14},{14,16},{16,18},{18... | collective-permute-start | bytes 786440 | tf_op jit(solution)/shard_map/ppermute | solution.py:23
  78.3 45.6 %collective-permute-start.5 = (bf16[2,2,256,128]{3,2,1,0:T(8,128)(2,1)S(1)}, bf16[2,2,256,128]{3,2,1,0:T(8,128)(2,1)}, u32[]{:S(2)}, u32[]{:S(2)}) collective-permute-start(bf16[2,2,256,128]{3,2,1,0:T(8,128)(2,1)S(1)} %get-tuple-element.48), channel_id=1, source_target_pairs={{4,0},{6,2},{8,4},{10,6},{12,8},{14,10},{16,12},{18,14},{20,16},{2... | collective-permute-start | bytes 786440 | tf_op jit(solution)/shard_map/ppermute | solution.py:23
  94.9 29.0 %collective-permute-start.2 = (bf16[2,2,256,128]{3,2,1,0:T(8,128)(2,1)S(1)}, bf16[2,2,256,128]{3,2,1,0:T(8,128)(2,1)}, u32[]{:S(2)}, u32[]{:S(2)}) collective-permute-start(bf16[2,2,256,128]{3,2,1,0:T(8,128)(2,1)S(1)} %get-tuple-element.48), channel_id=1, source_target_pairs={{0,4},{2,6},{4,8},{6,10},{8,12},{10,14},{12,16},{14,18},{16,20},{1... | collective-permute-start | bytes 786440 | tf_op jit(solution)/shard_map/ppermute | solution.py:23
  99.0 15.7 %collective-permute-start.3 = (bf16[2,2,128,128]{3,2,1,0:T(8,128)(2,1)}, bf16[2,2,128,128]{3,2,1,0:T(8,128)(2,1)S(1)}, u32[]{:S(2)}, u32[]{:S(2)}) collective-permute-start(bf16[2,2,128,128]{3,2,1,0:T(8,128)(2,1)} %get-tuple-element.49), channel_id=1, source_target_pairs={{0,8},{2,10},{4,12},{6,14},{8,16},{10,18},{12,20},{14,22},{16,24},... | collective-permute-start | bytes 393224 | tf_op jit(solution)/shard_map/ppermute | solution.py:23
  114.7 43.2 %collective-permute-start.28 = (bf16[2,2,64,128]{3,2,1,0:T(8,128)(2,1)S(1)}, bf16[2,2,64,128]{3,2,1,0:T(8,128)(2,1)S(1)}, u32[]{:S(2)}, u32[]{:S(2)}) collective-permute-start(bf16[2,2,64,128]{3,2,1,0:T(8,128)(2,1)S(1)} %get-tuple-element.76), channel_id=1, source_target_pairs={{16,0},{18,2},{20,4},{22,6},{24,8},{26,10},{28,12},{30,14},{32,16}... | collective-permute-start | bytes 196616 | tf_op jit(solution)/shard_map/ppermute | solution.py:23
  119.9 40.0 %collective-permute-start.31 = (bf16[2,2,64,128]{3,2,1,0:T(8,128)(2,1)S(1)}, bf16[2,2,64,128]{3,2,1,0:T(8,128)(2,1)S(1)}, u32[]{:S(2)}, u32[]{:S(2)}) collective-permute-start(bf16[2,2,64,128]{3,2,1,0:T(8,128)(2,1)S(1)} %get-tuple-element.79), channel_id=1, source_target_pairs={{0,16},{2,18},{4,20},{6,22},{8,24},{10,26},{12,28},{14,30},{16,32}... | collective-permute-start | bytes 196616 | tf_op jit(solution)/shard_map/ppermute | solution.py:23
  133.4 28.5 %collective-permute-start.20 = (bf16[2,2,64,128]{3,2,1,0:T(8,128)(2,1)S(1)}, bf16[2,2,64,128]{3,2,1,0:T(8,128)(2,1)S(1)}, u32[]{:S(2)}, u32[]{:S(2)}) collective-permute-start(bf16[2,2,64,128]{3,2,1,0:T(8,128)(2,1)S(1)} %get-tuple-element.67), channel_id=1, source_target_pairs={{16,0},{18,2},{20,4},{22,6},{24,8},{26,10},{28,12},{30,14},{32,16}... | collective-permute-start | bytes 196616 | tf_op jit(solution)/shard_map/ppermute | solution.py:23
  141.8 23.7 %collective-permute-start.23 = (bf16[2,2,64,128]{3,2,1,0:T(8,128)(2,1)S(1)}, bf16[2,2,64,128]{3,2,1,0:T(8,128)(2,1)S(1)}, u32[]{:S(2)}, u32[]{:S(2)}) collective-permute-start(bf16[2,2,64,128]{3,2,1,0:T(8,128)(2,1)S(1)} %get-tuple-element.70), channel_id=1, source_target_pairs={{0,16},{2,18},{4,20},{6,22},{8,24},{10,26},{12,28},{14,30},{16,32}... | collective-permute-start | bytes 196616 | tf_op jit(solution)/shard_map/ppermute | solution.py:23
  143.7 34.1 %collective-permute-start.27 = (bf16[2,2,128,128]{3,2,1,0:T(8,128)(2,1)S(1)}, bf16[2,2,128,128]{3,2,1,0:T(8,128)(2,1)S(1)}, u32[]{:S(2)}, u32[]{:S(2)}) collective-permute-start(bf16[2,2,128,128]{3,2,1,0:T(8,128)(2,1)S(1)} %get-tuple-element.75), channel_id=1, source_target_pairs={{8,0},{10,2},{12,4},{14,6},{16,8},{18,10},{20,12},{22,14},{24,16},... | collective-permute-start | bytes 393224 | tf_op jit(solution)/shard_map/ppermute | solution.py:23
  158.0 21.9 %collective-permute-start.30 = (bf16[2,2,128,128]{3,2,1,0:T(8,128)(2,1)S(1)}, bf16[2,2,128,128]{3,2,1,0:T(8,128)(2,1)S(1)}, u32[]{:S(2)}, u32[]{:S(2)}) collective-permute-start(bf16[2,2,128,128]{3,2,1,0:T(8,128)(2,1)S(1)} %get-tuple-element.78), channel_id=1, source_target_pairs={{0,8},{2,10},{4,12},{6,14},{8,16},{10,18},{12,20},{14,22},{16,24},... | collective-permute-start | bytes 393224 | tf_op jit(solution)/shard_map/ppermute | solution.py:23
  159.9 33.1 %collective-permute-start.24 = (bf16[2,2,256,128]{3,2,1,0:T(8,128)(2,1)S(1)}, bf16[2,2,256,128]{3,2,1,0:T(8,128)(2,1)S(1)}, u32[]{:S(2)}, u32[]{:S(2)}) collective-permute-start(bf16[2,2,256,128]{3,2,1,0:T(8,128)(2,1)S(1)} %get-tuple-element.72), channel_id=1, source_target_pairs={{2,0},{4,2},{6,4},{8,6},{10,8},{12,10},{14,12},{16,14},{18,16},{20... | collective-permute-start | bytes 786440 | tf_op jit(solution)/shard_map/ppermute | solution.py:23
  161.8 34.8 %collective-permute-start.25 = (bf16[2,2,256,128]{3,2,1,0:T(8,128)(2,1)S(1)}, bf16[2,2,256,128]{3,2,1,0:T(8,128)(2,1)S(1)}, u32[]{:S(2)}, u32[]{:S(2)}) collective-permute-start(bf16[2,2,256,128]{3,2,1,0:T(8,128)(2,1)S(1)} %get-tuple-element.73), channel_id=1, source_target_pairs={{0,2},{2,4},{4,6},{6,8},{8,10},{10,12},{12,14},{14,16},{16,18},{18... | collective-permute-start | bytes 786440 | tf_op jit(solution)/shard_map/ppermute | solution.py:23
  165.5 39.8 %collective-permute-start.26 = (bf16[2,2,256,128]{3,2,1,0:T(8,128)(2,1)S(1)}, bf16[2,2,256,128]{3,2,1,0:T(8,128)(2,1)S(1)}, u32[]{:S(2)}, u32[]{:S(2)}) collective-permute-start(bf16[2,2,256,128]{3,2,1,0:T(8,128)(2,1)S(1)} %get-tuple-element.74), channel_id=1, source_target_pairs={{4,0},{6,2},{8,4},{10,6},{12,8},{14,10},{16,12},{18,14},{20,16},{2... | collective-permute-start | bytes 786440 | tf_op jit(solution)/shard_map/ppermute | solution.py:23
  177.9 7.5 %collective-permute-start.19 = (bf16[2,2,128,128]{3,2,1,0:T(8,128)(2,1)S(1)}, bf16[2,2,128,128]{3,2,1,0:T(8,128)(2,1)S(1)}, u32[]{:S(2)}, u32[]{:S(2)}) collective-permute-start(bf16[2,2,128,128]{3,2,1,0:T(8,128)(2,1)S(1)} %get-tuple-element.66), channel_id=1, source_target_pairs={{8,0},{10,2},{12,4},{14,6},{16,8},{18,10},{20,12},{22,14},{24,16},... | collective-permute-start | bytes 393224 | tf_op jit(solution)/shard_map/ppermute | solution.py:23
  179.8 11.2 %collective-permute-start.22 = (bf16[2,2,128,128]{3,2,1,0:T(8,128)(2,1)S(1)}, bf16[2,2,128,128]{3,2,1,0:T(8,128)(2,1)S(1)}, u32[]{:S(2)}, u32[]{:S(2)}) collective-permute-start(bf16[2,2,128,128]{3,2,1,0:T(8,128)(2,1)S(1)} %get-tuple-element.69), channel_id=1, source_target_pairs={{0,8},{2,10},{4,12},{6,14},{8,16},{10,18},{12,20},{14,22},{16,24},... | collective-permute-start | bytes 393224 | tf_op jit(solution)/shard_map/ppermute | solution.py:23
  185.4 23.1 %collective-permute-start.29 = (bf16[2,2,256,128]{3,2,1,0:T(8,128)(2,1)S(1)}, bf16[2,2,256,128]{3,2,1,0:T(8,128)(2,1)S(1)}, u32[]{:S(2)}, u32[]{:S(2)}) collective-permute-start(bf16[2,2,256,128]{3,2,1,0:T(8,128)(2,1)S(1)} %get-tuple-element.77), channel_id=1, source_target_pairs={{0,4},{2,6},{4,8},{6,10},{8,12},{10,14},{12,16},{14,18},{16,20},{1... | collective-permute-start | bytes 786440 | tf_op jit(solution)/shard_map/ppermute | solution.py:23
  191.1 17.4 %collective-permute-start.16 = (bf16[2,2,256,128]{3,2,1,0:T(8,128)(2,1)S(1)}, bf16[2,2,256,128]{3,2,1,0:T(8,128)(2,1)S(1)}, u32[]{:S(2)}, u32[]{:S(2)}) collective-permute-start(bf16[2,2,256,128]{3,2,1,0:T(8,128)(2,1)S(1)} %get-tuple-element.63), channel_id=1, source_target_pairs={{2,0},{4,2},{6,4},{8,6},{10,8},{12,10},{14,12},{16,14},{18,16},{20... | collective-permute-start | bytes 786440 | tf_op jit(solution)/shard_map/ppermute | solution.py:23
  193.0 15.5 %collective-permute-start.17 = (bf16[2,2,256,128]{3,2,1,0:T(8,128)(2,1)S(1)}, bf16[2,2,256,128]{3,2,1,0:T(8,128)(2,1)S(1)}, u32[]{:S(2)}, u32[]{:S(2)}) collective-permute-start(bf16[2,2,256,128]{3,2,1,0:T(8,128)(2,1)S(1)} %get-tuple-element.64), channel_id=1, source_target_pairs={{0,2},{2,4},{4,6},{6,8},{8,10},{10,12},{12,14},{14,16},{16,18},{18... | collective-permute-start | bytes 786440 | tf_op jit(solution)/shard_map/ppermute | solution.py:23
  196.6 12.0 %collective-permute-start.18 = (bf16[2,2,256,128]{3,2,1,0:T(8,128)(2,1)S(1)}, bf16[2,2,256,128]{3,2,1,0:T(8,128)(2,1)S(1)}, u32[]{:S(2)}, u32[]{:S(2)}) collective-permute-start(bf16[2,2,256,128]{3,2,1,0:T(8,128)(2,1)S(1)} %get-tuple-element.65), channel_id=1, source_target_pairs={{4,0},{6,2},{8,4},{10,6},{12,8},{14,10},{16,12},{18,14},{20,16},{2... | collective-permute-start | bytes 786440 | tf_op jit(solution)/shard_map/ppermute | solution.py:23
  205.3 11.6 %collective-permute-start.21 = (bf16[2,2,256,128]{3,2,1,0:T(8,128)(2,1)S(1)}, bf16[2,2,256,128]{3,2,1,0:T(8,128)(2,1)S(1)}, u32[]{:S(2)}, u32[]{:S(2)}) collective-permute-start(bf16[2,2,256,128]{3,2,1,0:T(8,128)(2,1)S(1)} %get-tuple-element.68), channel_id=1, source_target_pairs={{0,4},{2,6},{4,8},{6,10},{8,12},{10,14},{12,16},{14,18},{16,20},{1... | collective-permute-start | bytes 786440 | tf_op jit(solution)/shard_map/ppermute | solution.py:23
  (21 other events, 257.0 us)
where the time goes:
time: 220 us; the launch traced here: 219 us
  starting transfers between devices  162 us (74%)
  Pallas kernels  24.3 us (11%)
  waiting for transfers between devices  18.6 us (8%)
  local copies, waits for them, and re-layouts  12.9 us (6%)
    ppermute x32, starting transfers between devices, passed_along(): lax.ppermute(value, 'seq', [(source, source + steps) for source in range(...  162 us
    pallas_call x2, Pallas kernels, attend(): pl.pallas_call(functools.partial(attend_kernel, count), grid=(per,), in_s...  18.7 us
    ppermute x32, waiting for transfers between devices, passed_along(): lax.ppermute(value, 'seq', [(source, source + steps) for source in range(...  18.6 us
    unnamed x42, local copies, waits for them, and re-layouts  12.9 us
  transfers between devices with their start and end apart: 32, of which 6 were waited for; matrix products, arithmetic and copies ran while one was open for 0% of the time, Pallas kernels for 10%

commit v1 on v0

v1 whole, which is shorter than its diff:
```python
import functools
import math

import jax
import jax.numpy as jnp
from jax import lax
from jax.experimental import pallas as pl
from jax.experimental.pallas import tpu as pltpu
from jax.sharding import PartitionSpec as P

BLOCK = 256
LEVELS = 3
LOG2E = math.log2(math.e)

BF = jnp.bfloat16
F32 = jnp.float32


def crossed(value, steps):
    count = lax.axis_size("seq")
    pairs = [(at, at + (steps if at % 2 == 0 else -steps)) for at in range(count)]
    return lax.ppermute(value, "seq", [(at, to) for at, to in pairs if 0 <= to < count])


def swapped(value):
    count = lax.axis_size("seq")
    return lax.ppermute(value, "seq", [(at, at ^ 1) for at in range(count)])


def nt(left, right):
    return lax.dot_general(left, right, (((1,), (1,)), ((), ())), preferred_element_type=F32)


def nn(left, right):
    return jnp.dot(left, right, preferred_element_type=F32)


def shape(dims, dtype=BF):
    return jax.ShapeDtypeStruct(dims, dtype)


def params(mib):
    return pltpu.CompilerParams(vmem_limit_bytes=mib * 2**20)


SMEM_SPEC = pl.BlockSpec(memory_space=pltpu.SMEM)
VMEM_SPEC = pl.BlockSpec(memory_space=pltpu.VMEM)


def turned(wide, ref, odd):
    half = wide.shape[0] // 2
    wide[pl.ds(pl.multiple_of(odd * half, half), half), :] = ref[:half].astype(F32)
    wide[pl.ds(pl.multiple_of((1 - odd) * half, half), half), :] = ref[half:].astype(F32)


def turned_back(ref, wide, odd):
    half = wide.shape[0] // 2
    ref[pl.ds(pl.multiple_of(odd * half, half), half), :] = wide[:half].astype(BF)
    ref[pl.ds(pl.multiple_of((1 - odd) * half, half), half), :] = wide[half:].astype(BF)


def pair_sums(wide, row, size, heads):
    return (
        wide[pl.ds(row, size, stride=2 * heads), :]
        + wide[pl.ds(row + heads, size, stride=2 * heads), :]
    )


def next_sums(sums, total):
    size = total.shape[0]
    sums[pl.ds(0, size), :] = total
    half = size // 2
    return sums[pl.ds(0, half, stride=2), :] + sums[pl.ds(1, half, stride=2), :]


def split_kv_kernel(heads, place_ref, k_ref, v_ref, outer, inner, *rest):
    coarse, (wide, sums) = rest[:LEVELS], rest[LEVELS:]
    block = inner.shape[2]
    odd = lax.rem(place_ref[0], 2)
    for at, ref in enumerate((k_ref, v_ref)):
        turned(wide, ref, odd)
        for head in range(heads):
            outer[2 + at, head] = wide[pl.ds(head, block, stride=heads), :].astype(BF)
            inner[at, head] = wide[pl.ds(head + heads * block, block, stride=heads), :].astype(BF)
            total = pair_sums(wide, head, block, heads)
            for level in range(LEVELS):
                mean = (total * (1.0 / 2 ** (level + 1))).astype(BF)
                coarse[level][at, head] = mean
                if level == 0:
                    outer[at, head] = mean
                if level + 1 < LEVELS:
                    total = next_sums(sums, total)


def split_kv(place, k2, v2, heads, span):
    block = span // 2
    outs = [shape((4, heads, block, 128)), shape((2, heads, block, 128))]
    outs += [shape((2, heads, span // 2 ** (level + 1), 128)) for level in range(LEVELS)]
    return pl.pallas_call(
        functools.partial(split_kv_kernel, heads),
        out_shape=outs,
        in_specs=[SMEM_SPEC, VMEM_SPEC, VMEM_SPEC],
        scratch_shapes=[
            pltpu.VMEM((heads * span, 128), F32),
            pltpu.VMEM((block, 128), F32),
        ],
        compiler_params=params(16),
        name="split_kv",
        cost_estimate=pl.CostEstimate(flops=0, bytes_accessed=4 * 2**20, transcendentals=0),
    )(place, k2, v2)


def relay_kernel(near, inner, *refs):
    refs[-1][:2] = near[2:]
    refs[-1][2:] = inner[...]


def relay(near, inner, earlier):
    return pl.pallas_call(
        relay_kernel,
        out_shape=shape(near.shape),
        in_specs=[VMEM_SPEC] * 2 + [pl.BlockSpec(memory_space=pl.ANY)] * len(earlier),
        compiler_params=params(8),
        name="relay",
        cost_estimate=pl.CostEstimate(flops=0, bytes_accessed=2 * 2**20, transcendentals=0),
    )(near, inner, *earlier)


def split_qd_kernel(heads, place_ref, q_ref, d_ref, q_out, d_out, rep_out, wide, sums, spread):
    span = q_out.shape[1]
    odd = lax.rem(place_ref[0], 2)
    turned(wide, d_ref, odd)
    for head in range(heads):
        d_out[head] = wide[pl.ds(head, span, stride=heads), :].astype(BF)
    turned(wide, q_ref, odd)
    for head in range(heads):
        q_out[head] = wide[pl.ds(head, span, stride=heads), :].astype(BF)
        total = pair_sums(wide, head, span // 2, heads)
        for level in range(LEVELS):
            factor = 2 ** (level + 1)
            mean = (total * (1.0 / factor)).astype(BF).astype(F32)
            for row in range(factor):
                spread[pl.ds(row, span // factor, stride=factor), :] = mean
            rep_out[level, head] = spread[...].astype(BF)
            if level + 1 < LEVELS:
                total = next_sums(sums, total)


def split_qd(place, q2, d2, heads, span):
    return pl.pallas_call(
        functools.partial(split_qd_kernel, heads),
        out_shape=[
            shape((heads, span, 128)),
            shape((heads, span, 128)),
            shape((LEVELS, heads, span, 128)),
        ],
        in_specs=[SMEM_SPEC] + [VMEM_SPEC] * 2,
        scratch_shapes=[
            pltpu.VMEM((heads * span, 128), F32),
            pltpu.VMEM((span // 2, 128), F32),
            pltpu.VMEM((span, 128), F32),
        ],
        compiler_params=params(16),
        name="split_qd",
        cost_estimate=pl.CostEstimate(flops=0, bytes_accessed=8 * 2**20, transcendentals=0),
    )(place, q2, d2)


def attend_kernel(count, place_ref, q_ref, d_ref, rep_ref, outer, inner, rim_out, rim_in, *rest):
    crossed_a, crossed_b = rest[:LEVELS], rest[LEVELS : 2 * LEVELS]
    att, gq, own, g_rims = rest[2 * LEVELS : 2 * LEVELS + 4]
    rest = rest[2 * LEVELS + 4 :]
    g_as, g_bs = rest[:LEVELS], rest[LEVELS : 2 * LEVELS]
    keys, vals, keys_t, vals_t, scores, grads, probs, dscores, rows, total_q = rest[2 * LEVELS :]
    place = place_ref[0]
    even = lax.rem(place, 2) == 0
    block = outer.shape[2]
    scale = 1.0 / math.sqrt(128)
    scale2 = scale * LOG2E

    def reaches(below, steps):
        return jnp.where(below, place >= steps, place < count - steps)

    parts = [(rim_out, reaches(even, 1), 0), (outer, None, 0), (inner, None, 0)]
    for level in range(LEVELS):
        factor = 2 ** (level + 1)
        parts.append((crossed_a[level], reaches(even, factor), level + 1))
        parts.append((crossed_b[level], reaches(jnp.logical_not(even), factor), level + 1))
    parts.append((rim_in, None, 0))
    at = 0
    segments = []
    for ref, ok, level in parts:
        size = ref.shape[2]
        keys[pl.ds(at, size), :] = ref[0, 0]
        vals[pl.ds(at, size), :] = ref[1, 0]
        bias = float(level)
        if ok is not None:
            bias = jnp.where(ok, bias, -jnp.inf).astype(F32)
        segments.append((at, size, bias, level))
        at += size
    keys_t[...] = keys[...].T
    vals_t[...] = vals[...].T

    held = None
    for turn in range(2):
        own_rows = pl.ds(turn * block, block)
        q_blk = q_ref[0, own_rows, :]
        d_blk = d_ref[0, own_rows, :]
        using = [q_blk] + [rep_ref[level, 0, own_rows, :] for level in range(LEVELS)]
        mine = segments[:-1] if turn == 0 else segments[1:]
        base = mine[0][0]
        width = mine[-1][0] + mine[-1][1] - base
        top = None
        for start, size, bias, level in mine:
            s = nt(keys[pl.ds(start, size), :], using[level])
            scores[pl.ds(start - base, size), :] = s
            high = jnp.max(s, axis=0, keepdims=True) * scale2 + bias
            top = high if top is None else jnp.maximum(top, high)
        total = jnp.zeros((1, block), F32)
        acc = jnp.zeros((1, block), F32)
        for start, size, bias, level in mine:
            here = pl.ds(start - base, size)
            e = jnp.exp2(scores[here, :] * scale2 - (top - bias))
            scores[here, :] = e
            total = total + jnp.sum(e, axis=0, keepdims=True)
            dp = nt(vals[pl.ds(start, size), :], d_blk)
            grads[here, :] = dp
            acc = acc + jnp.sum(e * dp, axis=0, keepdims=True)
        inverse = 1.0 / total
        delta = acc * inverse
        for start, size, bias, level in mine:
            here = pl.ds(start - base, size)
            p = scores[here, :] * inverse
            probs[here, :] = p.astype(BF)
            dscores[here, :] = (p * (grads[here, :] - delta)).astype(BF)
        att[0, own_rows, :] = nn(vals_t[:, base : base + width], probs[...]).T.astype(BF)
        gv = nn(probs[...], d_blk)
        pieces = {}
        fine = jnp.zeros((128, block), F32)
        for start, size, bias, level in mine:
            here = pl.ds(start - base, size)
            ds = dscores[here, :]
            gk = nn(ds, using[level]) * scale
            pieces[start] = (gk, gv[start - base : start - base + size])
        fine_at = [(s, z) for s, z, _, level in mine if level == 0]
        for start, size in fine_at:
            fine = fine + nn(keys_t[:, start : start + size], dscores[pl.ds(start - base, size), :])
        total_q[...] = fine.T
        for level in range(1, LEVELS + 1):
            spots = [(s, z) for s, z, _, lev in mine if lev == level]
            start, size = spots[0][0], spots[0][1] + spots[1][1]
            up = nn(keys_t[:, start : start + size], dscores[pl.ds(start - base, size), :])
            rows[...] = up.T
            factor = 2**level
            groups = block // factor
            mean = rows[pl.ds(0, groups, stride=factor), :]
            for row in range(1, factor):
                mean = mean + rows[pl.ds(row, groups, stride=factor), :]
            mean = mean * (1.0 / factor)
            for row in range(factor):
                spot = pl.ds(row, groups, stride=factor)
                total_q[spot, :] = total_q[spot, :] + mean
        gq[0, own_rows, :] = (total_q[...] * scale).astype(BF)
        if turn == 0:
            held = pieces
        else:
            for key, pair in pieces.items():
                if key in held:
                    held[key] = (held[key][0] + pair[0], held[key][1] + pair[1])
                else:
                    held[key] = pair

    places = [(g_rims, 0, None), (own, 0, 0), (own, 0, block)]
    for level in range(LEVELS):
        places += [(g_as[level], 0, None), (g_bs[level], 0, None)]
    places.append((g_rims, 2, None))
    for (ref, lead, offset), (start, size, bias, level) in zip(places, segments):
        for which in range(2):
            value = held[start][which]
            if offset is None:
                ref[lead + which, 0] = value.astype(ref.dtype)
            else:
                ref[which, 0, pl.ds(offset, size), :] = value


def attend(place, count, q, d, rep, outer, inner, rims, crossed_a, crossed_b):
    heads, block = inner.shape[1], inner.shape[2]
    span = 2 * block
    sizes = [span // 2 ** (level + 1) for level in range(LEVELS)]
    columns = 4 * block + 2 * sum(sizes)
    width = columns - block

    def pair(size, at=0):
        return pl.BlockSpec((2, 1, size, 128), lambda h: (at, h, 0, 0))

    head_spec = pl.BlockSpec((1, span, 128), lambda h: (h, 0, 0))
    flops = 2 * heads * span * width * 128 * 6
    return pl.pallas_call(
        functools.partial(attend_kernel, count),
        grid=(heads,),
        in_specs=[
            SMEM_SPEC,
            head_spec,
            head_spec,
            pl.BlockSpec((LEVELS, 1, span, 128), lambda h: (0, h, 0, 0)),
            pair(block, 1),
            pair(block),
            pair(block, 0),
            pair(block, 1),
        ]
        + [pair(size) for size in sizes] * 2,
        out_specs=[
            head_spec,
            head_spec,
            pair(span),
            pl.BlockSpec((4, 1, block, 128), lambda h: (0, h, 0, 0)),
        ]
        + [pair(size) for size in sizes] * 2,
        out_shape=[
            shape((heads, span, 128)),
            shape((heads, span, 128)),
            shape((2, heads, span, 128), F32),
            shape((4, heads, block, 128)),
        ]
        + [shape((2, heads, size, 128)) for size in sizes] * 2,
        scratch_shapes=[
            pltpu.VMEM((columns, 128), BF),
            pltpu.VMEM((columns, 128), BF),
            pltpu.VMEM((128, columns), BF),
            pltpu.VMEM((128, columns), BF),
            pltpu.VMEM((width, block), F32),
            pltpu.VMEM((width, block), F32),
            pltpu.VMEM((width, block), BF),
            pltpu.VMEM((width, block), BF),
            pltpu.VMEM((block, 128), F32),
            pltpu.VMEM((block, 128), F32),
        ],
        compiler_params=params(24),
        name="attend",
        cost_estimate=pl.CostEstimate(
            flops=flops, bytes_accessed=8 * 2**20, transcendentals=heads * span * width
        ),
    )(place, q, d, rep, outer, inner, rims, rims, *crossed_a, *crossed_b)


def merge_kernel(count, *refs):
    coarse, fine, tails = refs[:count], refs[count : 2 * count], refs[2 * count : -count - 1]
    outs, wide = refs[-count - 1 : -1], refs[-1]
    for at in range(count):
        rows = fine[at].shape[0]
        half = coarse[at][...].astype(F32) * 0.5
        wide[pl.ds(0, rows // 2, stride=2), :] = half
        wide[pl.ds(1, rows // 2, stride=2), :] = half
        outs[at][:rows] = (wide[...] + fine[at][...].astype(F32)).astype(BF)
    for at, tail in enumerate(tails):
        rows = fine[count - 1].shape[0]
        outs[count - 1][rows:] = tail[: outs[count - 1].shape[0] - rows]


def merge(coarse, fine, tail=None):
    def flat(x):
        return x.reshape(-1, 128)

    heads, size = fine[0].shape[1], fine[0].shape[2]
    rows = 2 * heads * size
    dims = [(2, heads, size, 128)] * 2
    extra = []
    if tail is not None:
        dims[1] = (4, heads, size, 128)
        extra = [flat(tail)]
    outs = pl.pallas_call(
        functools.partial(merge_kernel, 2),
        out_shape=[shape((math.prod(x[:3]), 128)) for x in dims],
        scratch_shapes=[pltpu.VMEM((rows, 128), F32)],
        compiler_params=params(12),
        name="merge",
        cost_estimate=pl.CostEstimate(flops=0, bytes_accessed=2 * 2**20, transcendentals=0),
    )(*map(flat, coarse), *map(flat, fine), *extra)
    return [x.reshape(dim) for x, dim in zip(outs, dims)]


def join_kernel(heads, place_ref, att, gq, att_out, gq_out, wide):
    span = att.shape[1]
    odd = lax.rem(place_ref[0], 2)
    for ref, out in ((att, att_out), (gq, gq_out)):
        for head in range(heads):
            wide[pl.ds(head, span, stride=heads), :] = ref[head].astype(F32)
        turned_back(out, wide, odd)


def join(place, att, gq):
    heads, span = att.shape[:2]
    return pl.pallas_call(
        functools.partial(join_kernel, heads),
        out_shape=[shape((heads * span, 128))] * 2,
        in_specs=[SMEM_SPEC, VMEM_SPEC, VMEM_SPEC],
        scratch_shapes=[pltpu.VMEM((heads * span, 128), F32)],
        compiler_params=params(12),
        name="join",
        cost_estimate=pl.CostEstimate(flops=0, bytes_accessed=4 * 2**20, transcendentals=0),
    )(place, att, gq)


def gather_kernel(heads, place_ref, own, rims, coarse_a, coarse_b, gk_out, gv_out, wide, mine):
    span = own.shape[2]
    block = span // 2
    odd = lax.rem(place_ref[0], 2)
    for which, out in enumerate((gk_out, gv_out)):
        for head in range(heads):
            spread = (
                coarse_a[which, head].astype(F32) + coarse_b[which, head].astype(F32)
            ) * 0.5
            outer, inner = coarse_b[2 + which, head], rims[2 + which, head]
            mine[pl.ds(0, block), :] = own[which, head, :block] + outer.astype(F32)
            mine[pl.ds(block, block), :] = own[which, head, block:] + inner.astype(F32)
            for second in range(2):
                wide[pl.ds(head + heads * second, block, stride=2 * heads), :] = (
                    mine[pl.ds(second, block, stride=2), :] + spread
                )
        turned_back(out, wide, odd)


def gather(place, own, rims, coarse_a, coarse_b):
    heads, span = own.shape[1:3]
    return pl.pallas_call(
        functools.partial(gather_kernel, heads),
        out_shape=[shape((heads * span, 128))] * 2,
        in_specs=[SMEM_SPEC] + [VMEM_SPEC] * 4,
        scratch_shapes=[
            pltpu.VMEM((heads * span, 128), F32),
            pltpu.VMEM((span, 128), F32),
        ],
        compiler_params=params(16),
        name="gather",
        cost_estimate=pl.CostEstimate(flops=0, bytes_accessed=8 * 2**20, transcendentals=0),
    )(place, own, rims, coarse_a, coarse_b)


def local(query, key, value, dout):
    span, heads, width = query.shape
    count = lax.axis_size("seq")
    place = jnp.reshape(lax.axis_index("seq"), (1,)).astype(jnp.int32)
    flat = (heads * span, width)
    q2, k2, v2, d2 = (x.reshape(flat) for x in (query, key, value, dout))
    outer, inner, *coarse = split_kv(place, k2, v2, heads, span)
    near_b = crossed(outer, -2)
    near_a = crossed(coarse[0], 2)
    crossed_a = [near_a] + [crossed(coarse[level], 2 ** (level + 1)) for level in (1, 2)]
    crossed_b = [near_b] + [crossed(coarse[level], -(2 ** (level + 1))) for level in (1, 2)]
    qh, dh, rep = split_qd(place, q2, d2, heads, span)
    rims = swapped(relay(near_b, inner, [near_a, crossed_a[1], crossed_b[1]]))
    att, gq, own, g_rims, *grads = attend(
        place, count, qh, dh, rep, outer, inner, rims, crossed_a, crossed_b
    )
    g_as, g_bs = grads[:LEVELS], grads[LEVELS:]
    far_a, far_b = crossed(g_as[2], -4), crossed(g_bs[2], 4)
    g_rims = swapped(g_rims)
    mid_a, mid_b = merge((far_a, far_b), (g_as[1], g_bs[1]))
    mid_a, mid_b = crossed(mid_a, -2), crossed(mid_b, 2)
    last_a, last_b = merge((mid_a, mid_b), (g_as[0], g_bs[0]), g_rims)
    last_a, last_b = crossed(last_a, -2), crossed(last_b, 2)
    attended, grad_query = join(place, att, gq)
    grad_key, grad_value = gather(place, own, g_rims, last_a, last_b)
    return tuple(
        x.reshape(span, heads, width) for x in (attended, grad_query, grad_key, grad_value)
    )


def solution(mesh):
    placed = P("seq", "head", None)
    return jax.shard_map(
        local,
        mesh=mesh,
        in_specs=(placed,) * 4,
        out_specs=(placed,) * 4,
        check_vma=False,
    )
```

time: 220 us -> 154 us (0.70)
  the two profiles are of different devices: /device:TPU:25 before, /device:TPU:24 now
where the time goes in v1:
time: 154 us
  starting transfers between devices  67.5 us (44%)
  waiting for transfers between devices  60.8 us (39%)
  Pallas kernels  22.6 us (15%)
  local copies, waits for them, and re-layouts  2.09 us (1%)
    ppermute x12, starting transfers between devices, crossed(): lax.ppermute(value, 'seq', [(at, to) for at, to in pairs if 0 <= to < cou...  63.6 us
    ppermute x12, waiting for transfers between devices, crossed(): lax.ppermute(value, 'seq', [(at, to) for at, to in pairs if 0 <= to < cou...  60.8 us
    pallas_call x1, Pallas kernels, attend(): pl.pallas_call(functools.partial(attend_kernel, count), grid=(heads,), in...  17 us
    ppermute x2, starting transfers between devices, swapped(): return lax.ppermute(value, 'seq', [(at, at ^ 1) for at in range(count)])  3.84 us
  transfers between devices with their start and end apart: 14, of which 9 were waited for; matrix products, arithmetic and copies ran while one was open for 0% of the time, Pallas kernels for 2%

profile of v1, /device:TPU:24, one launch (start us, length us, event | category | flops | bytes accessed | tf_op | source)
XLA Modules:
  0.0 153.8 jit_solution(16852248677570057618)
XLA Ops:
  0.6 1.0 copy-done
  1.7 1.0 copy-done.1
  2.7 0.9 split_kv.1
  3.6 14.2 %collective-permute-start = (bf16[4,4,256,128]{3,2,1,0:T(8,128)(2,1)S(1)}, bf16[4,4,256,128]{3,2,1,0:T(8,128)(2,1)S(1)}, u32[]{:S(2)}, u32[]{:S(2)}) collective-permute-start(bf16[4,4,256,128]{3,2,1,0:T(8,128)(2,1)S(1)} %get-tuple-element.33.outer), channel_id=1, source_target_pairs={{2,6},{4,0},{6,10},{8,4},{10,14},{12,8},{14,18},{16,12},{18,22},{2... | collective-permute-start | bytes 3145736 | tf_op jit(solution)/shard_map/ppermute | solution.py:22
  17.8 1.9 %collective-permute-start.1 = (bf16[2,4,256,128]{3,2,1,0:T(8,128)(2,1)S(1)}, bf16[2,4,256,128]{3,2,1,0:T(8,128)(2,1)S(1)}, u32[]{:S(2)}, u32[]{:S(2)}) collective-permute-start(bf16[2,4,256,128]{3,2,1,0:T(8,128)(2,1)S(1)} %get-tuple-element.35), channel_id=1, source_target_pairs={{0,4},{4,8},{6,2},{8,12},{10,6},{12,16},{14,10},{16,20},{18,14},{2... | collective-permute-start | bytes 1572872 | tf_op jit(solution)/shard_map/ppermute | solution.py:22
  19.7 4.4 %collective-permute-start.3 = (bf16[2,4,128,128]{3,2,1,0:T(8,128)(2,1)S(1)}, bf16[2,4,128,128]{3,2,1,0:T(8,128)(2,1)S(1)}, u32[]{:S(2)}, u32[]{:S(2)}) collective-permute-start(bf16[2,4,128,128]{3,2,1,0:T(8,128)(2,1)S(1)} %get-tuple-element.36), channel_id=1, source_target_pairs={{2,10},{6,14},{8,0},{10,18},{12,4},{14,22},{16,8},{18,26},{20,12},... | collective-permute-start | bytes 786440 | tf_op jit(solution)/shard_map/ppermute | solution.py:22
  24.1 2.4 %collective-permute-start.2 = (bf16[2,4,128,128]{3,2,1,0:T(8,128)(2,1)S(1)}, bf16[2,4,128,128]{3,2,1,0:T(8,128)(2,1)S(1)}, u32[]{:S(2)}, u32[]{:S(2)}) collective-permute-start(bf16[2,4,128,128]{3,2,1,0:T(8,128)(2,1)S(1)} %get-tuple-element.36), channel_id=1, source_target_pairs={{0,8},{4,12},{8,16},{10,2},{12,20},{14,6},{16,24},{18,10},{20,28},... | collective-permute-start | bytes 786440 | tf_op jit(solution)/shard_map/ppermute | solution.py:22
  26.5 20.5 %collective-permute-done.3.refs_2_.rest_4_ = bf16[2,4,128,128]{3,2,1,0:T(8,128)(2,1)S(1)} collective-permute-done((bf16[2,4,128,128]{3,2,1,0:T(8,128)(2,1)S(1)}, bf16[2,4,128,128]{3,2,1,0:T(8,128)(2,1)S(1)}, u32[]{:S(2)}, u32[]{:S(2)}) %collective-permute-start.3) | collective-permute-done | bytes 262176 | tf_op jit(solution)/shard_map/ppermute | solution.py:22
  47.0 1.9 %collective-permute-start.4 = (bf16[4,4,256,128]{3,2,1,0:T(8,128)(2,1)S(1)}, bf16[4,4,256,128]{3,2,1,0:T(8,128)(2,1)S(1)}, u32[]{:S(2)}, u32[]{:S(2)}) collective-permute-start(bf16[4,4,256,128]{3,2,1,0:T(8,128)(2,1)S(1)} %relay.1), channel_id=1, source_target_pairs={{0,2},{2,0},{4,6},{6,4},{8,10},{10,8},{12,14},{14,12},{16,18},{18,... | collective-permute-start | bytes 3145736 | tf_op jit(solution)/shard_map/ppermute | solution.py:27
  49.0 6.2 %collective-permute-start.6 = (bf16[2,4,64,128]{3,2,1,0:T(8,128)(2,1)S(1)}, bf16[2,4,64,128]{3,2,1,0:T(8,128)(2,1)S(1)}, u32[]{:S(2)}, u32[]{:S(2)}) collective-permute-start(bf16[2,4,64,128]{3,2,1,0:T(8,128)(2,1)S(1)} %get-tuple-element.37), channel_id=1, source_target_pairs={{2,18},{6,22},{10,26},{14,30},{16,0},{18,34},{20,4},{22,38},{24,8}... | collective-permute-start | bytes 393224 | tf_op jit(solution)/shard_map/ppermute | solution.py:22
  55.2 3.6 %collective-permute-start.5 = (bf16[2,4,64,128]{3,2,1,0:T(8,128)(2,1)S(1)}, bf16[2,4,64,128]{3,2,1,0:T(8,128)(2,1)S(1)}, u32[]{:S(2)}, u32[]{:S(2)}) collective-permute-start(bf16[2,4,64,128]{3,2,1,0:T(8,128)(2,1)S(1)} %get-tuple-element.37), channel_id=1, source_target_pairs={{0,16},{4,20},{8,24},{12,28},{16,32},{18,2},{20,36},{22,6},{24,40}... | collective-permute-start | bytes 393224 | tf_op jit(solution)/shard_map/ppermute | solution.py:22
  58.8 0.9 split_qd.1
  59.7 4.8 %collective-permute-done.6.rest_5_ = bf16[2,4,64,128]{3,2,1,0:T(8,128)(2,1)S(1)} collective-permute-done((bf16[2,4,64,128]{3,2,1,0:T(8,128)(2,1)S(1)}, bf16[2,4,64,128]{3,2,1,0:T(8,128)(2,1)S(1)}, u32[]{:S(2)}, u32[]{:S(2)}) %collective-permute-start.6) | collective-permute-done | bytes 131104 | tf_op jit(solution)/shard_map/ppermute | solution.py:22
  64.5 6.1 %collective-permute-done.5.rest_2_ = bf16[2,4,64,128]{3,2,1,0:T(8,128)(2,1)S(1)} collective-permute-done((bf16[2,4,64,128]{3,2,1,0:T(8,128)(2,1)S(1)}, bf16[2,4,64,128]{3,2,1,0:T(8,128)(2,1)S(1)}, u32[]{:S(2)}, u32[]{:S(2)}) %collective-permute-start.5) | collective-permute-done | bytes 131104 | tf_op jit(solution)/shard_map/ppermute | solution.py:22
  70.6 17.0 %attend.1 = (bf16[4,512,128]{2,1,0:T(8,128)(2,1)S(1)}, bf16[4,512,128]{2,1,0:T(8,128)(2,1)S(1)}, f32[2,4,512,128]{3,2,1,0:T(8,128)S(1)}, bf16[4,4,256,128]{3,2,1...) custom-call(s32[1]{0:T(128)} %bitcast.place_ref, ...), custom_call_target="tpu_custom_call" | custom-call | flops 5234491392 | bytes 8388608 | tf_op jit(solution)/shard_map/attend/pallas_call | solution.py:298
  87.6 1.9 %collective-permute-start.7 = (bf16[4,4,256,128]{3,2,1,0:T(8,128)(2,1)S(1)}, bf16[4,4,256,128]{3,2,1,0:T(8,128)(2,1)S(1)}, u32[]{:S(2)}, u32[]{:S(2)}) collective-permute-start(bf16[4,4,256,128]{3,2,1,0:T(8,128)(2,1)S(1)} %get-tuple-element.43), channel_id=1, source_target_pairs={{0,2},{2,0},{4,6},{6,4},{8,10},{10,8},{12,14},{14,12},{16,18},{18,... | collective-permute-start | bytes 3145736 | tf_op jit(solution)/shard_map/ppermute | solution.py:27
  89.6 7.9 %collective-permute-start.8 = (bf16[2,4,64,128]{3,2,1,0:T(8,128)(2,1)S(1)}, bf16[2,4,64,128]{3,2,1,0:T(8,128)(2,1)S(1)}, u32[]{:S(2)}, u32[]{:S(2)}) collective-permute-start(bf16[2,4,64,128]{3,2,1,0:T(8,128)(2,1)S(1)} %get-tuple-element.44), channel_id=1, source_target_pairs={{2,10},{6,14},{8,0},{10,18},{12,4},{14,22},{16,8},{18,26},{20,12},... | collective-permute-start | bytes 393224 | tf_op jit(solution)/shard_map/ppermute | solution.py:22
  97.5 1.9 %collective-permute-start.9 = (bf16[2,4,64,128]{3,2,1,0:T(8,128)(2,1)S(1)}, bf16[2,4,64,128]{3,2,1,0:T(8,128)(2,1)S(1)}, u32[]{:S(2)}, u32[]{:S(2)}) collective-permute-start(bf16[2,4,64,128]{3,2,1,0:T(8,128)(2,1)S(1)} %get-tuple-element.45), channel_id=1, source_target_pairs={{0,8},{4,12},{8,16},{10,2},{12,20},{14,6},{16,24},{18,10},{20,28},... | collective-permute-start | bytes 393224 | tf_op jit(solution)/shard_map/ppermute | solution.py:22
  99.5 2.9 %collective-permute-done.8 = bf16[2,4,64,128]{3,2,1,0:T(8,128)(2,1)S(1)} collective-permute-done((bf16[2,4,64,128]{3,2,1,0:T(8,128)(2,1)S(1)}, bf16[2,4,64,128]{3,2,1,0:T(8,128)(2,1)S(1)}, u32[]{:S(2)}, u32[]{:S(2)}) %collective-permute-start.8) | collective-permute-done | bytes 131104 | tf_op jit(solution)/shard_map/ppermute | solution.py:22
  102.4 7.4 %collective-permute-done.9 = bf16[2,4,64,128]{3,2,1,0:T(8,128)(2,1)S(1)} collective-permute-done((bf16[2,4,64,128]{3,2,1,0:T(8,128)(2,1)S(1)}, bf16[2,4,64,128]{3,2,1,0:T(8,128)(2,1)S(1)}, u32[]{:S(2)}, u32[]{:S(2)}) %collective-permute-start.9) | collective-permute-done | bytes 131104 | tf_op jit(solution)/shard_map/ppermute | solution.py:22
  109.8 0.2 merge.2
  110.0 1.9 %collective-permute-start.11 = (bf16[2,4,128,128]{3,2,1,0:T(8,128)(2,1)S(1)}, bf16[2,4,128,128]{3,2,1,0:T(8,128)(2,1)S(1)}, u32[]{:S(2)}, u32[]{:S(2)}) collective-permute-start(bf16[2,4,128,128]{3,2,1,0:T(8,128)(2,1)S(1)} %bitcast.38), channel_id=1, source_target_pairs={{0,4},{4,8},{6,2},{8,12},{10,6},{12,16},{14,10},{16,20},{18,14},{2... | collective-permute-start | bytes 786440 | tf_op jit(solution)/shard_map/ppermute | solution.py:22
  111.9 8.4 %collective-permute-start.10 = (bf16[2,4,128,128]{3,2,1,0:T(8,128)(2,1)S(1)}, bf16[2,4,128,128]{3,2,1,0:T(8,128)(2,1)S(1)}, u32[]{:S(2)}, u32[]{:S(2)}) collective-permute-start(bf16[2,4,128,128]{3,2,1,0:T(8,128)(2,1)S(1)} %bitcast.37), channel_id=1, source_target_pairs={{2,6},{4,0},{6,10},{8,4},{10,14},{12,8},{14,18},{16,12},{18,22},{2... | collective-permute-start | bytes 786440 | tf_op jit(solution)/shard_map/ppermute | solution.py:22
  120.4 2.7 %collective-permute-done.11 = bf16[2,4,128,128]{3,2,1,0:T(8,128)(2,1)S(1)} collective-permute-done((bf16[2,4,128,128]{3,2,1,0:T(8,128)(2,1)S(1)}, bf16[2,4,128,128]{3,2,1,0:T(8,128)(2,1)S(1)}, u32[]{:S(2)}, u32[]{:S(2)}) %collective-permute-start.11) | collective-permute-done | bytes 262176 | tf_op jit(solution)/shard_map/ppermute | solution.py:22
  123.0 1.2 collective-permute-done.10
  124.2 0.5 merge.3
  124.7 1.9 %collective-permute-start.13 = (bf16[4,4,256,128]{3,2,1,0:T(8,128)(2,1)S(1)}, bf16[4,4,256,128]{3,2,1,0:T(8,128)(2,1)S(1)}, u32[]{:S(2)}, u32[]{:S(2)}) collective-permute-start(bf16[4,4,256,128]{3,2,1,0:T(8,128)(2,1)S(1)} %bitcast.35), channel_id=1, source_target_pairs={{0,4},{4,8},{6,2},{8,12},{10,6},{12,16},{14,10},{16,20},{18,14},{2... | collective-permute-start | bytes 3145736 | tf_op jit(solution)/shard_map/ppermute | solution.py:22
  126.7 8.9 %collective-permute-start.12 = (bf16[2,4,256,128]{3,2,1,0:T(8,128)(2,1)S(1)}, bf16[2,4,256,128]{3,2,1,0:T(8,128)(2,1)S(1)}, u32[]{:S(2)}, u32[]{:S(2)}) collective-permute-start(bf16[2,4,256,128]{3,2,1,0:T(8,128)(2,1)S(1)} %bitcast.36), channel_id=1, source_target_pairs={{2,6},{4,0},{6,10},{8,4},{10,14},{12,8},{14,18},{16,12},{18,22},{2... | collective-permute-start | bytes 1572872 | tf_op jit(solution)/shard_map/ppermute | solution.py:22
  135.6 1.2 join.1
  136.8 8.3 %collective-permute-done.12.coarse_a = bf16[2,4,256,128]{3,2,1,0:T(8,128)(2,1)S(1)} collective-permute-done((bf16[2,4,256,128]{3,2,1,0:T(8,128)(2,1)S(1)}, bf16[2,4,256,128]{3,2,1,0:T(8,128)(2,1)S(1)}, u32[]{:S(2)}, u32[]{:S(2)}) %collective-permute-start.12) | collective-permute-done | bytes 524320 | tf_op jit(solution)/shard_map/ppermute | solution.py:22
  145.1 7.0 %collective-permute-done.13.coarse_b = bf16[4,4,256,128]{3,2,1,0:T(8,128)(2,1)S(1)} collective-permute-done((bf16[4,4,256,128]{3,2,1,0:T(8,128)(2,1)S(1)}, bf16[4,4,256,128]{3,2,1,0:T(8,128)(2,1)S(1)}, u32[]{:S(2)}, u32[]{:S(2)}) %collective-permute-start.13) | collective-permute-done | bytes 1048608 | tf_op jit(solution)/shard_map/ppermute | solution.py:22
  152.0 1.8 %gather.1 = (bf16[2048,128]{1,0:T(8,128)(2,1)}, bf16[2048,128]{1,0:T(8,128)(2,1)}) custom-call(s32[1]{0:T(128)} %bitcast.place_ref, f32[2,4,512,128]{3,2,1,0:T(8,128)S(1)} %get-tuple-element.42.own, bf16[4,4,256,128]{3,2,1,0:T(8,128)(2,1)S(1)} %collective-permute-done.7.rims, bf16[2,4,256,128]{3,2,1,0:T(8,128)(2,1)S(1)} %collective-permute-done.12.coarse_a, ...), custom_call_target="tpu_custom_call" | custom-call | bytes 8388608 | tf_op jit(solution)/shard_map/gather/pallas_call | solution.py:425
  (12 shorter events, 0.1 us)
Async XLA Ops:
  0.6 1.0 copy-start
  1.7 1.0 copy-start.1
  3.6 55.1 %copy-start.2 = (bf16[512,4,128]{2,1,0:T(4,128)(2,1)S(1)}, bf16[512,4,128]{2,1,0:T(4,128)(2,1)}, u32[]{:S(2)}) copy-start(bf16[512,4,128]{2,1,0:T(4,128)(2,1)} %param.4) | copy-start | bytes 1572868
  3.6 55.1 %copy-start.3 = (bf16[512,4,128]{2,1,0:T(4,128)(2,1)S(1)}, bf16[512,4,128]{2,1,0:T(4,128)(2,1)}, u32[]{:S(2)}) copy-start(bf16[512,4,128]{2,1,0:T(4,128)(2,1)} %param.7) | copy-start | bytes 1572868
  3.6 43.3 %collective-permute-start = (bf16[4,4,256,128]{3,2,1,0:T(8,128)(2,1)S(1)}, bf16[4,4,256,128]{3,2,1,0:T(8,128)(2,1)S(1)}, u32[]{:S(2)}, u32[]{:S(2)}) collective-permute-start(bf16[4,4,256,128]{3,2,1,0:T(8,128)(2,1)S(1)} %get-tuple-element.33.outer), channel_id=1, source_target_pairs={{2,6},{4,0},{6,10},{8,4},{10,14},{12,8},{14,18},{16,12},{18,22},{2... | collective-permute-start | bytes 3145736 | tf_op jit(solution)/shard_map/ppermute | solution.py:22
  17.8 29.2 %collective-permute-start.1 = (bf16[2,4,256,128]{3,2,1,0:T(8,128)(2,1)S(1)}, bf16[2,4,256,128]{3,2,1,0:T(8,128)(2,1)S(1)}, u32[]{:S(2)}, u32[]{:S(2)}) collective-permute-start(bf16[2,4,256,128]{3,2,1,0:T(8,128)(2,1)S(1)} %get-tuple-element.35), channel_id=1, source_target_pairs={{0,4},{4,8},{6,2},{8,12},{10,6},{12,16},{14,10},{16,20},{18,14},{2... | collective-permute-start | bytes 1572872 | tf_op jit(solution)/shard_map/ppermute | solution.py:22
  19.7 27.2 %collective-permute-start.3 = (bf16[2,4,128,128]{3,2,1,0:T(8,128)(2,1)S(1)}, bf16[2,4,128,128]{3,2,1,0:T(8,128)(2,1)S(1)}, u32[]{:S(2)}, u32[]{:S(2)}) collective-permute-start(bf16[2,4,128,128]{3,2,1,0:T(8,128)(2,1)S(1)} %get-tuple-element.36), channel_id=1, source_target_pairs={{2,10},{6,14},{8,0},{10,18},{12,4},{14,22},{16,8},{18,26},{20,12},... | collective-permute-start | bytes 786440 | tf_op jit(solution)/shard_map/ppermute | solution.py:22
  24.1 22.8 %collective-permute-start.2 = (bf16[2,4,128,128]{3,2,1,0:T(8,128)(2,1)S(1)}, bf16[2,4,128,128]{3,2,1,0:T(8,128)(2,1)S(1)}, u32[]{:S(2)}, u32[]{:S(2)}) collective-permute-start(bf16[2,4,128,128]{3,2,1,0:T(8,128)(2,1)S(1)} %get-tuple-element.36), channel_id=1, source_target_pairs={{0,8},{4,12},{8,16},{10,2},{12,20},{14,6},{16,24},{18,10},{20,28},... | collective-permute-start | bytes 786440 | tf_op jit(solution)/shard_map/ppermute | solution.py:22
  47.0 23.6 %collective-permute-start.4 = (bf16[4,4,256,128]{3,2,1,0:T(8,128)(2,1)S(1)}, bf16[4,4,256,128]{3,2,1,0:T(8,128)(2,1)S(1)}, u32[]{:S(2)}, u32[]{:S(2)}) collective-permute-start(bf16[4,4,256,128]{3,2,1,0:T(8,128)(2,1)S(1)} %relay.1), channel_id=1, source_target_pairs={{0,2},{2,0},{4,6},{6,4},{8,10},{10,8},{12,14},{14,12},{16,18},{18,... | collective-permute-start | bytes 3145736 | tf_op jit(solution)/shard_map/ppermute | solution.py:27
  49.0 15.5 %collective-permute-start.6 = (bf16[2,4,64,128]{3,2,1,0:T(8,128)(2,1)S(1)}, bf16[2,4,64,128]{3,2,1,0:T(8,128)(2,1)S(1)}, u32[]{:S(2)}, u32[]{:S(2)}) collective-permute-start(bf16[2,4,64,128]{3,2,1,0:T(8,128)(2,1)S(1)} %get-tuple-element.37), channel_id=1, source_target_pairs={{2,18},{6,22},{10,26},{14,30},{16,0},{18,34},{20,4},{22,38},{24,8}... | collective-permute-start | bytes 393224 | tf_op jit(solution)/shard_map/ppermute | solution.py:22
  55.2 15.4 %collective-permute-start.5 = (bf16[2,4,64,128]{3,2,1,0:T(8,128)(2,1)S(1)}, bf16[2,4,64,128]{3,2,1,0:T(8,128)(2,1)S(1)}, u32[]{:S(2)}, u32[]{:S(2)}) collective-permute-start(bf16[2,4,64,128]{3,2,1,0:T(8,128)(2,1)S(1)} %get-tuple-element.37), channel_id=1, source_target_pairs={{0,16},{4,20},{8,24},{12,28},{16,32},{18,2},{20,36},{22,6},{24,40}... | collective-permute-start | bytes 393224 | tf_op jit(solution)/shard_map/ppermute | solution.py:22
  87.6 36.6 %collective-permute-start.7 = (bf16[4,4,256,128]{3,2,1,0:T(8,128)(2,1)S(1)}, bf16[4,4,256,128]{3,2,1,0:T(8,128)(2,1)S(1)}, u32[]{:S(2)}, u32[]{:S(2)}) collective-permute-start(bf16[4,4,256,128]{3,2,1,0:T(8,128)(2,1)S(1)} %get-tuple-element.43), channel_id=1, source_target_pairs={{0,2},{2,0},{4,6},{6,4},{8,10},{10,8},{12,14},{14,12},{16,18},{18,... | collective-permute-start | bytes 3145736 | tf_op jit(solution)/shard_map/ppermute | solution.py:27
  89.6 12.8 %collective-permute-start.8 = (bf16[2,4,64,128]{3,2,1,0:T(8,128)(2,1)S(1)}, bf16[2,4,64,128]{3,2,1,0:T(8,128)(2,1)S(1)}, u32[]{:S(2)}, u32[]{:S(2)}) collective-permute-start(bf16[2,4,64,128]{3,2,1,0:T(8,128)(2,1)S(1)} %get-tuple-element.44), channel_id=1, source_target_pairs={{2,10},{6,14},{8,0},{10,18},{12,4},{14,22},{16,8},{18,26},{20,12},... | collective-permute-start | bytes 393224 | tf_op jit(solution)/shard_map/ppermute | solution.py:22
  97.5 12.3 %collective-permute-start.9 = (bf16[2,4,64,128]{3,2,1,0:T(8,128)(2,1)S(1)}, bf16[2,4,64,128]{3,2,1,0:T(8,128)(2,1)S(1)}, u32[]{:S(2)}, u32[]{:S(2)}) collective-permute-start(bf16[2,4,64,128]{3,2,1,0:T(8,128)(2,1)S(1)} %get-tuple-element.45), channel_id=1, source_target_pairs={{0,8},{4,12},{8,16},{10,2},{12,20},{14,6},{16,24},{18,10},{20,28},... | collective-permute-start | bytes 393224 | tf_op jit(solution)/shard_map/ppermute | solution.py:22
  110.0 13.0 %collective-permute-start.11 = (bf16[2,4,128,128]{3,2,1,0:T(8,128)(2,1)S(1)}, bf16[2,4,128,128]{3,2,1,0:T(8,128)(2,1)S(1)}, u32[]{:S(2)}, u32[]{:S(2)}) collective-permute-start(bf16[2,4,128,128]{3,2,1,0:T(8,128)(2,1)S(1)} %bitcast.38), channel_id=1, source_target_pairs={{0,4},{4,8},{6,2},{8,12},{10,6},{12,16},{14,10},{16,20},{18,14},{2... | collective-permute-start | bytes 786440 | tf_op jit(solution)/shard_map/ppermute | solution.py:22
  111.9 12.3 %collective-permute-start.10 = (bf16[2,4,128,128]{3,2,1,0:T(8,128)(2,1)S(1)}, bf16[2,4,128,128]{3,2,1,0:T(8,128)(2,1)S(1)}, u32[]{:S(2)}, u32[]{:S(2)}) collective-permute-start(bf16[2,4,128,128]{3,2,1,0:T(8,128)(2,1)S(1)} %bitcast.37), channel_id=1, source_target_pairs={{2,6},{4,0},{6,10},{8,4},{10,14},{12,8},{14,18},{16,12},{18,22},{2... | collective-permute-start | bytes 786440 | tf_op jit(solution)/shard_map/ppermute | solution.py:22
  124.7 27.3 %collective-permute-start.13 = (bf16[4,4,256,128]{3,2,1,0:T(8,128)(2,1)S(1)}, bf16[4,4,256,128]{3,2,1,0:T(8,128)(2,1)S(1)}, u32[]{:S(2)}, u32[]{:S(2)}) collective-permute-start(bf16[4,4,256,128]{3,2,1,0:T(8,128)(2,1)S(1)} %bitcast.35), channel_id=1, source_target_pairs={{0,4},{4,8},{6,2},{8,12},{10,6},{12,16},{14,10},{16,20},{18,14},{2... | collective-permute-start | bytes 3145736 | tf_op jit(solution)/shard_map/ppermute | solution.py:22
  126.7 18.4 %collective-permute-start.12 = (bf16[2,4,256,128]{3,2,1,0:T(8,128)(2,1)S(1)}, bf16[2,4,256,128]{3,2,1,0:T(8,128)(2,1)S(1)}, u32[]{:S(2)}, u32[]{:S(2)}) collective-permute-start(bf16[2,4,256,128]{3,2,1,0:T(8,128)(2,1)S(1)} %bitcast.36), channel_id=1, source_target_pairs={{2,6},{4,0},{6,10},{8,4},{10,14},{12,8},{14,18},{16,12},{18,22},{2... | collective-permute-start | bytes 1572872 | tf_op jit(solution)/shard_map/ppermute | solution.py:22

commit v2 on v1

v2 whole, which is shorter than its diff:
```python
import functools
import math

import jax
import jax.numpy as jnp
from jax import lax
from jax.experimental import pallas as pl
from jax.experimental.pallas import tpu as pltpu
from jax.sharding import PartitionSpec as P

BLOCK = 256
LEVELS = 3
LOG2E = math.log2(math.e)

BF = jnp.bfloat16
F32 = jnp.float32


def crossed(value, steps):
    count = lax.axis_size("seq")
    pairs = [(at, at + (steps if at % 2 == 0 else -steps)) for at in range(count)]
    return lax.ppermute(value, "seq", [(at, to) for at, to in pairs if 0 <= to < count])


def swapped(value, across):
    count = lax.axis_size("seq")
    pairs = [(at, at ^ 1) for at in range(count)]
    if across:
        pairs = [(at, at + 1 if at % 2 else at - 1) for at in range(count)]
    return lax.ppermute(value, "seq", [(at, to) for at, to in pairs if 0 <= to < count])


def nt(left, right):
    return lax.dot_general(left, right, (((1,), (1,)), ((), ())), preferred_element_type=F32)


def nn(left, right):
    return jnp.dot(left, right, preferred_element_type=F32)


def shape(dims, dtype=BF):
    return jax.ShapeDtypeStruct(dims, dtype)


def params(mib):
    return pltpu.CompilerParams(vmem_limit_bytes=mib * 2**20)


SMEM_SPEC = pl.BlockSpec(memory_space=pltpu.SMEM)
VMEM_SPEC = pl.BlockSpec(memory_space=pltpu.VMEM)


def turned(wide, ref, odd):
    half = wide.shape[0] // 2
    wide[pl.ds(pl.multiple_of(odd * half, half), half), :] = ref[:half].astype(F32)
    wide[pl.ds(pl.multiple_of((1 - odd) * half, half), half), :] = ref[half:].astype(F32)


def turned_back(ref, wide, odd):
    half = wide.shape[0] // 2
    ref[pl.ds(pl.multiple_of(odd * half, half), half), :] = wide[:half].astype(BF)
    ref[pl.ds(pl.multiple_of((1 - odd) * half, half), half), :] = wide[half:].astype(BF)


def pair_sums(wide, row, size, heads):
    return (
        wide[pl.ds(row, size, stride=2 * heads), :]
        + wide[pl.ds(row + heads, size, stride=2 * heads), :]
    )


def next_sums(sums, total):
    size = total.shape[0]
    sums[pl.ds(0, size), :] = total
    half = size // 2
    return sums[pl.ds(0, half, stride=2), :] + sums[pl.ds(1, half, stride=2), :]


def split_kv_kernel(heads, place_ref, k_ref, v_ref, outer, inner, *rest):
    coarse, (wide, sums) = rest[:LEVELS], rest[LEVELS:]
    block = inner.shape[2]
    odd = lax.rem(place_ref[0], 2)
    for at, ref in enumerate((k_ref, v_ref)):
        turned(wide, ref, odd)
        for head in range(heads):
            outer[at, head] = wide[pl.ds(head, block, stride=heads), :].astype(BF)
            inner[at, head] = wide[pl.ds(head + heads * block, block, stride=heads), :].astype(BF)
            total = pair_sums(wide, head, block, heads)
            for level in range(LEVELS):
                coarse[level][at, head] = (total * (1.0 / 2 ** (level + 1))).astype(BF)
                if level + 1 < LEVELS:
                    total = next_sums(sums, total)


def split_kv(place, k2, v2, heads, span):
    block = span // 2
    outs = [shape((2, heads, block, 128))] * 2
    outs += [shape((2, heads, span // 2 ** (level + 1), 128)) for level in range(LEVELS)]
    return pl.pallas_call(
        functools.partial(split_kv_kernel, heads),
        out_shape=outs,
        in_specs=[SMEM_SPEC, VMEM_SPEC, VMEM_SPEC],
        scratch_shapes=[
            pltpu.VMEM((heads * span, 128), F32),
            pltpu.VMEM((block, 128), F32),
        ],
        compiler_params=params(16),
        name="split_kv",
        cost_estimate=pl.CostEstimate(flops=0, bytes_accessed=4 * 2**20, transcendentals=0),
    )(place, k2, v2)


def later_kernel(count, *refs):
    for at in range(count):
        refs[len(refs) - count + at][...] = refs[at][...]


def later(after, arrays):
    return pl.pallas_call(
        functools.partial(later_kernel, len(arrays)),
        out_shape=[shape(x.shape) for x in arrays],
        in_specs=[VMEM_SPEC] * len(arrays) + [pl.BlockSpec(memory_space=pl.ANY)] * len(after),
        compiler_params=params(8),
        name="later",
        cost_estimate=pl.CostEstimate(flops=0, bytes_accessed=2 * 2**20, transcendentals=0),
    )(*arrays, *after)


def exchange(firsts, seconds, outer, inner):
    steps = [2 ** (level + 1) for level in range(LEVELS)]
    down = [crossed(x, -step) for x, step in zip(firsts, steps)]
    rims = swapped(outer, True), swapped(inner, False)
    up = [
        crossed(x, step) for x, step in zip(later((*down[1:], rims[1]), seconds), steps)
    ]
    return down, up, rims


def split_qd_kernel(heads, place_ref, q_ref, d_ref, q_out, d_out, rep_out, wide, sums, spread):
    span = q_out.shape[1]
    odd = lax.rem(place_ref[0], 2)
    turned(wide, d_ref, odd)
    for head in range(heads):
        d_out[head] = wide[pl.ds(head, span, stride=heads), :].astype(BF)
    turned(wide, q_ref, odd)
    for head in range(heads):
        q_out[head] = wide[pl.ds(head, span, stride=heads), :].astype(BF)
        total = pair_sums(wide, head, span // 2, heads)
        for level in range(LEVELS):
            factor = 2 ** (level + 1)
            mean = (total * (1.0 / factor)).astype(BF).astype(F32)
            for row in range(factor):
                spread[pl.ds(row, span // factor, stride=factor), :] = mean
            rep_out[level, head] = spread[...].astype(BF)
            if level + 1 < LEVELS:
                total = next_sums(sums, total)


def split_qd(place, q2, d2, heads, span):
    return pl.pallas_call(
        functools.partial(split_qd_kernel, heads),
        out_shape=[
            shape((heads, span, 128)),
            shape((heads, span, 128)),
            shape((LEVELS, heads, span, 128)),
        ],
        in_specs=[SMEM_SPEC] + [VMEM_SPEC] * 2,
        scratch_shapes=[
            pltpu.VMEM((heads * span, 128), F32),
            pltpu.VMEM((span // 2, 128), F32),
            pltpu.VMEM((span, 128), F32),
        ],
        compiler_params=params(16),
        name="split_qd",
        cost_estimate=pl.CostEstimate(flops=0, bytes_accessed=8 * 2**20, transcendentals=0),
    )(place, q2, d2)


def attend_kernel(count, place_ref, q_ref, d_ref, rep_ref, outer, inner, rim_out, rim_in, *rest):
    crossed_a, crossed_b = rest[:LEVELS], rest[LEVELS : 2 * LEVELS]
    att, gq, own, g_out, g_in = rest[2 * LEVELS : 2 * LEVELS + 5]
    rest = rest[2 * LEVELS + 5 :]
    g_as, g_bs = rest[:LEVELS], rest[LEVELS : 2 * LEVELS]
    keys, vals, keys_t, vals_t, scores, grads, probs, dscores, rows, total_q = rest[2 * LEVELS :]
    place = place_ref[0]
    even = lax.rem(place, 2) == 0
    block = outer.shape[2]
    scale = 1.0 / math.sqrt(128)
    scale2 = scale * LOG2E

    def reaches(below, steps):
        return jnp.where(below, place >= steps, place < count - steps)

    parts = [(rim_out, reaches(even, 1), 0), (outer, None, 0), (inner, None, 0)]
    for level in range(LEVELS):
        factor = 2 ** (level + 1)
        parts.append((crossed_a[level], reaches(even, factor), level + 1))
        parts.append((crossed_b[level], reaches(jnp.logical_not(even), factor), level + 1))
    parts.append((rim_in, None, 0))
    at = 0
    segments = []
    for ref, ok, level in parts:
        size = ref.shape[2]
        keys[pl.ds(at, size), :] = ref[0, 0]
        vals[pl.ds(at, size), :] = ref[1, 0]
        bias = float(level)
        if ok is not None:
            bias = jnp.where(ok, bias, -jnp.inf).astype(F32)
        segments.append((at, size, bias, level))
        at += size
    columns = at
    keys_t[...] = keys[...].T
    vals_t[...] = vals[...].T

    turns = (0, 1)
    cols = [pl.ds(turn * block, block) for turn in turns]
    met = [segments[:-1], segments[1:]]
    top = [None, None]
    for turn in turns:
        d_blk = d_ref[0, cols[turn], :]
        using = [q_ref[0, cols[turn], :]]
        using += [rep_ref[level, 0, cols[turn], :] for level in range(LEVELS)]
        for start, size, bias, level in met[turn]:
            here = pl.ds(start, size)
            s = nt(keys[here, :], using[level])
            scores[turn, here, :] = s
            high = jnp.max(s, axis=0, keepdims=True) * scale2 + bias
            top[turn] = high if top[turn] is None else jnp.maximum(top[turn], high)
            grads[turn, here, :] = nt(vals[here, :], d_blk)
    inverse, delta = [None, None], [None, None]
    for turn in turns:
        total = jnp.zeros((1, block), F32)
        acc = jnp.zeros((1, block), F32)
        for start, size, bias, level in met[turn]:
            here = pl.ds(start, size)
            e = jnp.exp2(scores[turn, here, :] * scale2 - (top[turn] - bias))
            scores[turn, here, :] = e
            total = total + jnp.sum(e, axis=0, keepdims=True)
            acc = acc + jnp.sum(e * grads[turn, here, :], axis=0, keepdims=True)
        inverse[turn] = 1.0 / total
        delta[turn] = acc * inverse[turn]
    for turn in turns:
        for start, size, bias, level in met[turn]:
            here = pl.ds(start, size)
            p = scores[turn, here, :] * inverse[turn]
            probs[here, cols[turn]] = p.astype(BF)
            dscores[here, cols[turn]] = (p * (grads[turn, here, :] - delta[turn])).astype(BF)
        first, last = met[turn][0][0], met[turn][-1][0] + met[turn][-1][1]
        up = nn(vals_t[:, first:last], probs[first:last, cols[turn]])
        att[0, cols[turn], :] = up.T.astype(BF)
        if turn == 0:
            fine = nn(keys_t[:, : 3 * block], dscores[: 3 * block, cols[turn]])
        else:
            fine = nn(keys_t[:, block : 3 * block], dscores[block : 3 * block, cols[turn]])
            tail = columns - block
            fine = fine + nn(keys_t[:, tail:], dscores[tail:, cols[turn]])
        total_q[turn] = fine.T
        for level in range(1, LEVELS + 1):
            spots = [(s, z) for s, z, _, lev in segments if lev == level]
            start, size = spots[0][0], spots[0][1] + spots[1][1]
            up = nn(keys_t[:, start : start + size], dscores[start : start + size, cols[turn]])
            rows[turn, level - 1] = up.T
            factor = 2**level
            groups = block // factor
            mean = rows[turn, level - 1, pl.ds(0, groups, stride=factor), :]
            for row in range(1, factor):
                mean = mean + rows[turn, level - 1, pl.ds(row, groups, stride=factor), :]
            mean = mean * (1.0 / factor)
            for row in range(factor):
                spot = pl.ds(row, groups, stride=factor)
                total_q[turn, spot, :] = total_q[turn, spot, :] + mean
        gq[0, cols[turn], :] = (total_q[turn] * scale).astype(BF)

    places = [(g_out, None), (own, 0), (own, block)]
    for level in range(LEVELS):
        places += [(g_as[level], None), (g_bs[level], None)]
    places.append((g_in, None))
    for (ref, offset), (start, size, bias, level) in zip(places, segments):
        queries = pl.ds(0, 2 * block)
        if ref is g_out:
            queries = cols[0]
        if ref is g_in:
            queries = cols[1]
        right = rep_ref[level - 1, 0, queries, :] if level else q_ref[0, queries, :]
        here = pl.ds(start, size)
        gk = nn(dscores[here, queries], right) * scale
        gv = nn(probs[here, queries], d_ref[0, queries, :])
        for which, value in enumerate((gk, gv)):
            if offset is None:
                ref[which, 0] = value.astype(BF)
            else:
                ref[which, 0, pl.ds(offset, size), :] = value


def attend(place, count, q, d, rep, outer, inner, rim_out, rim_in, crossed_a, crossed_b):
    heads, block = inner.shape[1], inner.shape[2]
    span = 2 * block
    sizes = [span // 2 ** (level + 1) for level in range(LEVELS)]
    columns = 4 * block + 2 * sum(sizes)
    width = columns - block

    def pair(size):
        return pl.BlockSpec((2, 1, size, 128), lambda h: (0, h, 0, 0))

    head_spec = pl.BlockSpec((1, span, 128), lambda h: (h, 0, 0))
    flops = 2 * heads * span * width * 128 * 6
    return pl.pallas_call(
        functools.partial(attend_kernel, count),
        grid=(heads,),
        in_specs=[
            SMEM_SPEC,
            head_spec,
            head_spec,
            pl.BlockSpec((LEVELS, 1, span, 128), lambda h: (0, h, 0, 0)),
        ]
        + [pair(block)] * 4
        + [pair(size) for size in sizes] * 2,
        out_specs=[head_spec, head_spec, pair(span), pair(block), pair(block)]
        + [pair(size) for size in sizes] * 2,
        out_shape=[
            shape((heads, span, 128)),
            shape((heads, span, 128)),
            shape((2, heads, span, 128), F32),
            shape((2, heads, block, 128)),
            shape((2, heads, block, 128)),
        ]
        + [shape((2, heads, size, 128)) for size in sizes] * 2,
        scratch_shapes=[
            pltpu.VMEM((columns, 128), BF),
            pltpu.VMEM((columns, 128), BF),
            pltpu.VMEM((128, columns), BF),
            pltpu.VMEM((128, columns), BF),
            pltpu.VMEM((2, columns, block), F32),
            pltpu.VMEM((2, columns, block), F32),
            pltpu.VMEM((columns, span), BF),
            pltpu.VMEM((columns, span), BF),
            pltpu.VMEM((2, LEVELS, block, 128), F32),
            pltpu.VMEM((2, block, 128), F32),
        ],
        compiler_params=params(30),
        name="attend",
        cost_estimate=pl.CostEstimate(
            flops=flops, bytes_accessed=8 * 2**20, transcendentals=heads * span * width
        ),
    )(place, q, d, rep, outer, inner, rim_out, rim_in, *crossed_a, *crossed_b)


def join_kernel(heads, place_ref, att, gq, att_out, gq_out, wide):
    span = att.shape[1]
    odd = lax.rem(place_ref[0], 2)
    for ref, out in ((att, att_out), (gq, gq_out)):
        for head in range(heads):
            wide[pl.ds(head, span, stride=heads), :] = ref[head].astype(F32)
        turned_back(out, wide, odd)


def join(place, att, gq):
    heads, span = att.shape[:2]
    return pl.pallas_call(
        functools.partial(join_kernel, heads),
        out_shape=[shape((heads * span, 128))] * 2,
        in_specs=[SMEM_SPEC, VMEM_SPEC, VMEM_SPEC],
        scratch_shapes=[pltpu.VMEM((heads * span, 128), F32)],
        compiler_params=params(12),
        name="join",
        cost_estimate=pl.CostEstimate(flops=0, bytes_accessed=4 * 2**20, transcendentals=0),
    )(place, att, gq)


def gather_kernel(heads, place_ref, own, outer, inner, *refs):
    downs, ups, outs = refs[:LEVELS], refs[LEVELS : 2 * LEVELS], refs[2 * LEVELS : 2 * LEVELS + 2]
    wide, mine, spread = refs[2 * LEVELS + 2 :]
    span = own.shape[2]
    block = span // 2
    odd = lax.rem(place_ref[0], 2)
    for which, out in enumerate(outs):
        for head in range(heads):
            both = None
            for level in reversed(range(LEVELS)):
                value = downs[level][which, head].astype(F32) + ups[level][which, head].astype(F32)
                value = value * (1.0 / 2 ** (level + 1))
                if both is not None:
                    size = both.shape[0]
                    spread[pl.ds(0, size, stride=2), :] = both
                    spread[pl.ds(1, size, stride=2), :] = both
                    value = value + spread[pl.ds(0, 2 * size), :]
                both = value
            mine[pl.ds(0, block), :] = own[which, head, :block] + outer[which, head].astype(F32)
            mine[pl.ds(block, block), :] = own[which, head, block:] + inner[which, head].astype(F32)
            for second in range(2):
                wide[pl.ds(head + heads * second, block, stride=2 * heads), :] = (
                    mine[pl.ds(second, block, stride=2), :] + both
                )
        turned_back(out, wide, odd)


def gather(place, own, *sums):
    heads, span = own.shape[1:3]
    return pl.pallas_call(
        functools.partial(gather_kernel, heads),
        out_shape=[shape((heads * span, 128))] * 2,
        in_specs=[SMEM_SPEC] + [VMEM_SPEC] * (1 + len(sums)),
        scratch_shapes=[
            pltpu.VMEM((heads * span, 128), F32),
            pltpu.VMEM((span, 128), F32),
            pltpu.VMEM((span // 2, 128), F32),
        ],
        compiler_params=params(16),
        name="gather",
        cost_estimate=pl.CostEstimate(flops=0, bytes_accessed=8 * 2**20, transcendentals=0),
    )(place, own, *sums)


def local(query, key, value, dout):
    span, heads, width = query.shape
    count = lax.axis_size("seq")
    place = jnp.reshape(lax.axis_index("seq"), (1,)).astype(jnp.int32)
    flat = (heads * span, width)
    q2, k2, v2, d2 = (x.reshape(flat) for x in (query, key, value, dout))
    outer, inner, *coarse = split_kv(place, k2, v2, heads, span)
    crossed_b, crossed_a, rims = exchange(coarse, coarse, outer, inner)
    qh, dh, rep = split_qd(place, q2, d2, heads, span)
    att, gq, own, g_out, g_in, *grads = attend(
        place, count, qh, dh, rep, outer, inner, *rims, crossed_a, crossed_b
    )
    downs, ups, rims = exchange(grads[:LEVELS], grads[LEVELS:], g_out, g_in)
    attended, grad_query = join(place, att, gq)
    grad_key, grad_value = gather(place, own, *rims, *downs, *ups)
    return tuple(
        x.reshape(span, heads, width) for x in (attended, grad_query, grad_key, grad_value)
    )


def solution(mesh):
    placed = P("seq", "head", None)
    return jax.shard_map(
        local,
        mesh=mesh,
        in_specs=(placed,) * 4,
        out_specs=(placed,) * 4,
        check_vma=False,
    )
```

time: 154 us -> 134 us (0.87)
  the two profiles are of different devices: /device:TPU:24 before, /device:TPU:25 now
where the time goes in v2:
time: 134 us; the launch traced here: 133 us
  starting transfers between devices  75.1 us (56%)
  waiting for transfers between devices  32.5 us (24%)
  Pallas kernels  22.8 us (17%)
  local copies, waits for them, and re-layouts  2.08 us (2%)
    ppermute x12, starting transfers between devices, crossed(): lax.ppermute(value, 'seq', [(at, to) for at, to in pairs if 0 <= to < cou...  51.4 us
    ppermute x12, waiting for transfers between devices, crossed(): lax.ppermute(value, 'seq', [(at, to) for at, to in pairs if 0 <= to < cou...  32.5 us
    ppermute x4, starting transfers between devices, swapped(): lax.ppermute(value, 'seq', [(at, to) for at, to in pairs if 0 <= to < cou...  23.8 us
    pallas_call x1, Pallas kernels, attend(): pl.pallas_call(functools.partial(attend_kernel, count), grid=(heads,), in...  17.7 us
  transfers between devices with their start and end apart: 16, of which 6 were waited for; matrix products, arithmetic and copies ran while one was open for 0% of the time, Pallas kernels for 2%

profile of v2, /device:TPU:25, one launch (start us, length us, event | category | flops | bytes accessed | tf_op | source)
XLA Modules:
  0.0 133.3 jit_solution(6288692257336330401)
XLA Ops:
  0.6 1.0 copy-done
  1.7 1.0 copy-done.1
  2.7 0.9 split_kv.1
  3.6 2.6 %collective-permute-start.1 = (bf16[2,4,256,128]{3,2,1,0:T(8,128)(2,1)S(1)}, bf16[2,4,256,128]{3,2,1,0:T(8,128)(2,1)S(1)}, u32[]{:S(2)}, u32[]{:S(2)}) collective-permute-start(bf16[2,4,256,128]{3,2,1,0:T(8,128)(2,1)S(1)} %get-tuple-element.37.inner), channel_id=1, source_target_pairs={{0,2},{2,0},{4,6},{6,4},{8,10},{10,8},{12,14},{14,12},{16,18},{18,... | collective-permute-start | bytes 1572872 | tf_op jit(solution)/shard_map/ppermute | solution.py:30
  6.2 4.9 %collective-permute-start.2 = (bf16[2,4,128,128]{3,2,1,0:T(8,128)(2,1)S(1)}, bf16[2,4,128,128]{3,2,1,0:T(8,128)(2,1)S(1)}, u32[]{:S(2)}, u32[]{:S(2)}) collective-permute-start(bf16[2,4,128,128]{3,2,1,0:T(8,128)(2,1)S(1)} %get-tuple-element.39.refs_1_), channel_id=1, source_target_pairs={{2,10},{6,14},{8,0},{10,18},{12,4},{14,22},{16,8},{18,26},{20,12},... | collective-permute-start | bytes 786440 | tf_op jit(solution)/shard_map/ppermute | solution.py:22
  11.1 8.8 %collective-permute-start.3 = (bf16[2,4,64,128]{3,2,1,0:T(8,128)(2,1)S(1)}, bf16[2,4,64,128]{3,2,1,0:T(8,128)(2,1)S(1)}, u32[]{:S(2)}, u32[]{:S(2)}) collective-permute-start(bf16[2,4,64,128]{3,2,1,0:T(8,128)(2,1)S(1)} %get-tuple-element.40.refs_2_), channel_id=1, source_target_pairs={{2,18},{6,22},{10,26},{14,30},{16,0},{18,34},{20,4},{22,38},{24,8}... | collective-permute-start | bytes 393224 | tf_op jit(solution)/shard_map/ppermute | solution.py:22
  19.9 8.8 %collective-permute-start = (bf16[2,4,256,128]{3,2,1,0:T(8,128)(2,1)S(1)}, bf16[2,4,256,128]{3,2,1,0:T(8,128)(2,1)S(1)}, u32[]{:S(2)}, u32[]{:S(2)}) collective-permute-start(bf16[2,4,256,128]{3,2,1,0:T(8,128)(2,1)S(1)} %get-tuple-element.36.outer), channel_id=1, source_target_pairs={{2,4},{4,2},{6,8},{8,6},{10,12},{12,10},{14,16},{16,14},{18,20},{2... | collective-permute-start | bytes 1572872 | tf_op jit(solution)/shard_map/ppermute | solution.py:30
  28.7 1.9 %collective-permute-start.7 = (bf16[2,4,256,128]{3,2,1,0:T(8,128)(2,1)S(1)}, bf16[2,4,256,128]{3,2,1,0:T(8,128)(2,1)S(1)}, u32[]{:S(2)}, u32[]{:S(2)}) collective-permute-start(bf16[2,4,256,128]{3,2,1,0:T(8,128)(2,1)S(1)} %get-tuple-element.38.refs_0_), channel_id=1, source_target_pairs={{2,6},{4,0},{6,10},{8,4},{10,14},{12,8},{14,18},{16,12},{18,22},{2... | collective-permute-start | bytes 1572872 | tf_op jit(solution)/shard_map/ppermute | solution.py:22
  30.6 0.6 collective-permute-done.3.refs_4_.rest_5_
  31.2 0.0 collective-permute-done.2.refs_3_.rest_4_
  31.2 0.1 later.2
  31.3 7.5 %collective-permute-start.4 = (bf16[2,4,256,128]{3,2,1,0:T(8,128)(2,1)S(1)}, bf16[2,4,256,128]{3,2,1,0:T(8,128)(2,1)S(1)}, u32[]{:S(2)}, u32[]{:S(2)}) collective-permute-start(bf16[2,4,256,128]{3,2,1,0:T(8,128)(2,1)S(1)} %get-tuple-element.41), channel_id=1, source_target_pairs={{0,4},{4,8},{6,2},{8,12},{10,6},{12,16},{14,10},{16,20},{18,14},{2... | collective-permute-start | bytes 1572872 | tf_op jit(solution)/shard_map/ppermute | solution.py:22
  38.8 2.2 %collective-permute-start.5 = (bf16[2,4,128,128]{3,2,1,0:T(8,128)(2,1)S(1)}, bf16[2,4,128,128]{3,2,1,0:T(8,128)(2,1)S(1)}, u32[]{:S(2)}, u32[]{:S(2)}) collective-permute-start(bf16[2,4,128,128]{3,2,1,0:T(8,128)(2,1)S(1)} %get-tuple-element.42), channel_id=1, source_target_pairs={{0,8},{4,12},{8,16},{10,2},{12,20},{14,6},{16,24},{18,10},{20,28},... | collective-permute-start | bytes 786440 | tf_op jit(solution)/shard_map/ppermute | solution.py:22
  41.0 5.0 %collective-permute-start.6 = (bf16[2,4,64,128]{3,2,1,0:T(8,128)(2,1)S(1)}, bf16[2,4,64,128]{3,2,1,0:T(8,128)(2,1)S(1)}, u32[]{:S(2)}, u32[]{:S(2)}) collective-permute-start(bf16[2,4,64,128]{3,2,1,0:T(8,128)(2,1)S(1)} %get-tuple-element.43), channel_id=1, source_target_pairs={{0,16},{4,20},{8,24},{12,28},{16,32},{18,2},{20,36},{22,6},{24,40}... | collective-permute-start | bytes 393224 | tf_op jit(solution)/shard_map/ppermute | solution.py:22
  46.0 0.9 split_qd.1
  46.9 3.0 %collective-permute-done.7.rest_3_ = bf16[2,4,256,128]{3,2,1,0:T(8,128)(2,1)S(1)} collective-permute-done((bf16[2,4,256,128]{3,2,1,0:T(8,128)(2,1)S(1)}, bf16[2,4,256,128]{3,2,1,0:T(8,128)(2,1)S(1)}, u32[]{:S(2)}, u32[]{:S(2)}) %collective-permute-start.7) | collective-permute-done | bytes 524320 | tf_op jit(solution)/shard_map/ppermute | solution.py:22
  50.0 10.8 %collective-permute-done.6.rest_2_ = bf16[2,4,64,128]{3,2,1,0:T(8,128)(2,1)S(1)} collective-permute-done((bf16[2,4,64,128]{3,2,1,0:T(8,128)(2,1)S(1)}, bf16[2,4,64,128]{3,2,1,0:T(8,128)(2,1)S(1)}, u32[]{:S(2)}, u32[]{:S(2)}) %collective-permute-start.6) | collective-permute-done | bytes 131104 | tf_op jit(solution)/shard_map/ppermute | solution.py:22
  60.8 17.7 %attend.1 = (bf16[4,512,128]{2,1,0:T(8,128)(2,1)S(1)}, bf16[4,512,128]{2,1,0:T(8,128)(2,1)S(1)}, f32[2,4,512,128]{3,2,1,0:T(8,128)S(1)}, bf16[2,4,256,128]{3,2,1...) custom-call(s32[1]{0:T(128)} %bitcast.place_ref, ...), custom_call_target="tpu_custom_call" | custom-call | flops 5234491392 | bytes 8388608 | tf_op jit(solution)/shard_map/attend/pallas_call | solution.py:307
  78.5 1.9 %collective-permute-start.9 = (bf16[2,4,256,128]{3,2,1,0:T(8,128)(2,1)S(1)}, bf16[2,4,256,128]{3,2,1,0:T(8,128)(2,1)S(1)}, u32[]{:S(2)}, u32[]{:S(2)}) collective-permute-start(bf16[2,4,256,128]{3,2,1,0:T(8,128)(2,1)S(1)} %get-tuple-element.50), channel_id=1, source_target_pairs={{0,2},{2,0},{4,6},{6,4},{8,10},{10,8},{12,14},{14,12},{16,18},{18,... | collective-permute-start | bytes 1572872 | tf_op jit(solution)/shard_map/ppermute | solution.py:30
  80.4 1.9 %collective-permute-start.11 = (bf16[2,4,128,128]{3,2,1,0:T(8,128)(2,1)S(1)}, bf16[2,4,128,128]{3,2,1,0:T(8,128)(2,1)S(1)}, u32[]{:S(2)}, u32[]{:S(2)}) collective-permute-start(bf16[2,4,128,128]{3,2,1,0:T(8,128)(2,1)S(1)} %get-tuple-element.52), channel_id=1, source_target_pairs={{2,10},{6,14},{8,0},{10,18},{12,4},{14,22},{16,8},{18,26},{20,12},... | collective-permute-start | bytes 786440 | tf_op jit(solution)/shard_map/ppermute | solution.py:22
  82.3 3.5 %collective-permute-start.12 = (bf16[2,4,64,128]{3,2,1,0:T(8,128)(2,1)S(1)}, bf16[2,4,64,128]{3,2,1,0:T(8,128)(2,1)S(1)}, u32[]{:S(2)}, u32[]{:S(2)}) collective-permute-start(bf16[2,4,64,128]{3,2,1,0:T(8,128)(2,1)S(1)} %get-tuple-element.53), channel_id=1, source_target_pairs={{2,18},{6,22},{10,26},{14,30},{16,0},{18,34},{20,4},{22,38},{24,8}... | collective-permute-start | bytes 393224 | tf_op jit(solution)/shard_map/ppermute | solution.py:22
  85.8 10.5 %collective-permute-start.8 = (bf16[2,4,256,128]{3,2,1,0:T(8,128)(2,1)S(1)}, bf16[2,4,256,128]{3,2,1,0:T(8,128)(2,1)S(1)}, u32[]{:S(2)}, u32[]{:S(2)}) collective-permute-start(bf16[2,4,256,128]{3,2,1,0:T(8,128)(2,1)S(1)} %get-tuple-element.49), channel_id=1, source_target_pairs={{2,4},{4,2},{6,8},{8,6},{10,12},{12,10},{14,16},{16,14},{18,20},{2... | collective-permute-start | bytes 1572872 | tf_op jit(solution)/shard_map/ppermute | solution.py:30
  96.3 4.4 %collective-permute-start.10 = (bf16[2,4,256,128]{3,2,1,0:T(8,128)(2,1)S(1)}, bf16[2,4,256,128]{3,2,1,0:T(8,128)(2,1)S(1)}, u32[]{:S(2)}, u32[]{:S(2)}) collective-permute-start(bf16[2,4,256,128]{3,2,1,0:T(8,128)(2,1)S(1)} %get-tuple-element.51), channel_id=1, source_target_pairs={{2,6},{4,0},{6,10},{8,4},{10,14},{12,8},{14,18},{16,12},{18,22},{2... | collective-permute-start | bytes 1572872 | tf_op jit(solution)/shard_map/ppermute | solution.py:22
  100.8 0.3 collective-permute-done.12.refs_4_.refs_2_
  101.0 0.1 later.3
  101.1 6.5 %collective-permute-start.13 = (bf16[2,4,256,128]{3,2,1,0:T(8,128)(2,1)S(1)}, bf16[2,4,256,128]{3,2,1,0:T(8,128)(2,1)S(1)}, u32[]{:S(2)}, u32[]{:S(2)}) collective-permute-start(bf16[2,4,256,128]{3,2,1,0:T(8,128)(2,1)S(1)} %get-tuple-element.57), channel_id=1, source_target_pairs={{0,4},{4,8},{6,2},{8,12},{10,6},{12,16},{14,10},{16,20},{18,14},{2... | collective-permute-start | bytes 1572872 | tf_op jit(solution)/shard_map/ppermute | solution.py:22
  107.6 1.9 %collective-permute-start.14 = (bf16[2,4,128,128]{3,2,1,0:T(8,128)(2,1)S(1)}, bf16[2,4,128,128]{3,2,1,0:T(8,128)(2,1)S(1)}, u32[]{:S(2)}, u32[]{:S(2)}) collective-permute-start(bf16[2,4,128,128]{3,2,1,0:T(8,128)(2,1)S(1)} %get-tuple-element.58), channel_id=1, source_target_pairs={{0,8},{4,12},{8,16},{10,2},{12,20},{14,6},{16,24},{18,10},{20,28},... | collective-permute-start | bytes 786440 | tf_op jit(solution)/shard_map/ppermute | solution.py:22
  109.5 2.8 %collective-permute-start.15 = (bf16[2,4,64,128]{3,2,1,0:T(8,128)(2,1)S(1)}, bf16[2,4,64,128]{3,2,1,0:T(8,128)(2,1)S(1)}, u32[]{:S(2)}, u32[]{:S(2)}) collective-permute-start(bf16[2,4,64,128]{3,2,1,0:T(8,128)(2,1)S(1)} %get-tuple-element.59), channel_id=1, source_target_pairs={{0,16},{4,20},{8,24},{12,28},{16,32},{18,2},{20,36},{22,6},{24,40}... | collective-permute-start | bytes 393224 | tf_op jit(solution)/shard_map/ppermute | solution.py:22
  112.3 1.2 join.1
  113.5 1.3 %collective-permute-done.10.refs_0_ = bf16[2,4,256,128]{3,2,1,0:T(8,128)(2,1)S(1)} collective-permute-done((bf16[2,4,256,128]{3,2,1,0:T(8,128)(2,1)S(1)}, bf16[2,4,256,128]{3,2,1,0:T(8,128)(2,1)S(1)}, u32[]{:S(2)}, u32[]{:S(2)}) %collective-permute-start.10) | collective-permute-done | bytes 524320 | tf_op jit(solution)/shard_map/ppermute | solution.py:22
  114.9 16.5 %collective-permute-done.15.refs_5_ = bf16[2,4,64,128]{3,2,1,0:T(8,128)(2,1)S(1)} collective-permute-done((bf16[2,4,64,128]{3,2,1,0:T(8,128)(2,1)S(1)}, bf16[2,4,64,128]{3,2,1,0:T(8,128)(2,1)S(1)}, u32[]{:S(2)}, u32[]{:S(2)}) %collective-permute-start.15) | collective-permute-done | bytes 131104 | tf_op jit(solution)/shard_map/ppermute | solution.py:22
  131.3 2.0 %gather.1 = (bf16[2048,128]{1,0:T(8,128)(2,1)}, bf16[2048,128]{1,0:T(8,128)(2,1)}) custom-call(s32[1]{0:T(128)} %bitcast.place_ref, f32[2,4,512,128]{3,2,1,0:T(8,128)S(1)} %get-tuple-element.48.own, bf16[2,4,256,128]{3,2,1,0:T(8,128)(2,1)S(1)} %collective-permute-done.8.outer, bf16[2,4,256,128]{3,2,1,0:T(8,128)(2,1)S(1)} %collective-permute-done.9.refs_5_.inner, ...), custom_call_target="tpu_custom_call" | custom-call | bytes 8388608 | tf_op jit(solution)/shard_map/gather/pallas_call | solution.py:399
  (15 shorter events, 0.0 us)
Async XLA Ops:
  0.6 1.0 copy-start
  1.7 1.0 copy-start.1
  2.7 43.2 %copy-start.2 = (bf16[512,4,128]{2,1,0:T(4,128)(2,1)S(1)}, bf16[512,4,128]{2,1,0:T(4,128)(2,1)}, u32[]{:S(2)}) copy-start(bf16[512,4,128]{2,1,0:T(4,128)(2,1)} %param.4) | copy-start | bytes 1572868
  2.7 43.3 %copy-start.3 = (bf16[512,4,128]{2,1,0:T(4,128)(2,1)S(1)}, bf16[512,4,128]{2,1,0:T(4,128)(2,1)}, u32[]{:S(2)}) copy-start(bf16[512,4,128]{2,1,0:T(4,128)(2,1)} %param.7) | copy-start | bytes 1572868
  3.6 27.6 %collective-permute-start.1 = (bf16[2,4,256,128]{3,2,1,0:T(8,128)(2,1)S(1)}, bf16[2,4,256,128]{3,2,1,0:T(8,128)(2,1)S(1)}, u32[]{:S(2)}, u32[]{:S(2)}) collective-permute-start(bf16[2,4,256,128]{3,2,1,0:T(8,128)(2,1)S(1)} %get-tuple-element.37.inner), channel_id=1, source_target_pairs={{0,2},{2,0},{4,6},{6,4},{8,10},{10,8},{12,14},{14,12},{16,18},{18,... | collective-permute-start | bytes 1572872 | tf_op jit(solution)/shard_map/ppermute | solution.py:30
  6.2 25.0 %collective-permute-start.2 = (bf16[2,4,128,128]{3,2,1,0:T(8,128)(2,1)S(1)}, bf16[2,4,128,128]{3,2,1,0:T(8,128)(2,1)S(1)}, u32[]{:S(2)}, u32[]{:S(2)}) collective-permute-start(bf16[2,4,128,128]{3,2,1,0:T(8,128)(2,1)S(1)} %get-tuple-element.39.refs_1_), channel_id=1, source_target_pairs={{2,10},{6,14},{8,0},{10,18},{12,4},{14,22},{16,8},{18,26},{20,12},... | collective-permute-start | bytes 786440 | tf_op jit(solution)/shard_map/ppermute | solution.py:22
  11.1 20.1 %collective-permute-start.3 = (bf16[2,4,64,128]{3,2,1,0:T(8,128)(2,1)S(1)}, bf16[2,4,64,128]{3,2,1,0:T(8,128)(2,1)S(1)}, u32[]{:S(2)}, u32[]{:S(2)}) collective-permute-start(bf16[2,4,64,128]{3,2,1,0:T(8,128)(2,1)S(1)} %get-tuple-element.40.refs_2_), channel_id=1, source_target_pairs={{2,18},{6,22},{10,26},{14,30},{16,0},{18,34},{20,4},{22,38},{24,8}... | collective-permute-start | bytes 393224 | tf_op jit(solution)/shard_map/ppermute | solution.py:22
  19.9 27.0 %collective-permute-start = (bf16[2,4,256,128]{3,2,1,0:T(8,128)(2,1)S(1)}, bf16[2,4,256,128]{3,2,1,0:T(8,128)(2,1)S(1)}, u32[]{:S(2)}, u32[]{:S(2)}) collective-permute-start(bf16[2,4,256,128]{3,2,1,0:T(8,128)(2,1)S(1)} %get-tuple-element.36.outer), channel_id=1, source_target_pairs={{2,4},{4,2},{6,8},{8,6},{10,12},{12,10},{14,16},{16,14},{18,20},{2... | collective-permute-start | bytes 1572872 | tf_op jit(solution)/shard_map/ppermute | solution.py:30
  28.7 21.3 %collective-permute-start.7 = (bf16[2,4,256,128]{3,2,1,0:T(8,128)(2,1)S(1)}, bf16[2,4,256,128]{3,2,1,0:T(8,128)(2,1)S(1)}, u32[]{:S(2)}, u32[]{:S(2)}) collective-permute-start(bf16[2,4,256,128]{3,2,1,0:T(8,128)(2,1)S(1)} %get-tuple-element.38.refs_0_), channel_id=1, source_target_pairs={{2,6},{4,0},{6,10},{8,4},{10,14},{12,8},{14,18},{16,12},{18,22},{2... | collective-permute-start | bytes 1572872 | tf_op jit(solution)/shard_map/ppermute | solution.py:22
  31.3 29.5 %collective-permute-start.4 = (bf16[2,4,256,128]{3,2,1,0:T(8,128)(2,1)S(1)}, bf16[2,4,256,128]{3,2,1,0:T(8,128)(2,1)S(1)}, u32[]{:S(2)}, u32[]{:S(2)}) collective-permute-start(bf16[2,4,256,128]{3,2,1,0:T(8,128)(2,1)S(1)} %get-tuple-element.41), channel_id=1, source_target_pairs={{0,4},{4,8},{6,2},{8,12},{10,6},{12,16},{14,10},{16,20},{18,14},{2... | collective-permute-start | bytes 1572872 | tf_op jit(solution)/shard_map/ppermute | solution.py:22
  38.8 21.9 %collective-permute-start.5 = (bf16[2,4,128,128]{3,2,1,0:T(8,128)(2,1)S(1)}, bf16[2,4,128,128]{3,2,1,0:T(8,128)(2,1)S(1)}, u32[]{:S(2)}, u32[]{:S(2)}) collective-permute-start(bf16[2,4,128,128]{3,2,1,0:T(8,128)(2,1)S(1)} %get-tuple-element.42), channel_id=1, source_target_pairs={{0,8},{4,12},{8,16},{10,2},{12,20},{14,6},{16,24},{18,10},{20,28},... | collective-permute-start | bytes 786440 | tf_op jit(solution)/shard_map/ppermute | solution.py:22
  41.0 19.8 %collective-permute-start.6 = (bf16[2,4,64,128]{3,2,1,0:T(8,128)(2,1)S(1)}, bf16[2,4,64,128]{3,2,1,0:T(8,128)(2,1)S(1)}, u32[]{:S(2)}, u32[]{:S(2)}) collective-permute-start(bf16[2,4,64,128]{3,2,1,0:T(8,128)(2,1)S(1)} %get-tuple-element.43), channel_id=1, source_target_pairs={{0,16},{4,20},{8,24},{12,28},{16,32},{18,2},{20,36},{22,6},{24,40}... | collective-permute-start | bytes 393224 | tf_op jit(solution)/shard_map/ppermute | solution.py:22
  78.5 22.6 %collective-permute-start.9 = (bf16[2,4,256,128]{3,2,1,0:T(8,128)(2,1)S(1)}, bf16[2,4,256,128]{3,2,1,0:T(8,128)(2,1)S(1)}, u32[]{:S(2)}, u32[]{:S(2)}) collective-permute-start(bf16[2,4,256,128]{3,2,1,0:T(8,128)(2,1)S(1)} %get-tuple-element.50), channel_id=1, source_target_pairs={{0,2},{2,0},{4,6},{6,4},{8,10},{10,8},{12,14},{14,12},{16,18},{18,... | collective-permute-start | bytes 1572872 | tf_op jit(solution)/shard_map/ppermute | solution.py:30
  80.4 20.7 %collective-permute-start.11 = (bf16[2,4,128,128]{3,2,1,0:T(8,128)(2,1)S(1)}, bf16[2,4,128,128]{3,2,1,0:T(8,128)(2,1)S(1)}, u32[]{:S(2)}, u32[]{:S(2)}) collective-permute-start(bf16[2,4,128,128]{3,2,1,0:T(8,128)(2,1)S(1)} %get-tuple-element.52), channel_id=1, source_target_pairs={{2,10},{6,14},{8,0},{10,18},{12,4},{14,22},{16,8},{18,26},{20,12},... | collective-permute-start | bytes 786440 | tf_op jit(solution)/shard_map/ppermute | solution.py:22
  82.3 18.7 %collective-permute-start.12 = (bf16[2,4,64,128]{3,2,1,0:T(8,128)(2,1)S(1)}, bf16[2,4,64,128]{3,2,1,0:T(8,128)(2,1)S(1)}, u32[]{:S(2)}, u32[]{:S(2)}) collective-permute-start(bf16[2,4,64,128]{3,2,1,0:T(8,128)(2,1)S(1)} %get-tuple-element.53), channel_id=1, source_target_pairs={{2,18},{6,22},{10,26},{14,30},{16,0},{18,34},{20,4},{22,38},{24,8}... | collective-permute-start | bytes 393224 | tf_op jit(solution)/shard_map/ppermute | solution.py:22
  85.8 27.7 %collective-permute-start.8 = (bf16[2,4,256,128]{3,2,1,0:T(8,128)(2,1)S(1)}, bf16[2,4,256,128]{3,2,1,0:T(8,128)(2,1)S(1)}, u32[]{:S(2)}, u32[]{:S(2)}) collective-permute-start(bf16[2,4,256,128]{3,2,1,0:T(8,128)(2,1)S(1)} %get-tuple-element.49), channel_id=1, source_target_pairs={{2,4},{4,2},{6,8},{8,6},{10,12},{12,10},{14,16},{16,14},{18,20},{2... | collective-permute-start | bytes 1572872 | tf_op jit(solution)/shard_map/ppermute | solution.py:30
  96.3 18.5 %collective-permute-start.10 = (bf16[2,4,256,128]{3,2,1,0:T(8,128)(2,1)S(1)}, bf16[2,4,256,128]{3,2,1,0:T(8,128)(2,1)S(1)}, u32[]{:S(2)}, u32[]{:S(2)}) collective-permute-start(bf16[2,4,256,128]{3,2,1,0:T(8,128)(2,1)S(1)} %get-tuple-element.51), channel_id=1, source_target_pairs={{2,6},{4,0},{6,10},{8,4},{10,14},{12,8},{14,18},{16,12},{18,22},{2... | collective-permute-start | bytes 1572872 | tf_op jit(solution)/shard_map/ppermute | solution.py:22
  101.1 30.2 %collective-permute-start.13 = (bf16[2,4,256,128]{3,2,1,0:T(8,128)(2,1)S(1)}, bf16[2,4,256,128]{3,2,1,0:T(8,128)(2,1)S(1)}, u32[]{:S(2)}, u32[]{:S(2)}) collective-permute-start(bf16[2,4,256,128]{3,2,1,0:T(8,128)(2,1)S(1)} %get-tuple-element.57), channel_id=1, source_target_pairs={{0,4},{4,8},{6,2},{8,12},{10,6},{12,16},{14,10},{16,20},{18,14},{2... | collective-permute-start | bytes 1572872 | tf_op jit(solution)/shard_map/ppermute | solution.py:22
  107.6 23.7 %collective-permute-start.14 = (bf16[2,4,128,128]{3,2,1,0:T(8,128)(2,1)S(1)}, bf16[2,4,128,128]{3,2,1,0:T(8,128)(2,1)S(1)}, u32[]{:S(2)}, u32[]{:S(2)}) collective-permute-start(bf16[2,4,128,128]{3,2,1,0:T(8,128)(2,1)S(1)} %get-tuple-element.58), channel_id=1, source_target_pairs={{0,8},{4,12},{8,16},{10,2},{12,20},{14,6},{16,24},{18,10},{20,28},... | collective-permute-start | bytes 786440 | tf_op jit(solution)/shard_map/ppermute | solution.py:22
  109.5 21.8 %collective-permute-start.15 = (bf16[2,4,64,128]{3,2,1,0:T(8,128)(2,1)S(1)}, bf16[2,4,64,128]{3,2,1,0:T(8,128)(2,1)S(1)}, u32[]{:S(2)}, u32[]{:S(2)}) collective-permute-start(bf16[2,4,64,128]{3,2,1,0:T(8,128)(2,1)S(1)} %get-tuple-element.59), channel_id=1, source_target_pairs={{0,16},{4,20},{8,24},{12,28},{16,32},{18,2},{20,36},{22,6},{24,40}... | collective-permute-start | bytes 393224 | tf_op jit(solution)/shard_map/ppermute | solution.py:22

commit v3 on v2

--- a/solution.py
+++ b/solution.py
@@ -10,6 +10,7 @@
 
 BLOCK = 256
 LEVELS = 3
+CHUNKS = 2
 LOG2E = math.log2(math.e)
 
 BF = jnp.bfloat16
@@ -111,29 +112,25 @@
 
 
 def later_kernel(count, *refs):
+    outs = refs[len(refs) - count * CHUNKS :]
     for at in range(count):
-        refs[len(refs) - count + at][...] = refs[at][...]
+        per = refs[at].shape[1] // CHUNKS
+        for chunk in range(CHUNKS):
+            outs[chunk * count + at][...] = refs[at][:, chunk * per : (chunk + 1) * per]
 
 
 def later(after, arrays):
-    return pl.pallas_call(
+    halves = [shape((2, x.shape[1] // CHUNKS, *x.shape[2:])) for x in arrays]
+    outs = pl.pallas_call(
         functools.partial(later_kernel, len(arrays)),
-        out_shape=[shape(x.shape) for x in arrays],
+        out_shape=halves * CHUNKS,
         in_specs=[VMEM_SPEC] * len(arrays) + [pl.BlockSpec(memory_space=pl.ANY)] * len(after),
         compiler_params=params(8),
         name="later",
         cost_estimate=pl.CostEstimate(flops=0, bytes_accessed=2 * 2**20, transcendentals=0),
     )(*arrays, *after)
-
-
-def exchange(firsts, seconds, outer, inner):
-    steps = [2 ** (level + 1) for level in range(LEVELS)]
-    down = [crossed(x, -step) for x, step in zip(firsts, steps)]
-    rims = swapped(outer, True), swapped(inner, False)
-    up = [
-        crossed(x, step) for x, step in zip(later((*down[1:], rims[1]), seconds), steps)
-    ]
-    return down, up, rims
+    count = len(arrays)
+    return [outs[chunk * count : (chunk + 1) * count] for chunk in range(CHUNKS)]
 
 
 def split_qd_kernel(heads, place_ref, q_ref, d_ref, q_out, d_out, rep_out, wide, sums, spread):
@@ -176,8 +173,11 @@
     )(place, q2, d2)
 
 
-def attend_kernel(count, place_ref, q_ref, d_ref, rep_ref, outer, inner, rim_out, rim_in, *rest):
+def attend_kernel(
+    count, skip, place_ref, q_ref, d_ref, rep_ref, outer, inner, rim_out, rim_in, *rest
+):
     crossed_a, crossed_b = rest[:LEVELS], rest[LEVELS : 2 * LEVELS]
+    rest = rest[: 2 * LEVELS] + rest[2 * LEVELS + skip :]
     att, gq, own, g_out, g_in = rest[2 * LEVELS : 2 * LEVELS + 5]
     rest = rest[2 * LEVELS + 5 :]
     g_as, g_bs = rest[:LEVELS], rest[LEVELS : 2 * LEVELS]
@@ -292,29 +292,33 @@
                 ref[which, 0, pl.ds(offset, size), :] = value
 
 
-def attend(place, count, q, d, rep, outer, inner, rim_out, rim_in, crossed_a, crossed_b):
+def attend(chunk, before, place, count, q, d, rep, outer, inner, rims, crossed_a, crossed_b):
     heads, block = inner.shape[1], inner.shape[2]
+    per = heads // CHUNKS
+    base = chunk * per
     span = 2 * block
     sizes = [span // 2 ** (level + 1) for level in range(LEVELS)]
     columns = 4 * block + 2 * sum(sizes)
     width = columns - block
 
-    def pair(size):
-        return pl.BlockSpec((2, 1, size, 128), lambda h: (0, h, 0, 0))
-
-    head_spec = pl.BlockSpec((1, span, 128), lambda h: (h, 0, 0))
-    flops = 2 * heads * span * width * 128 * 6
+    def pair(size, first=base):
+        return pl.BlockSpec((2, 1, size, 128), lambda h: (0, first + h, 0, 0))
+
+    head_spec = pl.BlockSpec((1, span, 128), lambda h: (base + h, 0, 0))
+    flops = 2 * per * span * width * 128 * 6
+    in_specs = [
+        SMEM_SPEC,
+        head_spec,
+        head_spec,
+        pl.BlockSpec((LEVELS, 1, span, 128), lambda h: (0, base + h, 0, 0)),
+    ]
+    in_specs += [pair(block)] * 4
+    in_specs += [pair(size, 0) for size in sizes] + [pair(size) for size in sizes]
+    aliases = {len(in_specs) + at: at for at in range(len(before))}
     return pl.pallas_call(
-        functools.partial(attend_kernel, count),
-        grid=(heads,),
-        in_specs=[
-            SMEM_SPEC,
-            head_spec,
-            head_spec,
-            pl.BlockSpec((LEVELS, 1, span, 128), lambda h: (0, h, 0, 0)),
-        ]
-        + [pair(block)] * 4
-        + [pair(size) for size in sizes] * 2,
+        functools.partial(attend_kernel, count, len(before)),
+        grid=(per,),
+        in_specs=in_specs + [pl.BlockSpec(memory_space=pl.ANY)] * len(before),
         out_specs=[head_spec, head_spec, pair(span), pair(block), pair(block)]
         + [pair(size) for size in sizes] * 2,
         out_shape=[
@@ -337,12 +341,38 @@
             pltpu.VMEM((2, LEVELS, block, 128), F32),
             pltpu.VMEM((2, block, 128), F32),
         ],
+        input_output_aliases=aliases,
         compiler_params=params(30),
         name="attend",
         cost_estimate=pl.CostEstimate(
-            flops=flops, bytes_accessed=8 * 2**20, transcendentals=heads * span * width
+            flops=flops, bytes_accessed=8 * 2**20, transcendentals=per * span * width
         ),
-    )(place, q, d, rep, outer, inner, rim_out, rim_in, *crossed_a, *crossed_b)
+    )(place, q, d, rep, outer, inner, *rims, *crossed_a, *crossed_b, *before)
+
+
+def merge_kernel(count, coarse, fine, *refs):
+    outs, wide = refs[len(refs) - count - 2 : -1], refs[-1]
+    rows = fine.shape[0]
+    half = coarse[...].astype(F32) * 0.5
+    wide[pl.ds(0, rows // 2, stride=2), :] = half
+    wide[pl.ds(1, rows // 2, stride=2), :] = half
+    outs[0][...] = (wide[...] + fine[...].astype(F32)).astype(BF)
+    for at in range(count):
+        outs[1 + at][...] = refs[at][...]
+
+
+def merge(coarse, fine, rest=(), after=()):
+    flat = [x.reshape(-1, 128) for x in (coarse, fine, *rest)]
+    outs = pl.pallas_call(
+        functools.partial(merge_kernel, len(rest)),
+        out_shape=[shape(x.shape) for x in flat[1:]],
+        in_specs=[VMEM_SPEC] * len(flat) + [pl.BlockSpec(memory_space=pl.ANY)] * len(after),
+        scratch_shapes=[pltpu.VMEM(flat[1].shape, F32)],
+        compiler_params=params(12),
+        name="merge",
+        cost_estimate=pl.CostEstimate(flops=0, bytes_accessed=2 * 2**20, transcendentals=0),
+    )(*flat, *after)
+    return [x.reshape(y.shape) for x, y in zip(outs, (fine, *rest))]
 
 
 def join_kernel(heads, place_ref, att, gq, att_out, gq_out, wide):
@@ -368,15 +398,14 @@
 
 
 def gather_kernel(heads, place_ref, own, outer, inner, *refs):
-    downs, ups, outs = refs[:LEVELS], refs[LEVELS : 2 * LEVELS], refs[2 * LEVELS : 2 * LEVELS + 2]
-    wide, mine, spread = refs[2 * LEVELS + 2 :]
+    downs, ups, outs, (wide, mine, spread) = refs[:2], refs[2:4], refs[4:6], refs[6:]
     span = own.shape[2]
     block = span // 2
     odd = lax.rem(place_ref[0], 2)
     for which, out in enumerate(outs):
         for head in range(heads):
             both = None
-            for level in reversed(range(LEVELS)):
+            for level in (1, 0):
                 value = downs[level][which, head].astype(F32) + ups[level][which, head].astype(F32)
                 value = value * (1.0 / 2 ** (level + 1))
                 if both is not None:
@@ -418,14 +447,26 @@
     flat = (heads * span, width)
     q2, k2, v2, d2 = (x.reshape(flat) for x in (query, key, value, dout))
     outer, inner, *coarse = split_kv(place, k2, v2, heads, span)
-    crossed_b, crossed_a, rims = exchange(coarse, coarse, outer, inner)
+    steps = [2 ** (level + 1) for level in range(LEVELS)]
+    crossed_b = [crossed(x, -step) for x, step in zip(coarse, steps)]
+    rims = swapped(outer, True), swapped(inner, False)
+    chunks = later((*crossed_b[1:], rims[1]), coarse)
     qh, dh, rep = split_qd(place, q2, d2, heads, span)
-    att, gq, own, g_out, g_in, *grads = attend(
-        place, count, qh, dh, rep, outer, inner, *rims, crossed_a, crossed_b
-    )
-    downs, ups, rims = exchange(grads[:LEVELS], grads[LEVELS:], g_out, g_in)
+    results = ()
+    for chunk in range(CHUNKS):
+        crossed_a = [crossed(x, step) for x, step in zip(chunks[chunk], steps)]
+        results = attend(
+            chunk, results, place, count, qh, dh, rep, outer, inner, rims, crossed_a, crossed_b
+        )
+    att, gq, own, g_out, g_in, *grads = results
+    g_as, g_bs = grads[:LEVELS], grads[LEVELS:]
+    far_a, one_a = crossed(g_as[2], -4), crossed(g_as[0], -2)
+    g_out, g_in = swapped(g_out, True), swapped(g_in, False)
+    mid_a, far_b, one_b = merge(far_a, g_as[1], (g_bs[2], g_bs[0]), (g_in,))
+    far_b, one_b, two_a = crossed(far_b, 4), crossed(one_b, 2), crossed(mid_a, -4)
+    two_b = crossed(merge(far_b, g_bs[1])[0], 4)
     attended, grad_query = join(place, att, gq)
-    grad_key, grad_value = gather(place, own, *rims, *downs, *ups)
+    grad_key, grad_value = gather(place, own, g_out, g_in, one_a, two_a, one_b, two_b)
     return tuple(
         x.reshape(span, heads, width) for x in (attended, grad_query, grad_key, grad_value)
     )

time: 134 us -> 148 us (1.10)
  the two profiles are of different devices: /device:TPU:25 before, /device:TPU:42 now
where the time goes in v3:
time: 148 us
  starting transfers between devices  83.9 us (57%)
  waiting for transfers between devices  37.4 us (25%)
  Pallas kernels  23.4 us (16%)
  local copies, waits for them, and re-layouts  2.08 us (1%)
    ppermute x15, starting transfers between devices, crossed(): lax.ppermute(value, 'seq', [(at, to) for at, to in pairs if 0 <= to < cou...  74.5 us
    ppermute x15, waiting for transfers between devices, crossed(): lax.ppermute(value, 'seq', [(at, to) for at, to in pairs if 0 <= to < cou...  37.4 us
    pallas_call x2, Pallas kernels, attend(): pl.pallas_call(functools.partial(attend_kernel, count, len(before)), grid...  18.2 us
    ppermute x4, starting transfers between devices, swapped(): lax.ppermute(value, 'seq', [(at, to) for at, to in pairs if 0 <= to < cou...  9.41 us
  transfers between devices with their start and end apart: 19, of which 4 were waited for; matrix products, arithmetic and copies ran while one was open for 0% of the time, Pallas kernels for 8%

profile of v3, /device:TPU:42, one launch (start us, length us, event | category | flops | bytes accessed | tf_op | source)
XLA Modules:
  0.0 147.7 jit_solution(13630676928394024185)
XLA Ops:
  0.6 1.0 copy-done
  1.7 1.0 copy-done.1
  2.7 0.9 split_kv.1
  3.6 1.9 %collective-permute-start.1 = (bf16[2,4,256,128]{3,2,1,0:T(8,128)(2,1)S(1)}, bf16[2,4,256,128]{3,2,1,0:T(8,128)(2,1)S(1)}, u32[]{:S(2)}, u32[]{:S(2)}) collective-permute-start(bf16[2,4,256,128]{3,2,1,0:T(8,128)(2,1)S(1)} %get-tuple-element.51.inner), channel_id=1, source_target_pairs={{0,2},{2,0},{4,6},{6,4},{8,10},{10,8},{12,14},{14,12},{16,18},{18,... | collective-permute-start | bytes 1572872 | tf_op jit(solution)/shard_map/ppermute | solution.py:31
  5.5 2.0 %collective-permute-start.7 = (bf16[2,4,256,128]{3,2,1,0:T(8,128)(2,1)S(1)}, bf16[2,4,256,128]{3,2,1,0:T(8,128)(2,1)S(1)}, u32[]{:S(2)}, u32[]{:S(2)}) collective-permute-start(bf16[2,4,256,128]{3,2,1,0:T(8,128)(2,1)S(1)} %get-tuple-element.52.refs_0_), channel_id=1, source_target_pairs={{2,6},{4,0},{6,10},{8,4},{10,14},{12,8},{14,18},{16,12},{18,22},{2... | collective-permute-start | bytes 1572872 | tf_op jit(solution)/shard_map/ppermute | solution.py:23
  7.5 3.6 %collective-permute-start = (bf16[2,4,256,128]{3,2,1,0:T(8,128)(2,1)S(1)}, bf16[2,4,256,128]{3,2,1,0:T(8,128)(2,1)S(1)}, u32[]{:S(2)}, u32[]{:S(2)}) collective-permute-start(bf16[2,4,256,128]{3,2,1,0:T(8,128)(2,1)S(1)} %get-tuple-element.50.outer), channel_id=1, source_target_pairs={{2,4},{4,2},{6,8},{8,6},{10,12},{12,10},{14,16},{16,14},{18,20},{2... | collective-permute-start | bytes 1572872 | tf_op jit(solution)/shard_map/ppermute | solution.py:31
  11.2 12.4 %collective-permute-start.2 = (bf16[2,4,128,128]{3,2,1,0:T(8,128)(2,1)S(1)}, bf16[2,4,128,128]{3,2,1,0:T(8,128)(2,1)S(1)}, u32[]{:S(2)}, u32[]{:S(2)}) collective-permute-start(bf16[2,4,128,128]{3,2,1,0:T(8,128)(2,1)S(1)} %get-tuple-element.53.refs_1_), channel_id=1, source_target_pairs={{2,10},{6,14},{8,0},{10,18},{12,4},{14,22},{16,8},{18,26},{20,12},... | collective-permute-start | bytes 786440 | tf_op jit(solution)/shard_map/ppermute | solution.py:23
  23.6 5.5 %collective-permute-start.3 = (bf16[2,4,64,128]{3,2,1,0:T(8,128)(2,1)S(1)}, bf16[2,4,64,128]{3,2,1,0:T(8,128)(2,1)S(1)}, u32[]{:S(2)}, u32[]{:S(2)}) collective-permute-start(bf16[2,4,64,128]{3,2,1,0:T(8,128)(2,1)S(1)} %get-tuple-element.54.refs_2_), channel_id=1, source_target_pairs={{2,18},{6,22},{10,26},{14,30},{16,0},{18,34},{20,4},{22,38},{24,8}... | collective-permute-start | bytes 393224 | tf_op jit(solution)/shard_map/ppermute | solution.py:23
  29.1 9.5 %collective-permute-done.3.refs_4_.rest_5_ = bf16[2,4,64,128]{3,2,1,0:T(8,128)(2,1)S(1)} collective-permute-done((bf16[2,4,64,128]{3,2,1,0:T(8,128)(2,1)S(1)}, bf16[2,4,64,128]{3,2,1,0:T(8,128)(2,1)S(1)}, u32[]{:S(2)}, u32[]{:S(2)}) %collective-permute-start.3) | collective-permute-done | bytes 131104 | tf_op jit(solution)/shard_map/ppermute | solution.py:23
  38.6 1.9 %collective-permute-start.8 = (bf16[2,2,256,128]{3,2,1,0:T(8,128)(2,1)S(1)}, bf16[2,2,256,128]{3,2,1,0:T(8,128)(2,1)S(1)}, u32[]{:S(2)}, u32[]{:S(2)}) collective-permute-start(bf16[2,2,256,128]{3,2,1,0:T(8,128)(2,1)S(1)} %get-tuple-element.58), channel_id=1, source_target_pairs={{0,4},{4,8},{6,2},{8,12},{10,6},{12,16},{14,10},{16,20},{18,14},{2... | collective-permute-start | bytes 786440 | tf_op jit(solution)/shard_map/ppermute | solution.py:23
  40.5 6.8 %collective-permute-start.9 = (bf16[2,2,128,128]{3,2,1,0:T(8,128)(2,1)S(1)}, bf16[2,2,128,128]{3,2,1,0:T(8,128)(2,1)S(1)}, u32[]{:S(2)}, u32[]{:S(2)}) collective-permute-start(bf16[2,2,128,128]{3,2,1,0:T(8,128)(2,1)S(1)} %get-tuple-element.59), channel_id=1, source_target_pairs={{0,8},{4,12},{8,16},{10,2},{12,20},{14,6},{16,24},{18,10},{20,28},... | collective-permute-start | bytes 393224 | tf_op jit(solution)/shard_map/ppermute | solution.py:23
  47.4 8.0 %collective-permute-start.10 = (bf16[2,2,64,128]{3,2,1,0:T(8,128)(2,1)S(1)}, bf16[2,2,64,128]{3,2,1,0:T(8,128)(2,1)S(1)}, u32[]{:S(2)}, u32[]{:S(2)}) collective-permute-start(bf16[2,2,64,128]{3,2,1,0:T(8,128)(2,1)S(1)} %get-tuple-element.60), channel_id=1, source_target_pairs={{0,16},{4,20},{8,24},{12,28},{16,32},{18,2},{20,36},{22,6},{24,40}... | collective-permute-start | bytes 196616 | tf_op jit(solution)/shard_map/ppermute | solution.py:23
  55.4 1.9 %collective-permute-start.4 = (bf16[2,2,256,128]{3,2,1,0:T(8,128)(2,1)S(1)}, bf16[2,2,256,128]{3,2,1,0:T(8,128)(2,1)S(1)}, u32[]{:S(2)}, u32[]{:S(2)}) collective-permute-start(bf16[2,2,256,128]{3,2,1,0:T(8,128)(2,1)S(1)} %get-tuple-element.55), channel_id=1, source_target_pairs={{0,4},{4,8},{6,2},{8,12},{10,6},{12,16},{14,10},{16,20},{18,14},{2... | collective-permute-start | bytes 786440 | tf_op jit(solution)/shard_map/ppermute | solution.py:23
  57.4 0.9 split_qd.1
  58.3 6.7 %collective-permute-start.6 = (bf16[2,2,64,128]{3,2,1,0:T(8,128)(2,1)S(1)}, bf16[2,2,64,128]{3,2,1,0:T(8,128)(2,1)S(1)}, u32[]{:S(2)}, u32[]{:S(2)}) collective-permute-start(bf16[2,2,64,128]{3,2,1,0:T(8,128)(2,1)S(1)} %get-tuple-element.57), channel_id=1, source_target_pairs={{0,16},{4,20},{8,24},{12,28},{16,32},{18,2},{20,36},{22,6},{24,40}... | collective-permute-start | bytes 196616 | tf_op jit(solution)/shard_map/ppermute | solution.py:23
  65.1 1.9 %collective-permute-start.5 = (bf16[2,2,128,128]{3,2,1,0:T(8,128)(2,1)S(1)}, bf16[2,2,128,128]{3,2,1,0:T(8,128)(2,1)S(1)}, u32[]{:S(2)}, u32[]{:S(2)}) collective-permute-start(bf16[2,2,128,128]{3,2,1,0:T(8,128)(2,1)S(1)} %get-tuple-element.56), channel_id=1, source_target_pairs={{0,8},{4,12},{8,16},{10,2},{12,20},{14,6},{16,24},{18,10},{20,28},... | collective-permute-start | bytes 393224 | tf_op jit(solution)/shard_map/ppermute | solution.py:23
  67.0 8.9 %attend.2 = (bf16[4,512,128]{2,1,0:T(8,128)(2,1)S(1)}, bf16[4,512,128]{2,1,0:T(8,128)(2,1)S(1)}, f32[2,4,512,128]{3,2,1,0:T(8,128)S(1)}, bf16[2,4,256,128]{3,2,1...) custom-call(s32[1]{0:T(128)} %bitcast.place_ref, ...), custom_call_target="tpu_custom_call" | custom-call | flops 2617245696 | bytes 8388608 | tf_op jit(solution)/shard_map/attend/pallas_call | solution.py:318
  75.9 1.4 collective-permute-done.5.rest_1_
  77.3 9.3 %attend.3 = (bf16[4,512,128]{2,1,0:T(8,128)(2,1)S(1)}, bf16[4,512,128]{2,1,0:T(8,128)(2,1)S(1)}, f32[2,4,512,128]{3,2,1,0:T(8,128)S(1)}, bf16[2,4,256,128]{3,2,1...) custom-call(s32[1]{0:T(128)} %bitcast.place_ref, ...), custom_call_target="tpu_custom_call", output_to_operand_aliasing={{0}: (14, {}), {1}: (15, {}), {2}: (16, {}), {3}: (17, {}),... | custom-call | flops 2617245696 | bytes 8388608 | tf_op jit(solution)/shard_map/attend/pallas_call | solution.py:318
  86.6 1.9 %collective-permute-start.12 = (bf16[2,4,256,128]{3,2,1,0:T(8,128)(2,1)S(1)}, bf16[2,4,256,128]{3,2,1,0:T(8,128)(2,1)S(1)}, u32[]{:S(2)}, u32[]{:S(2)}) collective-permute-start(bf16[2,4,256,128]{3,2,1,0:T(8,128)(2,1)S(1)} %get-tuple-element.78), channel_id=1, source_target_pairs={{0,2},{2,0},{4,6},{6,4},{8,10},{10,8},{12,14},{14,12},{16,18},{18,... | collective-permute-start | bytes 1572872 | tf_op jit(solution)/shard_map/ppermute | solution.py:31
  88.5 8.0 %collective-permute-start.14 = (bf16[2,4,64,128]{3,2,1,0:T(8,128)(2,1)S(1)}, bf16[2,4,64,128]{3,2,1,0:T(8,128)(2,1)S(1)}, u32[]{:S(2)}, u32[]{:S(2)}) collective-permute-start(bf16[2,4,64,128]{3,2,1,0:T(8,128)(2,1)S(1)} %get-tuple-element.80), channel_id=1, source_target_pairs={{2,10},{6,14},{8,0},{10,18},{12,4},{14,22},{16,8},{18,26},{20,12},... | collective-permute-start | bytes 393224 | tf_op jit(solution)/shard_map/ppermute | solution.py:23
  96.5 1.9 %collective-permute-start.11 = (bf16[2,4,256,128]{3,2,1,0:T(8,128)(2,1)S(1)}, bf16[2,4,256,128]{3,2,1,0:T(8,128)(2,1)S(1)}, u32[]{:S(2)}, u32[]{:S(2)}) collective-permute-start(bf16[2,4,256,128]{3,2,1,0:T(8,128)(2,1)S(1)} %get-tuple-element.77), channel_id=1, source_target_pairs={{2,4},{4,2},{6,8},{8,6},{10,12},{12,10},{14,16},{16,14},{18,20},{2... | collective-permute-start | bytes 1572872 | tf_op jit(solution)/shard_map/ppermute | solution.py:31
  98.5 3.9 %collective-permute-start.13 = (bf16[2,4,256,128]{3,2,1,0:T(8,128)(2,1)S(1)}, bf16[2,4,256,128]{3,2,1,0:T(8,128)(2,1)S(1)}, u32[]{:S(2)}, u32[]{:S(2)}) collective-permute-start(bf16[2,4,256,128]{3,2,1,0:T(8,128)(2,1)S(1)} %get-tuple-element.79), channel_id=1, source_target_pairs={{2,6},{4,0},{6,10},{8,4},{10,14},{12,8},{14,18},{16,12},{18,22},{2... | collective-permute-start | bytes 1572872 | tf_op jit(solution)/shard_map/ppermute | solution.py:23
  102.4 0.1 merge.2
  102.6 1.9 %collective-permute-start.16 = (bf16[2,4,256,128]{3,2,1,0:T(8,128)(2,1)S(1)}, bf16[2,4,256,128]{3,2,1,0:T(8,128)(2,1)S(1)}, u32[]{:S(2)}, u32[]{:S(2)}) collective-permute-start(bf16[2,4,256,128]{3,2,1,0:T(8,128)(2,1)S(1)} %bitcast.30), channel_id=1, source_target_pairs={{0,4},{4,8},{6,2},{8,12},{10,6},{12,16},{14,10},{16,20},{18,14},{2... | collective-permute-start | bytes 1572872 | tf_op jit(solution)/shard_map/ppermute | solution.py:23
  104.5 1.9 %collective-permute-start.17 = (bf16[2,4,64,128]{3,2,1,0:T(8,128)(2,1)S(1)}, bf16[2,4,64,128]{3,2,1,0:T(8,128)(2,1)S(1)}, u32[]{:S(2)}, u32[]{:S(2)}) collective-permute-start(bf16[2,4,64,128]{3,2,1,0:T(8,128)(2,1)S(1)} %bitcast.32), channel_id=1, source_target_pairs={{0,8},{4,12},{8,16},{10,2},{12,20},{14,6},{16,24},{18,10},{20,28},... | collective-permute-start | bytes 393224 | tf_op jit(solution)/shard_map/ppermute | solution.py:23
  106.4 9.6 %collective-permute-start.15 = (bf16[2,4,128,128]{3,2,1,0:T(8,128)(2,1)S(1)}, bf16[2,4,128,128]{3,2,1,0:T(8,128)(2,1)S(1)}, u32[]{:S(2)}, u32[]{:S(2)}) collective-permute-start(bf16[2,4,128,128]{3,2,1,0:T(8,128)(2,1)S(1)} %bitcast.31), channel_id=1, source_target_pairs={{2,10},{6,14},{8,0},{10,18},{12,4},{14,22},{16,8},{18,26},{20,12},... | collective-permute-start | bytes 786440 | tf_op jit(solution)/shard_map/ppermute | solution.py:23
  116.0 16.0 %collective-permute-done.17 = bf16[2,4,64,128]{3,2,1,0:T(8,128)(2,1)S(1)} collective-permute-done((bf16[2,4,64,128]{3,2,1,0:T(8,128)(2,1)S(1)}, bf16[2,4,64,128]{3,2,1,0:T(8,128)(2,1)S(1)}, u32[]{:S(2)}, u32[]{:S(2)}) %collective-permute-start.17) | collective-permute-done | bytes 131104 | tf_op jit(solution)/shard_map/ppermute | solution.py:23
  132.1 1.9 %collective-permute-start.18 = (bf16[2,4,128,128]{3,2,1,0:T(8,128)(2,1)S(1)}, bf16[2,4,128,128]{3,2,1,0:T(8,128)(2,1)S(1)}, u32[]{:S(2)}, u32[]{:S(2)}) collective-permute-start(bf16[2,4,128,128]{3,2,1,0:T(8,128)(2,1)S(1)} %bitcast.27), channel_id=1, source_target_pairs={{0,8},{4,12},{8,16},{10,2},{12,20},{14,6},{16,24},{18,10},{20,28},... | collective-permute-start | bytes 786440 | tf_op jit(solution)/shard_map/ppermute | solution.py:23
  134.1 1.2 join.1
  135.3 10.5 %collective-permute-done.18.refs_3_ = bf16[2,4,128,128]{3,2,1,0:T(8,128)(2,1)S(1)} collective-permute-done((bf16[2,4,128,128]{3,2,1,0:T(8,128)(2,1)S(1)}, bf16[2,4,128,128]{3,2,1,0:T(8,128)(2,1)S(1)}, u32[]{:S(2)}, u32[]{:S(2)}) %collective-permute-start.18) | collective-permute-done | bytes 262176 | tf_op jit(solution)/shard_map/ppermute | solution.py:23
  145.8 1.9 %gather.1 = (bf16[2048,128]{1,0:T(8,128)(2,1)}, bf16[2048,128]{1,0:T(8,128)(2,1)}) custom-call(s32[1]{0:T(128)} %bitcast.place_ref, f32[2,4,512,128]{3,2,1,0:T(8,128)S(1)} %get-tuple-element.76.own, bf16[2,4,256,128]{3,2,1,0:T(8,128)(2,1)S(1)} %collective-permute-done.11.outer, bf16[2,4,256,128]{3,2,1,0:T(8,128)(2,1)S(1)} %collective-permute-done.12.refs_2_.inner, ...), custom_call_target="tpu_custom_call" | custom-call | bytes 8388608 | tf_op jit(solution)/shard_map/gather/pallas_call | solution.py:428
  (23 shorter events, 0.2 us)
Async XLA Ops:
  0.6 1.0 copy-start
  1.7 1.0 copy-start.1
  2.7 54.6 %copy-start.2 = (bf16[512,4,128]{2,1,0:T(4,128)(2,1)S(1)}, bf16[512,4,128]{2,1,0:T(4,128)(2,1)}, u32[]{:S(2)}) copy-start(bf16[512,4,128]{2,1,0:T(4,128)(2,1)} %param.4) | copy-start | bytes 1572868
  2.7 54.7 %copy-start.3 = (bf16[512,4,128]{2,1,0:T(4,128)(2,1)S(1)}, bf16[512,4,128]{2,1,0:T(4,128)(2,1)}, u32[]{:S(2)}) copy-start(bf16[512,4,128]{2,1,0:T(4,128)(2,1)} %param.7) | copy-start | bytes 1572868
  3.6 34.9 %collective-permute-start.1 = (bf16[2,4,256,128]{3,2,1,0:T(8,128)(2,1)S(1)}, bf16[2,4,256,128]{3,2,1,0:T(8,128)(2,1)S(1)}, u32[]{:S(2)}, u32[]{:S(2)}) collective-permute-start(bf16[2,4,256,128]{3,2,1,0:T(8,128)(2,1)S(1)} %get-tuple-element.51.inner), channel_id=1, source_target_pairs={{0,2},{2,0},{4,6},{6,4},{8,10},{10,8},{12,14},{14,12},{16,18},{18,... | collective-permute-start | bytes 1572872 | tf_op jit(solution)/shard_map/ppermute | solution.py:31
  5.5 49.9 %collective-permute-start.7 = (bf16[2,4,256,128]{3,2,1,0:T(8,128)(2,1)S(1)}, bf16[2,4,256,128]{3,2,1,0:T(8,128)(2,1)S(1)}, u32[]{:S(2)}, u32[]{:S(2)}) collective-permute-start(bf16[2,4,256,128]{3,2,1,0:T(8,128)(2,1)S(1)} %get-tuple-element.52.refs_0_), channel_id=1, source_target_pairs={{2,6},{4,0},{6,10},{8,4},{10,14},{12,8},{14,18},{16,12},{18,22},{2... | collective-permute-start | bytes 1572872 | tf_op jit(solution)/shard_map/ppermute | solution.py:23
  7.5 50.8 %collective-permute-start = (bf16[2,4,256,128]{3,2,1,0:T(8,128)(2,1)S(1)}, bf16[2,4,256,128]{3,2,1,0:T(8,128)(2,1)S(1)}, u32[]{:S(2)}, u32[]{:S(2)}) collective-permute-start(bf16[2,4,256,128]{3,2,1,0:T(8,128)(2,1)S(1)} %get-tuple-element.50.outer), channel_id=1, source_target_pairs={{2,4},{4,2},{6,8},{8,6},{10,12},{12,10},{14,16},{16,14},{18,20},{2... | collective-permute-start | bytes 1572872 | tf_op jit(solution)/shard_map/ppermute | solution.py:31
  11.2 27.3 %collective-permute-start.2 = (bf16[2,4,128,128]{3,2,1,0:T(8,128)(2,1)S(1)}, bf16[2,4,128,128]{3,2,1,0:T(8,128)(2,1)S(1)}, u32[]{:S(2)}, u32[]{:S(2)}) collective-permute-start(bf16[2,4,128,128]{3,2,1,0:T(8,128)(2,1)S(1)} %get-tuple-element.53.refs_1_), channel_id=1, source_target_pairs={{2,10},{6,14},{8,0},{10,18},{12,4},{14,22},{16,8},{18,26},{20,12},... | collective-permute-start | bytes 786440 | tf_op jit(solution)/shard_map/ppermute | solution.py:23
  23.6 14.9 %collective-permute-start.3 = (bf16[2,4,64,128]{3,2,1,0:T(8,128)(2,1)S(1)}, bf16[2,4,64,128]{3,2,1,0:T(8,128)(2,1)S(1)}, u32[]{:S(2)}, u32[]{:S(2)}) collective-permute-start(bf16[2,4,64,128]{3,2,1,0:T(8,128)(2,1)S(1)} %get-tuple-element.54.refs_2_), channel_id=1, source_target_pairs={{2,18},{6,22},{10,26},{14,30},{16,0},{18,34},{20,4},{22,38},{24,8}... | collective-permute-start | bytes 393224 | tf_op jit(solution)/shard_map/ppermute | solution.py:23
  38.6 28.4 %collective-permute-start.8 = (bf16[2,2,256,128]{3,2,1,0:T(8,128)(2,1)S(1)}, bf16[2,2,256,128]{3,2,1,0:T(8,128)(2,1)S(1)}, u32[]{:S(2)}, u32[]{:S(2)}) collective-permute-start(bf16[2,2,256,128]{3,2,1,0:T(8,128)(2,1)S(1)} %get-tuple-element.58), channel_id=1, source_target_pairs={{0,4},{4,8},{6,2},{8,12},{10,6},{12,16},{14,10},{16,20},{18,14},{2... | collective-permute-start | bytes 786440 | tf_op jit(solution)/shard_map/ppermute | solution.py:23
  40.5 26.5 %collective-permute-start.9 = (bf16[2,2,128,128]{3,2,1,0:T(8,128)(2,1)S(1)}, bf16[2,2,128,128]{3,2,1,0:T(8,128)(2,1)S(1)}, u32[]{:S(2)}, u32[]{:S(2)}) collective-permute-start(bf16[2,2,128,128]{3,2,1,0:T(8,128)(2,1)S(1)} %get-tuple-element.59), channel_id=1, source_target_pairs={{0,8},{4,12},{8,16},{10,2},{12,20},{14,6},{16,24},{18,10},{20,28},... | collective-permute-start | bytes 393224 | tf_op jit(solution)/shard_map/ppermute | solution.py:23
  47.4 17.7 %collective-permute-start.10 = (bf16[2,2,64,128]{3,2,1,0:T(8,128)(2,1)S(1)}, bf16[2,2,64,128]{3,2,1,0:T(8,128)(2,1)S(1)}, u32[]{:S(2)}, u32[]{:S(2)}) collective-permute-start(bf16[2,2,64,128]{3,2,1,0:T(8,128)(2,1)S(1)} %get-tuple-element.60), channel_id=1, source_target_pairs={{0,16},{4,20},{8,24},{12,28},{16,32},{18,2},{20,36},{22,6},{24,40}... | collective-permute-start | bytes 196616 | tf_op jit(solution)/shard_map/ppermute | solution.py:23
  55.4 21.9 %collective-permute-start.4 = (bf16[2,2,256,128]{3,2,1,0:T(8,128)(2,1)S(1)}, bf16[2,2,256,128]{3,2,1,0:T(8,128)(2,1)S(1)}, u32[]{:S(2)}, u32[]{:S(2)}) collective-permute-start(bf16[2,2,256,128]{3,2,1,0:T(8,128)(2,1)S(1)} %get-tuple-element.55), channel_id=1, source_target_pairs={{0,4},{4,8},{6,2},{8,12},{10,6},{12,16},{14,10},{16,20},{18,14},{2... | collective-permute-start | bytes 786440 | tf_op jit(solution)/shard_map/ppermute | solution.py:23
  58.3 17.6 %collective-permute-start.6 = (bf16[2,2,64,128]{3,2,1,0:T(8,128)(2,1)S(1)}, bf16[2,2,64,128]{3,2,1,0:T(8,128)(2,1)S(1)}, u32[]{:S(2)}, u32[]{:S(2)}) collective-permute-start(bf16[2,2,64,128]{3,2,1,0:T(8,128)(2,1)S(1)} %get-tuple-element.57), channel_id=1, source_target_pairs={{0,16},{4,20},{8,24},{12,28},{16,32},{18,2},{20,36},{22,6},{24,40}... | collective-permute-start | bytes 196616 | tf_op jit(solution)/shard_map/ppermute | solution.py:23
  65.1 12.3 %collective-permute-start.5 = (bf16[2,2,128,128]{3,2,1,0:T(8,128)(2,1)S(1)}, bf16[2,2,128,128]{3,2,1,0:T(8,128)(2,1)S(1)}, u32[]{:S(2)}, u32[]{:S(2)}) collective-permute-start(bf16[2,2,128,128]{3,2,1,0:T(8,128)(2,1)S(1)} %get-tuple-element.56), channel_id=1, source_target_pairs={{0,8},{4,12},{8,16},{10,2},{12,20},{14,6},{16,24},{18,10},{20,28},... | collective-permute-start | bytes 393224 | tf_op jit(solution)/shard_map/ppermute | solution.py:23
  86.6 15.8 %collective-permute-start.12 = (bf16[2,4,256,128]{3,2,1,0:T(8,128)(2,1)S(1)}, bf16[2,4,256,128]{3,2,1,0:T(8,128)(2,1)S(1)}, u32[]{:S(2)}, u32[]{:S(2)}) collective-permute-start(bf16[2,4,256,128]{3,2,1,0:T(8,128)(2,1)S(1)} %get-tuple-element.78), channel_id=1, source_target_pairs={{0,2},{2,0},{4,6},{6,4},{8,10},{10,8},{12,14},{14,12},{16,18},{18,... | collective-permute-start | bytes 1572872 | tf_op jit(solution)/shard_map/ppermute | solution.py:31
  88.5 13.8 %collective-permute-start.14 = (bf16[2,4,64,128]{3,2,1,0:T(8,128)(2,1)S(1)}, bf16[2,4,64,128]{3,2,1,0:T(8,128)(2,1)S(1)}, u32[]{:S(2)}, u32[]{:S(2)}) collective-permute-start(bf16[2,4,64,128]{3,2,1,0:T(8,128)(2,1)S(1)} %get-tuple-element.80), channel_id=1, source_target_pairs={{2,10},{6,14},{8,0},{10,18},{12,4},{14,22},{16,8},{18,26},{20,12},... | collective-permute-start | bytes 393224 | tf_op jit(solution)/shard_map/ppermute | solution.py:23
  96.5 38.7 %collective-permute-start.11 = (bf16[2,4,256,128]{3,2,1,0:T(8,128)(2,1)S(1)}, bf16[2,4,256,128]{3,2,1,0:T(8,128)(2,1)S(1)}, u32[]{:S(2)}, u32[]{:S(2)}) collective-permute-start(bf16[2,4,256,128]{3,2,1,0:T(8,128)(2,1)S(1)} %get-tuple-element.77), channel_id=1, source_target_pairs={{2,4},{4,2},{6,8},{8,6},{10,12},{12,10},{14,16},{16,14},{18,20},{2... | collective-permute-start | bytes 1572872 | tf_op jit(solution)/shard_map/ppermute | solution.py:31
  98.5 36.8 %collective-permute-start.13 = (bf16[2,4,256,128]{3,2,1,0:T(8,128)(2,1)S(1)}, bf16[2,4,256,128]{3,2,1,0:T(8,128)(2,1)S(1)}, u32[]{:S(2)}, u32[]{:S(2)}) collective-permute-start(bf16[2,4,256,128]{3,2,1,0:T(8,128)(2,1)S(1)} %get-tuple-element.79), channel_id=1, source_target_pairs={{2,6},{4,0},{6,10},{8,4},{10,14},{12,8},{14,18},{16,12},{18,22},{2... | collective-permute-start | bytes 1572872 | tf_op jit(solution)/shard_map/ppermute | solution.py:23
  102.6 43.3 %collective-permute-start.16 = (bf16[2,4,256,128]{3,2,1,0:T(8,128)(2,1)S(1)}, bf16[2,4,256,128]{3,2,1,0:T(8,128)(2,1)S(1)}, u32[]{:S(2)}, u32[]{:S(2)}) collective-permute-start(bf16[2,4,256,128]{3,2,1,0:T(8,128)(2,1)S(1)} %bitcast.30), channel_id=1, source_target_pairs={{0,4},{4,8},{6,2},{8,12},{10,6},{12,16},{14,10},{16,20},{18,14},{2... | collective-permute-start | bytes 1572872 | tf_op jit(solution)/shard_map/ppermute | solution.py:23
  104.5 27.5 %collective-permute-start.17 = (bf16[2,4,64,128]{3,2,1,0:T(8,128)(2,1)S(1)}, bf16[2,4,64,128]{3,2,1,0:T(8,128)(2,1)S(1)}, u32[]{:S(2)}, u32[]{:S(2)}) collective-permute-start(bf16[2,4,64,128]{3,2,1,0:T(8,128)(2,1)S(1)} %bitcast.32), channel_id=1, source_target_pairs={{0,8},{4,12},{8,16},{10,2},{12,20},{14,6},{16,24},{18,10},{20,28},... | collective-permute-start | bytes 393224 | tf_op jit(solution)/shard_map/ppermute | solution.py:23
  106.4 28.9 %collective-permute-start.15 = (bf16[2,4,128,128]{3,2,1,0:T(8,128)(2,1)S(1)}, bf16[2,4,128,128]{3,2,1,0:T(8,128)(2,1)S(1)}, u32[]{:S(2)}, u32[]{:S(2)}) collective-permute-start(bf16[2,4,128,128]{3,2,1,0:T(8,128)(2,1)S(1)} %bitcast.31), channel_id=1, source_target_pairs={{2,10},{6,14},{8,0},{10,18},{12,4},{14,22},{16,8},{18,26},{20,12},... | collective-permute-start | bytes 786440 | tf_op jit(solution)/shard_map/ppermute | solution.py:23
  132.1 13.7 %collective-permute-start.18 = (bf16[2,4,128,128]{3,2,1,0:T(8,128)(2,1)S(1)}, bf16[2,4,128,128]{3,2,1,0:T(8,128)(2,1)S(1)}, u32[]{:S(2)}, u32[]{:S(2)}) collective-permute-start(bf16[2,4,128,128]{3,2,1,0:T(8,128)(2,1)S(1)} %bitcast.27), channel_id=1, source_target_pairs={{0,8},{4,12},{8,16},{10,2},{12,20},{14,6},{16,24},{18,10},{20,28},... | collective-permute-start | bytes 786440 | tf_op jit(solution)/shard_map/ppermute | solution.py:23

commit v4 on v2

--- a/solution.py
+++ b/solution.py
@@ -178,10 +178,10 @@
 
 def attend_kernel(count, place_ref, q_ref, d_ref, rep_ref, outer, inner, rim_out, rim_in, *rest):
     crossed_a, crossed_b = rest[:LEVELS], rest[LEVELS : 2 * LEVELS]
-    att, gq, own, g_out, g_in = rest[2 * LEVELS : 2 * LEVELS + 5]
-    rest = rest[2 * LEVELS + 5 :]
+    g_out, g_in = rest[2 * LEVELS : 2 * LEVELS + 2]
+    rest = rest[2 * LEVELS + 2 :]
     g_as, g_bs = rest[:LEVELS], rest[LEVELS : 2 * LEVELS]
-    keys, vals, keys_t, vals_t, scores, grads, probs, dscores, rows, total_q = rest[2 * LEVELS :]
+    probs, dscores, keys_t, vals_t, keys, vals, scores, grads = rest[2 * LEVELS :]
     place = place_ref[0]
     even = lax.rem(place, 2) == 0
     block = outer.shape[2]
@@ -208,58 +208,94 @@
             bias = jnp.where(ok, bias, -jnp.inf).astype(F32)
         segments.append((at, size, bias, level))
         at += size
-    columns = at
-    keys_t[...] = keys[...].T
-    vals_t[...] = vals[...].T
+    keys_t[0] = keys[...].T
+    vals_t[0] = vals[...].T
 
     turns = (0, 1)
     cols = [pl.ds(turn * block, block) for turn in turns]
     met = [segments[:-1], segments[1:]]
+    d_blks = [d_ref[0, cols[turn], :] for turn in turns]
+    using = [[q_ref[0, cols[turn], :]] for turn in turns]
+    for turn in turns:
+        using[turn] += [rep_ref[level, 0, cols[turn], :] for level in range(LEVELS)]
     top = [None, None]
+    total = [jnp.zeros((1, block), F32)] * 2
+    acc = [jnp.zeros((1, block), F32)] * 2
+
+    def products(turn, start, size, bias, level):
+        here = pl.ds(start, size)
+        s = nt(keys[here, :], using[turn][level])
+        scores[turn, here, :] = s
+        high = jnp.max(s, axis=0, keepdims=True) * scale2 + bias
+        top[turn] = high if top[turn] is None else jnp.maximum(top[turn], high)
+        grads[turn, here, :] = nt(vals[here, :], d_blks[turn])
+
+    def weights(turn, start, size, bias, level):
+        here = pl.ds(start, size)
+        e = jnp.exp2(scores[turn, here, :] * scale2 - (top[turn] - bias))
+        scores[turn, here, :] = e
+        total[turn] = total[turn] + jnp.sum(e, axis=0, keepdims=True)
+        acc[turn] = acc[turn] + jnp.sum(e * grads[turn, here, :], axis=0, keepdims=True)
+
+    for part in met[0]:
+        products(0, *part)
+    for part, other in zip(met[0], met[1]):
+        products(1, *other)
+        weights(0, *part)
+    for part in met[1]:
+        weights(1, *part)
     for turn in turns:
-        d_blk = d_ref[0, cols[turn], :]
-        using = [q_ref[0, cols[turn], :]]
-        using += [rep_ref[level, 0, cols[turn], :] for level in range(LEVELS)]
+        inverse = 1.0 / total[turn]
+        delta = acc[turn] * inverse
         for start, size, bias, level in met[turn]:
             here = pl.ds(start, size)
-            s = nt(keys[here, :], using[level])
-            scores[turn, here, :] = s
-            high = jnp.max(s, axis=0, keepdims=True) * scale2 + bias
-            top[turn] = high if top[turn] is None else jnp.maximum(top[turn], high)
-            grads[turn, here, :] = nt(vals[here, :], d_blk)
-    inverse, delta = [None, None], [None, None]
-    for turn in turns:
-        total = jnp.zeros((1, block), F32)
-        acc = jnp.zeros((1, block), F32)
-        for start, size, bias, level in met[turn]:
+            p = scores[turn, here, :] * inverse
+            probs[0, here, cols[turn]] = p.astype(BF)
+            dscores[0, here, cols[turn]] = (p * (grads[turn, here, :] - delta)).astype(BF)
+
+    places = [g_out, None, None]
+    for level in range(LEVELS):
+        places += [g_as[level], g_bs[level]]
+    places.append(g_in)
+    for ref, (start, size, bias, level) in zip(places, segments):
+        if ref is None:
+            continue
+        queries = pl.ds(0, 2 * block)
+        if ref is g_out:
+            queries = cols[0]
+        if ref is g_in:
+            queries = cols[1]
+        right = rep_ref[level - 1, 0, queries, :] if level else q_ref[0, queries, :]
+        here = pl.ds(start, size)
+        ref[0, 0] = (nn(dscores[0, here, queries], right) * scale).astype(BF)
+        ref[1, 0] = nn(probs[0, here, queries], d_ref[0, queries, :]).astype(BF)
+
+
+def finish_kernel(q_ref, d_ref, probs, dscores, keys_t, vals_t, att, gq, own, rows, total_q):
+    span = q_ref.shape[1]
+    block = span // 2
+    columns = probs.shape[1]
+    width = columns - block
+    scale = 1.0 / math.sqrt(128)
+    mine = pl.ds(block, span)
+    own[0, 0] = nn(dscores[0, mine, :], q_ref[0]) * scale
+    own[1, 0] = nn(probs[0, mine, :], d_ref[0])
+    for turn in (0, 1):
+        cols = pl.ds(turn * block, block)
+        met = pl.ds(turn * block, width)
+        att[0, cols, :] = nn(vals_t[0, :, met], probs[0, met, cols]).T.astype(BF)
+        if turn == 0:
+            fine = nn(keys_t[0, :, : 3 * block], dscores[0, : 3 * block, cols])
+        else:
+            fine = nn(keys_t[0, :, block : 3 * block], dscores[0, block : 3 * block, cols])
+            fine = fine + nn(keys_t[0, :, width:], dscores[0, width:, cols])
+        total_q[turn] = fine.T
+        start = 3 * block
+        for level in range(1, LEVELS + 1):
+            size = 2 * (span // 2**level)
             here = pl.ds(start, size)
-            e = jnp.exp2(scores[turn, here, :] * scale2 - (top[turn] - bias))
-            scores[turn, here, :] = e
-            total = total + jnp.sum(e, axis=0, keepdims=True)
-            acc = acc + jnp.sum(e * grads[turn, here, :], axis=0, keepdims=True)
-        inverse[turn] = 1.0 / total
-        delta[turn] = acc * inverse[turn]
-    for turn in turns:
-        for start, size, bias, level in met[turn]:
-            here = pl.ds(start, size)
-            p = scores[turn, here, :] * inverse[turn]
-            probs[here, cols[turn]] = p.astype(BF)
-            dscores[here, cols[turn]] = (p * (grads[turn, here, :] - delta[turn])).astype(BF)
-        first, last = met[turn][0][0], met[turn][-1][0] + met[turn][-1][1]
-        up = nn(vals_t[:, first:last], probs[first:last, cols[turn]])
-        att[0, cols[turn], :] = up.T.astype(BF)
-        if turn == 0:
-            fine = nn(keys_t[:, : 3 * block], dscores[: 3 * block, cols[turn]])
-        else:
-            fine = nn(keys_t[:, block : 3 * block], dscores[block : 3 * block, cols[turn]])
-            tail = columns - block
-            fine = fine + nn(keys_t[:, tail:], dscores[tail:, cols[turn]])
-        total_q[turn] = fine.T
-        for level in range(1, LEVELS + 1):
-            spots = [(s, z) for s, z, _, lev in segments if lev == level]
-            start, size = spots[0][0], spots[0][1] + spots[1][1]
-            up = nn(keys_t[:, start : start + size], dscores[start : start + size, cols[turn]])
-            rows[turn, level - 1] = up.T
+            start += size
+            rows[turn, level - 1] = nn(keys_t[0, :, here], dscores[0, here, cols]).T
             factor = 2**level
             groups = block // factor
             mean = rows[turn, level - 1, pl.ds(0, groups, stride=factor), :]
@@ -269,27 +305,7 @@
             for row in range(factor):
                 spot = pl.ds(row, groups, stride=factor)
                 total_q[turn, spot, :] = total_q[turn, spot, :] + mean
-        gq[0, cols[turn], :] = (total_q[turn] * scale).astype(BF)
-
-    places = [(g_out, None), (own, 0), (own, block)]
-    for level in range(LEVELS):
-        places += [(g_as[level], None), (g_bs[level], None)]
-    places.append((g_in, None))
-    for (ref, offset), (start, size, bias, level) in zip(places, segments):
-        queries = pl.ds(0, 2 * block)
-        if ref is g_out:
-            queries = cols[0]
-        if ref is g_in:
-            queries = cols[1]
-        right = rep_ref[level - 1, 0, queries, :] if level else q_ref[0, queries, :]
-        here = pl.ds(start, size)
-        gk = nn(dscores[here, queries], right) * scale
-        gv = nn(probs[here, queries], d_ref[0, queries, :])
-        for which, value in enumerate((gk, gv)):
-            if offset is None:
-                ref[which, 0] = value.astype(BF)
-            else:
-                ref[which, 0, pl.ds(offset, size), :] = value
+        gq[0, cols, :] = (total_q[turn] * scale).astype(BF)
 
 
 def attend(place, count, q, d, rep, outer, inner, rim_out, rim_in, crossed_a, crossed_b):
@@ -315,27 +331,17 @@
         ]
         + [pair(block)] * 4
         + [pair(size) for size in sizes] * 2,
-        out_specs=[head_spec, head_spec, pair(span), pair(block), pair(block)]
-        + [pair(size) for size in sizes] * 2,
-        out_shape=[
-            shape((heads, span, 128)),
-            shape((heads, span, 128)),
-            shape((2, heads, span, 128), F32),
-            shape((2, heads, block, 128)),
-            shape((2, heads, block, 128)),
-        ]
-        + [shape((2, heads, size, 128)) for size in sizes] * 2,
+        out_specs=[pair(size) for size in [block, block] + sizes * 2]
+        + [pl.BlockSpec((1, columns, span), lambda h: (h, 0, 0))] * 2
+        + [pl.BlockSpec((1, 128, columns), lambda h: (h, 0, 0))] * 2,
+        out_shape=[shape((2, heads, size, 128)) for size in [block, block] + sizes * 2]
+        + [shape((heads, columns, span))] * 2
+        + [shape((heads, 128, columns))] * 2,
         scratch_shapes=[
             pltpu.VMEM((columns, 128), BF),
             pltpu.VMEM((columns, 128), BF),
-            pltpu.VMEM((128, columns), BF),
-            pltpu.VMEM((128, columns), BF),
             pltpu.VMEM((2, columns, block), F32),
             pltpu.VMEM((2, columns, block), F32),
-            pltpu.VMEM((columns, span), BF),
-            pltpu.VMEM((columns, span), BF),
-            pltpu.VMEM((2, LEVELS, block, 128), F32),
-            pltpu.VMEM((2, block, 128), F32),
         ],
         compiler_params=params(30),
         name="attend",
@@ -343,6 +349,38 @@
             flops=flops, bytes_accessed=8 * 2**20, transcendentals=heads * span * width
         ),
     )(place, q, d, rep, outer, inner, rim_out, rim_in, *crossed_a, *crossed_b)
+
+
+def finish(q, d, probs, dscores, keys_t, vals_t):
+    heads, span = q.shape[:2]
+    columns = probs.shape[1]
+    block = span // 2
+
+    def head(*dims):
+        return pl.BlockSpec((1, *dims), lambda h: (h, 0, 0))
+
+    return pl.pallas_call(
+        finish_kernel,
+        grid=(heads,),
+        in_specs=[head(span, 128)] * 2 + [head(columns, span)] * 2 + [head(128, columns)] * 2,
+        out_specs=[head(span, 128)] * 2 + [pl.BlockSpec((2, 1, span, 128), lambda h: (0, h, 0, 0))],
+        out_shape=[
+            shape((heads, span, 128)),
+            shape((heads, span, 128)),
+            shape((2, heads, span, 128), F32),
+        ],
+        scratch_shapes=[
+            pltpu.VMEM((2, LEVELS, block, 128), F32),
+            pltpu.VMEM((2, block, 128), F32),
+        ],
+        compiler_params=params(40),
+        name="finish",
+        cost_estimate=pl.CostEstimate(
+            flops=2 * heads * span * columns * 128 * 3,
+            bytes_accessed=20 * 2**20,
+            transcendentals=0,
+        ),
+    )(q, d, probs, dscores, keys_t, vals_t)
 
 
 def join_kernel(heads, place_ref, att, gq, att_out, gq_out, wide):
@@ -420,10 +458,12 @@
     outer, inner, *coarse = split_kv(place, k2, v2, heads, span)
     crossed_b, crossed_a, rims = exchange(coarse, coarse, outer, inner)
     qh, dh, rep = split_qd(place, q2, d2, heads, span)
-    att, gq, own, g_out, g_in, *grads = attend(
+    g_out, g_in, *grads = attend(
         place, count, qh, dh, rep, outer, inner, *rims, crossed_a, crossed_b
     )
+    grads, kept = grads[: 2 * LEVELS], grads[2 * LEVELS :]
     downs, ups, rims = exchange(grads[:LEVELS], grads[LEVELS:], g_out, g_in)
+    att, gq, own = finish(qh, dh, *kept)
     attended, grad_query = join(place, att, gq)
     grad_key, grad_value = gather(place, own, *rims, *downs, *ups)
     return tuple(

time: 134 us -> 136 us (1.015)
  waiting for transfers between devices: 32.5 us -> 23.2 us
  Pallas kernels: 22.8 us -> 31 us
  local copies, waits for them, and re-layouts: 2.08 us -> 5.21 us
    ppermute x12, waiting for transfers between devices: 32.5 us -> 23.2 us  [crossed(): lax.ppermute(value, 'seq', [(at, to) for at, to in pairs if 0 <= to < cou...]
    pallas_call x0 -> x1, Pallas kernels: none -> 8.15 us  [finish(): pl.pallas_call(finish_kernel, grid=(heads,), in_specs=[head(span, 128)] *...]
    unnamed x8 -> x10, local copies, waits for them, and re-layouts: 2.08 us -> 5.21 us
  transfers between devices with their start and end apart: 16 -> 16, of which waited for: 6 -> 6; matrix products, arithmetic and copies ran while one was open for 0% -> 0% of each run, Pallas kernels for 2% -> 8%
where the time goes in v4:
time: 136 us; the launch traced here: 135 us
  starting transfers between devices  75.1 us (55%)
  Pallas kernels  31 us (23%)
  waiting for transfers between devices  23.2 us (17%)
  local copies, waits for them, and re-layouts  5.21 us (4%)
    ppermute x12, starting transfers between devices, crossed(): lax.ppermute(value, 'seq', [(at, to) for at, to in pairs if 0 <= to < cou...  51.4 us
    ppermute x4, starting transfers between devices, swapped(): lax.ppermute(value, 'seq', [(at, to) for at, to in pairs if 0 <= to < cou...  23.7 us
    ppermute x12, waiting for transfers between devices, crossed(): lax.ppermute(value, 'seq', [(at, to) for at, to in pairs if 0 <= to < cou...  23.2 us
    pallas_call x1, Pallas kernels, attend(): pl.pallas_call(functools.partial(attend_kernel, count), grid=(heads,), in...  17.7 us
    pallas_call x1, Pallas kernels, finish(): pl.pallas_call(finish_kernel, grid=(heads,), in_specs=[head(span, 128)] *...  8.15 us
    unnamed x10, local copies, waits for them, and re-layouts  5.21 us
  transfers between devices with their start and end apart: 16, of which 6 were waited for; matrix products, arithmetic and copies ran while one was open for 0% of the time, Pallas kernels for 8%

profile of v4, /device:TPU:25, one launch (start us, length us, event | category | flops | bytes accessed | tf_op | source)
XLA Modules:
  0.0 135.3 jit_solution(18171011836564268145)
XLA Ops:
  0.6 1.0 copy-done.1
  1.7 1.0 copy-done.2
  2.7 0.9 split_kv.1
  3.6 2.6 %collective-permute-start.1 = (bf16[2,4,256,128]{3,2,1,0:T(8,128)(2,1)S(1)}, bf16[2,4,256,128]{3,2,1,0:T(8,128)(2,1)S(1)}, u32[]{:S(2)}, u32[]{:S(2)}) collective-permute-start(bf16[2,4,256,128]{3,2,1,0:T(8,128)(2,1)S(1)} %get-tuple-element.41.inner), channel_id=1, source_target_pairs={{0,2},{2,0},{4,6},{6,4},{8,10},{10,8},{12,14},{14,12},{16,18},{18,... | collective-permute-start | bytes 1572872 | tf_op jit(solution)/shard_map/ppermute | solution.py:30
  6.2 4.9 %collective-permute-start.2 = (bf16[2,4,128,128]{3,2,1,0:T(8,128)(2,1)S(1)}, bf16[2,4,128,128]{3,2,1,0:T(8,128)(2,1)S(1)}, u32[]{:S(2)}, u32[]{:S(2)}) collective-permute-start(bf16[2,4,128,128]{3,2,1,0:T(8,128)(2,1)S(1)} %get-tuple-element.43.refs_1_), channel_id=1, source_target_pairs={{2,10},{6,14},{8,0},{10,18},{12,4},{14,22},{16,8},{18,26},{20,12},... | collective-permute-start | bytes 786440 | tf_op jit(solution)/shard_map/ppermute | solution.py:22
  11.1 8.8 %collective-permute-start.3 = (bf16[2,4,64,128]{3,2,1,0:T(8,128)(2,1)S(1)}, bf16[2,4,64,128]{3,2,1,0:T(8,128)(2,1)S(1)}, u32[]{:S(2)}, u32[]{:S(2)}) collective-permute-start(bf16[2,4,64,128]{3,2,1,0:T(8,128)(2,1)S(1)} %get-tuple-element.44.refs_2_), channel_id=1, source_target_pairs={{2,18},{6,22},{10,26},{14,30},{16,0},{18,34},{20,4},{22,38},{24,8}... | collective-permute-start | bytes 393224 | tf_op jit(solution)/shard_map/ppermute | solution.py:22
  19.9 8.8 %collective-permute-start = (bf16[2,4,256,128]{3,2,1,0:T(8,128)(2,1)S(1)}, bf16[2,4,256,128]{3,2,1,0:T(8,128)(2,1)S(1)}, u32[]{:S(2)}, u32[]{:S(2)}) collective-permute-start(bf16[2,4,256,128]{3,2,1,0:T(8,128)(2,1)S(1)} %get-tuple-element.40.outer), channel_id=1, source_target_pairs={{2,4},{4,2},{6,8},{8,6},{10,12},{12,10},{14,16},{16,14},{18,20},{2... | collective-permute-start | bytes 1572872 | tf_op jit(solution)/shard_map/ppermute | solution.py:30
  28.7 1.9 %collective-permute-start.7 = (bf16[2,4,256,128]{3,2,1,0:T(8,128)(2,1)S(1)}, bf16[2,4,256,128]{3,2,1,0:T(8,128)(2,1)S(1)}, u32[]{:S(2)}, u32[]{:S(2)}) collective-permute-start(bf16[2,4,256,128]{3,2,1,0:T(8,128)(2,1)S(1)} %get-tuple-element.42.refs_0_), channel_id=1, source_target_pairs={{2,6},{4,0},{6,10},{8,4},{10,14},{12,8},{14,18},{16,12},{18,22},{2... | collective-permute-start | bytes 1572872 | tf_op jit(solution)/shard_map/ppermute | solution.py:22
  30.6 0.6 collective-permute-done.3.refs_4_.rest_5_
  31.2 0.1 later.2
  31.3 7.5 %collective-permute-start.4 = (bf16[2,4,256,128]{3,2,1,0:T(8,128)(2,1)S(1)}, bf16[2,4,256,128]{3,2,1,0:T(8,128)(2,1)S(1)}, u32[]{:S(2)}, u32[]{:S(2)}) collective-permute-start(bf16[2,4,256,128]{3,2,1,0:T(8,128)(2,1)S(1)} %get-tuple-element.45), channel_id=1, source_target_pairs={{0,4},{4,8},{6,2},{8,12},{10,6},{12,16},{14,10},{16,20},{18,14},{2... | collective-permute-start | bytes 1572872 | tf_op jit(solution)/shard_map/ppermute | solution.py:22
  38.8 2.2 %collective-permute-start.5 = (bf16[2,4,128,128]{3,2,1,0:T(8,128)(2,1)S(1)}, bf16[2,4,128,128]{3,2,1,0:T(8,128)(2,1)S(1)}, u32[]{:S(2)}, u32[]{:S(2)}) collective-permute-start(bf16[2,4,128,128]{3,2,1,0:T(8,128)(2,1)S(1)} %get-tuple-element.46), channel_id=1, source_target_pairs={{0,8},{4,12},{8,16},{10,2},{12,20},{14,6},{16,24},{18,10},{20,28},... | collective-permute-start | bytes 786440 | tf_op jit(solution)/shard_map/ppermute | solution.py:22
  41.0 5.0 %collective-permute-start.6 = (bf16[2,4,64,128]{3,2,1,0:T(8,128)(2,1)S(1)}, bf16[2,4,64,128]{3,2,1,0:T(8,128)(2,1)S(1)}, u32[]{:S(2)}, u32[]{:S(2)}) collective-permute-start(bf16[2,4,64,128]{3,2,1,0:T(8,128)(2,1)S(1)} %get-tuple-element.47), channel_id=1, source_target_pairs={{0,16},{4,20},{8,24},{12,28},{16,32},{18,2},{20,36},{22,6},{24,40}... | collective-permute-start | bytes 393224 | tf_op jit(solution)/shard_map/ppermute | solution.py:22
  46.0 0.9 split_qd.1
  46.9 3.0 %collective-permute-done.7.rest_3_ = bf16[2,4,256,128]{3,2,1,0:T(8,128)(2,1)S(1)} collective-permute-done((bf16[2,4,256,128]{3,2,1,0:T(8,128)(2,1)S(1)}, bf16[2,4,256,128]{3,2,1,0:T(8,128)(2,1)S(1)}, u32[]{:S(2)}, u32[]{:S(2)}) %collective-permute-start.7) | collective-permute-done | bytes 524320 | tf_op jit(solution)/shard_map/ppermute | solution.py:22
  50.0 10.8 %collective-permute-done.6.rest_2_ = bf16[2,4,64,128]{3,2,1,0:T(8,128)(2,1)S(1)} collective-permute-done((bf16[2,4,64,128]{3,2,1,0:T(8,128)(2,1)S(1)}, bf16[2,4,64,128]{3,2,1,0:T(8,128)(2,1)S(1)}, u32[]{:S(2)}, u32[]{:S(2)}) %collective-permute-start.6) | collective-permute-done | bytes 131104 | tf_op jit(solution)/shard_map/ppermute | solution.py:22
  60.8 17.7 %attend.1 = (bf16[2,4,256,128]{3,2,1,0:T(8,128)(2,1)S(1)}, bf16[2,4,256,128]{3,2,1,0:T(8,128)(2,1)S(1)}, bf16[2,4,256,128]{3,2,1,0:T(8,128)(2,1)S(1)}, bf16[2,4,...) custom-call(s32[1]{0:T(128)} %bitcast.place_ref, ...), custom_call_target="tpu_custom_call" | custom-call | flops 5234491392 | bytes 8388608 | tf_op jit(solution)/shard_map/attend/pallas_call | solution.py:323
  78.5 3.1 %copy-done = bf16[4,1920,512]{2,1,0:T(8,128)(2,1)} copy-done((bf16[4,1920,512]{2,1,0:T(8,128)(2,1)}, bf16[4,1920,512]{2,1,0:T(8,128)(2,1)S(1)}, u32[]{:S(2)}) %copy-start) | copy-done | bytes 7864344
  81.6 1.9 %collective-permute-start.9 = (bf16[2,4,256,128]{3,2,1,0:T(8,128)(2,1)S(1)}, bf16[2,4,256,128]{3,2,1,0:T(8,128)(2,1)S(1)}, u32[]{:S(2)}, u32[]{:S(2)}) collective-permute-start(bf16[2,4,256,128]{3,2,1,0:T(8,128)(2,1)S(1)} %get-tuple-element.58), channel_id=1, source_target_pairs={{0,2},{2,0},{4,6},{6,4},{8,10},{10,8},{12,14},{14,12},{16,18},{18,... | collective-permute-start | bytes 1572872 | tf_op jit(solution)/shard_map/ppermute | solution.py:30
  83.6 1.9 %collective-permute-start.11 = (bf16[2,4,128,128]{3,2,1,0:T(8,128)(2,1)S(1)}, bf16[2,4,128,128]{3,2,1,0:T(8,128)(2,1)S(1)}, u32[]{:S(2)}, u32[]{:S(2)}) collective-permute-start(bf16[2,4,128,128]{3,2,1,0:T(8,128)(2,1)S(1)} %get-tuple-element.60), channel_id=1, source_target_pairs={{2,10},{6,14},{8,0},{10,18},{12,4},{14,22},{16,8},{18,26},{20,12},... | collective-permute-start | bytes 786440 | tf_op jit(solution)/shard_map/ppermute | solution.py:22
  85.5 3.5 %collective-permute-start.12 = (bf16[2,4,64,128]{3,2,1,0:T(8,128)(2,1)S(1)}, bf16[2,4,64,128]{3,2,1,0:T(8,128)(2,1)S(1)}, u32[]{:S(2)}, u32[]{:S(2)}) collective-permute-start(bf16[2,4,64,128]{3,2,1,0:T(8,128)(2,1)S(1)} %get-tuple-element.61), channel_id=1, source_target_pairs={{2,18},{6,22},{10,26},{14,30},{16,0},{18,34},{20,4},{22,38},{24,8}... | collective-permute-start | bytes 393224 | tf_op jit(solution)/shard_map/ppermute | solution.py:22
  89.0 10.5 %collective-permute-start.8 = (bf16[2,4,256,128]{3,2,1,0:T(8,128)(2,1)S(1)}, bf16[2,4,256,128]{3,2,1,0:T(8,128)(2,1)S(1)}, u32[]{:S(2)}, u32[]{:S(2)}) collective-permute-start(bf16[2,4,256,128]{3,2,1,0:T(8,128)(2,1)S(1)} %get-tuple-element.57), channel_id=1, source_target_pairs={{2,4},{4,2},{6,8},{8,6},{10,12},{12,10},{14,16},{16,14},{18,20},{2... | collective-permute-start | bytes 1572872 | tf_op jit(solution)/shard_map/ppermute | solution.py:30
  99.5 4.4 %collective-permute-start.10 = (bf16[2,4,256,128]{3,2,1,0:T(8,128)(2,1)S(1)}, bf16[2,4,256,128]{3,2,1,0:T(8,128)(2,1)S(1)}, u32[]{:S(2)}, u32[]{:S(2)}) collective-permute-start(bf16[2,4,256,128]{3,2,1,0:T(8,128)(2,1)S(1)} %get-tuple-element.59), channel_id=1, source_target_pairs={{2,6},{4,0},{6,10},{8,4},{10,14},{12,8},{14,18},{16,12},{18,22},{2... | collective-permute-start | bytes 1572872 | tf_op jit(solution)/shard_map/ppermute | solution.py:22
  103.9 0.3 collective-permute-done.12.refs_4_.refs_2_
  104.3 6.5 %collective-permute-start.13 = (bf16[2,4,256,128]{3,2,1,0:T(8,128)(2,1)S(1)}, bf16[2,4,256,128]{3,2,1,0:T(8,128)(2,1)S(1)}, u32[]{:S(2)}, u32[]{:S(2)}) collective-permute-start(bf16[2,4,256,128]{3,2,1,0:T(8,128)(2,1)S(1)} %get-tuple-element.65), channel_id=1, source_target_pairs={{0,4},{4,8},{6,2},{8,12},{10,6},{12,16},{14,10},{16,20},{18,14},{2... | collective-permute-start | bytes 1572872 | tf_op jit(solution)/shard_map/ppermute | solution.py:22
  110.7 2.8 %collective-permute-start.15 = (bf16[2,4,64,128]{3,2,1,0:T(8,128)(2,1)S(1)}, bf16[2,4,64,128]{3,2,1,0:T(8,128)(2,1)S(1)}, u32[]{:S(2)}, u32[]{:S(2)}) collective-permute-start(bf16[2,4,64,128]{3,2,1,0:T(8,128)(2,1)S(1)} %get-tuple-element.67), channel_id=1, source_target_pairs={{0,16},{4,20},{8,24},{12,28},{16,32},{18,2},{20,36},{22,6},{24,40}... | collective-permute-start | bytes 393224 | tf_op jit(solution)/shard_map/ppermute | solution.py:22
  113.6 1.9 %collective-permute-start.14 = (bf16[2,4,128,128]{3,2,1,0:T(8,128)(2,1)S(1)}, bf16[2,4,128,128]{3,2,1,0:T(8,128)(2,1)S(1)}, u32[]{:S(2)}, u32[]{:S(2)}) collective-permute-start(bf16[2,4,128,128]{3,2,1,0:T(8,128)(2,1)S(1)} %get-tuple-element.66), channel_id=1, source_target_pairs={{0,8},{4,12},{8,16},{10,2},{12,20},{14,6},{16,24},{18,10},{20,28},... | collective-permute-start | bytes 786440 | tf_op jit(solution)/shard_map/ppermute | solution.py:22
  115.5 8.1 %finish.1 = (bf16[4,512,128]{2,1,0:T(8,128)(2,1)S(1)}, bf16[4,512,128]{2,1,0:T(8,128)(2,1)S(1)}, f32[2,4,512,128]{3,2,1,0:T(8,128)S(1)}) custom-call(bf16[4,512,128]{2,1,0:T(8,128)(2,1)S(1)} %get-tuple-element.37.q_ref, bf16[4,512,128]{2,1,0:T(8,128)(2,1)S(1)} %get-tuple-element.38.d_ref, bf16[4,1920,512]{2,1,0:T(8,128)(2,1)} %copy-done, ...), custom_call_target="tpu_custom_call" | custom-call | flops 3019898880 | bytes 20971520 | tf_op jit(solution)/shard_map/finish/pallas_call | solution.py:362
  123.6 1.2 join.1
  124.9 3.7 %collective-permute-done.15.refs_5_ = bf16[2,4,64,128]{3,2,1,0:T(8,128)(2,1)S(1)} collective-permute-done((bf16[2,4,64,128]{3,2,1,0:T(8,128)(2,1)S(1)}, bf16[2,4,64,128]{3,2,1,0:T(8,128)(2,1)S(1)}, u32[]{:S(2)}, u32[]{:S(2)}) %collective-permute-start.15) | collective-permute-done | bytes 131104 | tf_op jit(solution)/shard_map/ppermute | solution.py:22
  128.6 4.8 %collective-permute-done.14.refs_4_ = bf16[2,4,128,128]{3,2,1,0:T(8,128)(2,1)S(1)} collective-permute-done((bf16[2,4,128,128]{3,2,1,0:T(8,128)(2,1)S(1)}, bf16[2,4,128,128]{3,2,1,0:T(8,128)(2,1)S(1)}, u32[]{:S(2)}, u32[]{:S(2)}) %collective-permute-start.14) | collective-permute-done | bytes 262176 | tf_op jit(solution)/shard_map/ppermute | solution.py:22
  133.4 2.0 %gather.1 = (bf16[2048,128]{1,0:T(8,128)(2,1)}, bf16[2048,128]{1,0:T(8,128)(2,1)}) custom-call(s32[1]{0:T(128)} %bitcast.place_ref, f32[2,4,512,128]{3,2,1,0:T(8,128)S(1)} %get-tuple-element.56.own, bf16[2,4,256,128]{3,2,1,0:T(8,128)(2,1)S(1)} %collective-permute-done.8.outer, bf16[2,4,256,128]{3,2,1,0:T(8,128)(2,1)S(1)} %collective-permute-done.9.refs_5_.inner, ...), custom_call_target="tpu_custom_call" | custom-call | bytes 8388608 | tf_op jit(solution)/shard_map/gather/pallas_call | solution.py:437
  (18 shorter events, 0.1 us)
Async XLA Ops:
  0.6 1.0 copy-start.1
  1.7 1.0 copy-start.2
  2.7 43.2 %copy-start.3 = (bf16[512,4,128]{2,1,0:T(4,128)(2,1)S(1)}, bf16[512,4,128]{2,1,0:T(4,128)(2,1)}, u32[]{:S(2)}) copy-start(bf16[512,4,128]{2,1,0:T(4,128)(2,1)} %param.4) | copy-start | bytes 1572868
  2.7 43.3 %copy-start.4 = (bf16[512,4,128]{2,1,0:T(4,128)(2,1)S(1)}, bf16[512,4,128]{2,1,0:T(4,128)(2,1)}, u32[]{:S(2)}) copy-start(bf16[512,4,128]{2,1,0:T(4,128)(2,1)} %param.7) | copy-start | bytes 1572868
  3.6 27.6 %collective-permute-start.1 = (bf16[2,4,256,128]{3,2,1,0:T(8,128)(2,1)S(1)}, bf16[2,4,256,128]{3,2,1,0:T(8,128)(2,1)S(1)}, u32[]{:S(2)}, u32[]{:S(2)}) collective-permute-start(bf16[2,4,256,128]{3,2,1,0:T(8,128)(2,1)S(1)} %get-tuple-element.41.inner), channel_id=1, source_target_pairs={{0,2},{2,0},{4,6},{6,4},{8,10},{10,8},{12,14},{14,12},{16,18},{18,... | collective-permute-start | bytes 1572872 | tf_op jit(solution)/shard_map/ppermute | solution.py:30
  6.2 25.0 %collective-permute-start.2 = (bf16[2,4,128,128]{3,2,1,0:T(8,128)(2,1)S(1)}, bf16[2,4,128,128]{3,2,1,0:T(8,128)(2,1)S(1)}, u32[]{:S(2)}, u32[]{:S(2)}) collective-permute-start(bf16[2,4,128,128]{3,2,1,0:T(8,128)(2,1)S(1)} %get-tuple-element.43.refs_1_), channel_id=1, source_target_pairs={{2,10},{6,14},{8,0},{10,18},{12,4},{14,22},{16,8},{18,26},{20,12},... | collective-permute-start | bytes 786440 | tf_op jit(solution)/shard_map/ppermute | solution.py:22
  11.1 20.1 %collective-permute-start.3 = (bf16[2,4,64,128]{3,2,1,0:T(8,128)(2,1)S(1)}, bf16[2,4,64,128]{3,2,1,0:T(8,128)(2,1)S(1)}, u32[]{:S(2)}, u32[]{:S(2)}) collective-permute-start(bf16[2,4,64,128]{3,2,1,0:T(8,128)(2,1)S(1)} %get-tuple-element.44.refs_2_), channel_id=1, source_target_pairs={{2,18},{6,22},{10,26},{14,30},{16,0},{18,34},{20,4},{22,38},{24,8}... | collective-permute-start | bytes 393224 | tf_op jit(solution)/shard_map/ppermute | solution.py:22
  19.9 27.0 %collective-permute-start = (bf16[2,4,256,128]{3,2,1,0:T(8,128)(2,1)S(1)}, bf16[2,4,256,128]{3,2,1,0:T(8,128)(2,1)S(1)}, u32[]{:S(2)}, u32[]{:S(2)}) collective-permute-start(bf16[2,4,256,128]{3,2,1,0:T(8,128)(2,1)S(1)} %get-tuple-element.40.outer), channel_id=1, source_target_pairs={{2,4},{4,2},{6,8},{8,6},{10,12},{12,10},{14,16},{16,14},{18,20},{2... | collective-permute-start | bytes 1572872 | tf_op jit(solution)/shard_map/ppermute | solution.py:30
  28.7 21.3 %collective-permute-start.7 = (bf16[2,4,256,128]{3,2,1,0:T(8,128)(2,1)S(1)}, bf16[2,4,256,128]{3,2,1,0:T(8,128)(2,1)S(1)}, u32[]{:S(2)}, u32[]{:S(2)}) collective-permute-start(bf16[2,4,256,128]{3,2,1,0:T(8,128)(2,1)S(1)} %get-tuple-element.42.refs_0_), channel_id=1, source_target_pairs={{2,6},{4,0},{6,10},{8,4},{10,14},{12,8},{14,18},{16,12},{18,22},{2... | collective-permute-start | bytes 1572872 | tf_op jit(solution)/shard_map/ppermute | solution.py:22
  31.3 29.5 %collective-permute-start.4 = (bf16[2,4,256,128]{3,2,1,0:T(8,128)(2,1)S(1)}, bf16[2,4,256,128]{3,2,1,0:T(8,128)(2,1)S(1)}, u32[]{:S(2)}, u32[]{:S(2)}) collective-permute-start(bf16[2,4,256,128]{3,2,1,0:T(8,128)(2,1)S(1)} %get-tuple-element.45), channel_id=1, source_target_pairs={{0,4},{4,8},{6,2},{8,12},{10,6},{12,16},{14,10},{16,20},{18,14},{2... | collective-permute-start | bytes 1572872 | tf_op jit(solution)/shard_map/ppermute | solution.py:22
  38.8 21.9 %collective-permute-start.5 = (bf16[2,4,128,128]{3,2,1,0:T(8,128)(2,1)S(1)}, bf16[2,4,128,128]{3,2,1,0:T(8,128)(2,1)S(1)}, u32[]{:S(2)}, u32[]{:S(2)}) collective-permute-start(bf16[2,4,128,128]{3,2,1,0:T(8,128)(2,1)S(1)} %get-tuple-element.46), channel_id=1, source_target_pairs={{0,8},{4,12},{8,16},{10,2},{12,20},{14,6},{16,24},{18,10},{20,28},... | collective-permute-start | bytes 786440 | tf_op jit(solution)/shard_map/ppermute | solution.py:22
  41.0 19.8 %collective-permute-start.6 = (bf16[2,4,64,128]{3,2,1,0:T(8,128)(2,1)S(1)}, bf16[2,4,64,128]{3,2,1,0:T(8,128)(2,1)S(1)}, u32[]{:S(2)}, u32[]{:S(2)}) collective-permute-start(bf16[2,4,64,128]{3,2,1,0:T(8,128)(2,1)S(1)} %get-tuple-element.47), channel_id=1, source_target_pairs={{0,16},{4,20},{8,24},{12,28},{16,32},{18,2},{20,36},{22,6},{24,40}... | collective-permute-start | bytes 393224 | tf_op jit(solution)/shard_map/ppermute | solution.py:22
  78.5 3.1 %copy-start = (bf16[4,1920,512]{2,1,0:T(8,128)(2,1)}, bf16[4,1920,512]{2,1,0:T(8,128)(2,1)S(1)}, u32[]{:S(2)}) copy-start(bf16[4,1920,512]{2,1,0:T(8,128)(2,1)S(1)} %get-tuple-element.48.probs) | copy-start | bytes 23592964
  81.6 22.6 %collective-permute-start.9 = (bf16[2,4,256,128]{3,2,1,0:T(8,128)(2,1)S(1)}, bf16[2,4,256,128]{3,2,1,0:T(8,128)(2,1)S(1)}, u32[]{:S(2)}, u32[]{:S(2)}) collective-permute-start(bf16[2,4,256,128]{3,2,1,0:T(8,128)(2,1)S(1)} %get-tuple-element.58), channel_id=1, source_target_pairs={{0,2},{2,0},{4,6},{6,4},{8,10},{10,8},{12,14},{14,12},{16,18},{18,... | collective-permute-start | bytes 1572872 | tf_op jit(solution)/shard_map/ppermute | solution.py:30
  83.6 20.6 %collective-permute-start.11 = (bf16[2,4,128,128]{3,2,1,0:T(8,128)(2,1)S(1)}, bf16[2,4,128,128]{3,2,1,0:T(8,128)(2,1)S(1)}, u32[]{:S(2)}, u32[]{:S(2)}) collective-permute-start(bf16[2,4,128,128]{3,2,1,0:T(8,128)(2,1)S(1)} %get-tuple-element.60), channel_id=1, source_target_pairs={{2,10},{6,14},{8,0},{10,18},{12,4},{14,22},{16,8},{18,26},{20,12},... | collective-permute-start | bytes 786440 | tf_op jit(solution)/shard_map/ppermute | solution.py:22
  85.5 18.7 %collective-permute-start.12 = (bf16[2,4,64,128]{3,2,1,0:T(8,128)(2,1)S(1)}, bf16[2,4,64,128]{3,2,1,0:T(8,128)(2,1)S(1)}, u32[]{:S(2)}, u32[]{:S(2)}) collective-permute-start(bf16[2,4,64,128]{3,2,1,0:T(8,128)(2,1)S(1)} %get-tuple-element.61), channel_id=1, source_target_pairs={{2,18},{6,22},{10,26},{14,30},{16,0},{18,34},{20,4},{22,38},{24,8}... | collective-permute-start | bytes 393224 | tf_op jit(solution)/shard_map/ppermute | solution.py:22
  89.0 35.8 %collective-permute-start.8 = (bf16[2,4,256,128]{3,2,1,0:T(8,128)(2,1)S(1)}, bf16[2,4,256,128]{3,2,1,0:T(8,128)(2,1)S(1)}, u32[]{:S(2)}, u32[]{:S(2)}) collective-permute-start(bf16[2,4,256,128]{3,2,1,0:T(8,128)(2,1)S(1)} %get-tuple-element.57), channel_id=1, source_target_pairs={{2,4},{4,2},{6,8},{8,6},{10,12},{12,10},{14,16},{16,14},{18,20},{2... | collective-permute-start | bytes 1572872 | tf_op jit(solution)/shard_map/ppermute | solution.py:30
  99.5 25.4 %collective-permute-start.10 = (bf16[2,4,256,128]{3,2,1,0:T(8,128)(2,1)S(1)}, bf16[2,4,256,128]{3,2,1,0:T(8,128)(2,1)S(1)}, u32[]{:S(2)}, u32[]{:S(2)}) collective-permute-start(bf16[2,4,256,128]{3,2,1,0:T(8,128)(2,1)S(1)} %get-tuple-element.59), channel_id=1, source_target_pairs={{2,6},{4,0},{6,10},{8,4},{10,14},{12,8},{14,18},{16,12},{18,22},{2... | collective-permute-start | bytes 1572872 | tf_op jit(solution)/shard_map/ppermute | solution.py:22
  104.3 29.1 %collective-permute-start.13 = (bf16[2,4,256,128]{3,2,1,0:T(8,128)(2,1)S(1)}, bf16[2,4,256,128]{3,2,1,0:T(8,128)(2,1)S(1)}, u32[]{:S(2)}, u32[]{:S(2)}) collective-permute-start(bf16[2,4,256,128]{3,2,1,0:T(8,128)(2,1)S(1)} %get-tuple-element.65), channel_id=1, source_target_pairs={{0,4},{4,8},{6,2},{8,12},{10,6},{12,16},{14,10},{16,20},{18,14},{2... | collective-permute-start | bytes 1572872 | tf_op jit(solution)/shard_map/ppermute | solution.py:22
  110.7 17.9 %collective-permute-start.15 = (bf16[2,4,64,128]{3,2,1,0:T(8,128)(2,1)S(1)}, bf16[2,4,64,128]{3,2,1,0:T(8,128)(2,1)S(1)}, u32[]{:S(2)}, u32[]{:S(2)}) collective-permute-start(bf16[2,4,64,128]{3,2,1,0:T(8,128)(2,1)S(1)} %get-tuple-element.67), channel_id=1, source_target_pairs={{0,16},{4,20},{8,24},{12,28},{16,32},{18,2},{20,36},{22,6},{24,40}... | collective-permute-start | bytes 393224 | tf_op jit(solution)/shard_map/ppermute | solution.py:22
  113.6 19.8 %collective-permute-start.14 = (bf16[2,4,128,128]{3,2,1,0:T(8,128)(2,1)S(1)}, bf16[2,4,128,128]{3,2,1,0:T(8,128)(2,1)S(1)}, u32[]{:S(2)}, u32[]{:S(2)}) collective-permute-start(bf16[2,4,128,128]{3,2,1,0:T(8,128)(2,1)S(1)} %get-tuple-element.66), channel_id=1, source_target_pairs={{0,8},{4,12},{8,16},{10,2},{12,20},{14,6},{16,24},{18,10},{20,28},... | collective-permute-start | bytes 786440 | tf_op jit(solution)/shard_map/ppermute | solution.py:22

commit v5 on v2

--- a/solution.py
+++ b/solution.py
@@ -10,6 +10,7 @@
 
 BLOCK = 256
 LEVELS = 3
+STEP = 32
 LOG2E = math.log2(math.e)
 
 BF = jnp.bfloat16
@@ -174,6 +175,13 @@
         name="split_qd",
         cost_estimate=pl.CostEstimate(flops=0, bytes_accessed=8 * 2**20, transcendentals=0),
     )(place, q2, d2)
+
+
+def folded(x, op):
+    result = x[:8]
+    for row in range(8, x.shape[0], 8):
+        result = op(result, x[row : row + 8])
+    return result
 
 
 def attend_kernel(count, place_ref, q_ref, d_ref, rep_ref, outer, inner, rim_out, rim_in, *rest):
@@ -224,24 +232,26 @@
             here = pl.ds(start, size)
             s = nt(keys[here, :], using[level])
             scores[turn, here, :] = s
-            high = jnp.max(s, axis=0, keepdims=True) * scale2 + bias
+            high = jnp.max(folded(s, jnp.maximum), axis=0, keepdims=True) * scale2 + bias
             top[turn] = high if top[turn] is None else jnp.maximum(top[turn], high)
             grads[turn, here, :] = nt(vals[here, :], d_blk)
     inverse, delta = [None, None], [None, None]
     for turn in turns:
-        total = jnp.zeros((1, block), F32)
-        acc = jnp.zeros((1, block), F32)
+        total = jnp.zeros((8, block), F32)
+        acc = jnp.zeros((8, block), F32)
         for start, size, bias, level in met[turn]:
-            here = pl.ds(start, size)
-            e = jnp.exp2(scores[turn, here, :] * scale2 - (top[turn] - bias))
-            scores[turn, here, :] = e
-            total = total + jnp.sum(e, axis=0, keepdims=True)
-            acc = acc + jnp.sum(e * grads[turn, here, :], axis=0, keepdims=True)
-        inverse[turn] = 1.0 / total
-        delta[turn] = acc * inverse[turn]
+            shift = top[turn] - bias
+            for row in range(start, start + size, STEP):
+                here = pl.ds(row, STEP)
+                e = jnp.exp2(scores[turn, here, :] * scale2 - shift)
+                scores[turn, here, :] = e
+                total = total + folded(e, jnp.add)
+                acc = acc + folded(e * grads[turn, here, :], jnp.add)
+        inverse[turn] = 1.0 / jnp.sum(total, axis=0, keepdims=True)
+        delta[turn] = jnp.sum(acc, axis=0, keepdims=True) * inverse[turn]
     for turn in turns:
-        for start, size, bias, level in met[turn]:
-            here = pl.ds(start, size)
+        for row in range(met[turn][0][0], met[turn][-1][0] + met[turn][-1][1], STEP):
+            here = pl.ds(row, STEP)
             p = scores[turn, here, :] * inverse[turn]
             probs[here, cols[turn]] = p.astype(BF)
             dscores[here, cols[turn]] = (p * (grads[turn, here, :] - delta[turn])).astype(BF)

time: 134 us -> 134 us (level)
  no operation moved by 1% of the time
where the time goes in v5:
time: 134 us; the launch traced here: 133 us
  starting transfers between devices  75.1 us (56%)
  waiting for transfers between devices  32.5 us (24%)
  Pallas kernels  22.6 us (17%)
  local copies, waits for them, and re-layouts  2.08 us (2%)
    ppermute x12, starting transfers between devices, crossed(): lax.ppermute(value, 'seq', [(at, to) for at, to in pairs if 0 <= to < cou...  51.3 us
    ppermute x12, waiting for transfers between devices, crossed(): lax.ppermute(value, 'seq', [(at, to) for at, to in pairs if 0 <= to < cou...  32.5 us
    ppermute x4, starting transfers between devices, swapped(): lax.ppermute(value, 'seq', [(at, to) for at, to in pairs if 0 <= to < cou...  23.8 us
    pallas_call x1, Pallas kernels, attend(): pl.pallas_call(functools.partial(attend_kernel, count), grid=(heads,), in...  17.5 us
  transfers between devices with their start and end apart: 16, of which 6 were waited for; matrix products, arithmetic and copies ran while one was open for 0% of the time, Pallas kernels for 2%

profile of v5, /device:TPU:25, one launch (start us, length us, event | category | flops | bytes accessed | tf_op | source)
XLA Modules:
  0.0 133.1 jit_solution(10614362294129224750)
XLA Ops:
  0.6 1.0 copy-done
  1.7 1.0 copy-done.1
  2.7 0.9 split_kv.1
  3.6 2.6 %collective-permute-start.1 = (bf16[2,4,256,128]{3,2,1,0:T(8,128)(2,1)S(1)}, bf16[2,4,256,128]{3,2,1,0:T(8,128)(2,1)S(1)}, u32[]{:S(2)}, u32[]{:S(2)}) collective-permute-start(bf16[2,4,256,128]{3,2,1,0:T(8,128)(2,1)S(1)} %get-tuple-element.37.inner), channel_id=1, source_target_pairs={{0,2},{2,0},{4,6},{6,4},{8,10},{10,8},{12,14},{14,12},{16,18},{18,... | collective-permute-start | bytes 1572872 | tf_op jit(solution)/shard_map/ppermute | solution.py:31
  6.2 4.9 %collective-permute-start.2 = (bf16[2,4,128,128]{3,2,1,0:T(8,128)(2,1)S(1)}, bf16[2,4,128,128]{3,2,1,0:T(8,128)(2,1)S(1)}, u32[]{:S(2)}, u32[]{:S(2)}) collective-permute-start(bf16[2,4,128,128]{3,2,1,0:T(8,128)(2,1)S(1)} %get-tuple-element.39.refs_1_), channel_id=1, source_target_pairs={{2,10},{6,14},{8,0},{10,18},{12,4},{14,22},{16,8},{18,26},{20,12},... | collective-permute-start | bytes 786440 | tf_op jit(solution)/shard_map/ppermute | solution.py:23
  11.1 8.8 %collective-permute-start.3 = (bf16[2,4,64,128]{3,2,1,0:T(8,128)(2,1)S(1)}, bf16[2,4,64,128]{3,2,1,0:T(8,128)(2,1)S(1)}, u32[]{:S(2)}, u32[]{:S(2)}) collective-permute-start(bf16[2,4,64,128]{3,2,1,0:T(8,128)(2,1)S(1)} %get-tuple-element.40.refs_2_), channel_id=1, source_target_pairs={{2,18},{6,22},{10,26},{14,30},{16,0},{18,34},{20,4},{22,38},{24,8}... | collective-permute-start | bytes 393224 | tf_op jit(solution)/shard_map/ppermute | solution.py:23
  19.9 8.8 %collective-permute-start = (bf16[2,4,256,128]{3,2,1,0:T(8,128)(2,1)S(1)}, bf16[2,4,256,128]{3,2,1,0:T(8,128)(2,1)S(1)}, u32[]{:S(2)}, u32[]{:S(2)}) collective-permute-start(bf16[2,4,256,128]{3,2,1,0:T(8,128)(2,1)S(1)} %get-tuple-element.36.outer), channel_id=1, source_target_pairs={{2,4},{4,2},{6,8},{8,6},{10,12},{12,10},{14,16},{16,14},{18,20},{2... | collective-permute-start | bytes 1572872 | tf_op jit(solution)/shard_map/ppermute | solution.py:31
  28.7 1.9 %collective-permute-start.7 = (bf16[2,4,256,128]{3,2,1,0:T(8,128)(2,1)S(1)}, bf16[2,4,256,128]{3,2,1,0:T(8,128)(2,1)S(1)}, u32[]{:S(2)}, u32[]{:S(2)}) collective-permute-start(bf16[2,4,256,128]{3,2,1,0:T(8,128)(2,1)S(1)} %get-tuple-element.38.refs_0_), channel_id=1, source_target_pairs={{2,6},{4,0},{6,10},{8,4},{10,14},{12,8},{14,18},{16,12},{18,22},{2... | collective-permute-start | bytes 1572872 | tf_op jit(solution)/shard_map/ppermute | solution.py:23
  30.6 0.6 collective-permute-done.3.refs_4_.rest_5_
  31.2 0.0 collective-permute-done.2.refs_3_.rest_4_
  31.2 0.1 later.2
  31.3 7.5 %collective-permute-start.4 = (bf16[2,4,256,128]{3,2,1,0:T(8,128)(2,1)S(1)}, bf16[2,4,256,128]{3,2,1,0:T(8,128)(2,1)S(1)}, u32[]{:S(2)}, u32[]{:S(2)}) collective-permute-start(bf16[2,4,256,128]{3,2,1,0:T(8,128)(2,1)S(1)} %get-tuple-element.41), channel_id=1, source_target_pairs={{0,4},{4,8},{6,2},{8,12},{10,6},{12,16},{14,10},{16,20},{18,14},{2... | collective-permute-start | bytes 1572872 | tf_op jit(solution)/shard_map/ppermute | solution.py:23
  38.8 2.2 %collective-permute-start.5 = (bf16[2,4,128,128]{3,2,1,0:T(8,128)(2,1)S(1)}, bf16[2,4,128,128]{3,2,1,0:T(8,128)(2,1)S(1)}, u32[]{:S(2)}, u32[]{:S(2)}) collective-permute-start(bf16[2,4,128,128]{3,2,1,0:T(8,128)(2,1)S(1)} %get-tuple-element.42), channel_id=1, source_target_pairs={{0,8},{4,12},{8,16},{10,2},{12,20},{14,6},{16,24},{18,10},{20,28},... | collective-permute-start | bytes 786440 | tf_op jit(solution)/shard_map/ppermute | solution.py:23
  41.0 5.0 %collective-permute-start.6 = (bf16[2,4,64,128]{3,2,1,0:T(8,128)(2,1)S(1)}, bf16[2,4,64,128]{3,2,1,0:T(8,128)(2,1)S(1)}, u32[]{:S(2)}, u32[]{:S(2)}) collective-permute-start(bf16[2,4,64,128]{3,2,1,0:T(8,128)(2,1)S(1)} %get-tuple-element.43), channel_id=1, source_target_pairs={{0,16},{4,20},{8,24},{12,28},{16,32},{18,2},{20,36},{22,6},{24,40}... | collective-permute-start | bytes 393224 | tf_op jit(solution)/shard_map/ppermute | solution.py:23
  46.0 0.9 split_qd.1
  46.9 3.0 %collective-permute-done.7.rest_3_ = bf16[2,4,256,128]{3,2,1,0:T(8,128)(2,1)S(1)} collective-permute-done((bf16[2,4,256,128]{3,2,1,0:T(8,128)(2,1)S(1)}, bf16[2,4,256,128]{3,2,1,0:T(8,128)(2,1)S(1)}, u32[]{:S(2)}, u32[]{:S(2)}) %collective-permute-start.7) | collective-permute-done | bytes 524320 | tf_op jit(solution)/shard_map/ppermute | solution.py:23
  50.0 10.8 %collective-permute-done.6.rest_2_ = bf16[2,4,64,128]{3,2,1,0:T(8,128)(2,1)S(1)} collective-permute-done((bf16[2,4,64,128]{3,2,1,0:T(8,128)(2,1)S(1)}, bf16[2,4,64,128]{3,2,1,0:T(8,128)(2,1)S(1)}, u32[]{:S(2)}, u32[]{:S(2)}) %collective-permute-start.6) | collective-permute-done | bytes 131104 | tf_op jit(solution)/shard_map/ppermute | solution.py:23
  60.8 17.5 %attend.1 = (bf16[4,512,128]{2,1,0:T(8,128)(2,1)S(1)}, bf16[4,512,128]{2,1,0:T(8,128)(2,1)S(1)}, f32[2,4,512,128]{3,2,1,0:T(8,128)S(1)}, bf16[2,4,256,128]{3,2,1...) custom-call(s32[1]{0:T(128)} %bitcast.place_ref, ...), custom_call_target="tpu_custom_call" | custom-call | flops 5234491392 | bytes 8388608 | tf_op jit(solution)/shard_map/attend/pallas_call | solution.py:317
  78.3 1.9 %collective-permute-start.9 = (bf16[2,4,256,128]{3,2,1,0:T(8,128)(2,1)S(1)}, bf16[2,4,256,128]{3,2,1,0:T(8,128)(2,1)S(1)}, u32[]{:S(2)}, u32[]{:S(2)}) collective-permute-start(bf16[2,4,256,128]{3,2,1,0:T(8,128)(2,1)S(1)} %get-tuple-element.50), channel_id=1, source_target_pairs={{0,2},{2,0},{4,6},{6,4},{8,10},{10,8},{12,14},{14,12},{16,18},{18,... | collective-permute-start | bytes 1572872 | tf_op jit(solution)/shard_map/ppermute | solution.py:31
  80.2 1.9 %collective-permute-start.11 = (bf16[2,4,128,128]{3,2,1,0:T(8,128)(2,1)S(1)}, bf16[2,4,128,128]{3,2,1,0:T(8,128)(2,1)S(1)}, u32[]{:S(2)}, u32[]{:S(2)}) collective-permute-start(bf16[2,4,128,128]{3,2,1,0:T(8,128)(2,1)S(1)} %get-tuple-element.52), channel_id=1, source_target_pairs={{2,10},{6,14},{8,0},{10,18},{12,4},{14,22},{16,8},{18,26},{20,12},... | collective-permute-start | bytes 786440 | tf_op jit(solution)/shard_map/ppermute | solution.py:23
  82.1 3.5 %collective-permute-start.12 = (bf16[2,4,64,128]{3,2,1,0:T(8,128)(2,1)S(1)}, bf16[2,4,64,128]{3,2,1,0:T(8,128)(2,1)S(1)}, u32[]{:S(2)}, u32[]{:S(2)}) collective-permute-start(bf16[2,4,64,128]{3,2,1,0:T(8,128)(2,1)S(1)} %get-tuple-element.53), channel_id=1, source_target_pairs={{2,18},{6,22},{10,26},{14,30},{16,0},{18,34},{20,4},{22,38},{24,8}... | collective-permute-start | bytes 393224 | tf_op jit(solution)/shard_map/ppermute | solution.py:23
  85.6 10.5 %collective-permute-start.8 = (bf16[2,4,256,128]{3,2,1,0:T(8,128)(2,1)S(1)}, bf16[2,4,256,128]{3,2,1,0:T(8,128)(2,1)S(1)}, u32[]{:S(2)}, u32[]{:S(2)}) collective-permute-start(bf16[2,4,256,128]{3,2,1,0:T(8,128)(2,1)S(1)} %get-tuple-element.49), channel_id=1, source_target_pairs={{2,4},{4,2},{6,8},{8,6},{10,12},{12,10},{14,16},{16,14},{18,20},{2... | collective-permute-start | bytes 1572872 | tf_op jit(solution)/shard_map/ppermute | solution.py:31
  96.1 4.4 %collective-permute-start.10 = (bf16[2,4,256,128]{3,2,1,0:T(8,128)(2,1)S(1)}, bf16[2,4,256,128]{3,2,1,0:T(8,128)(2,1)S(1)}, u32[]{:S(2)}, u32[]{:S(2)}) collective-permute-start(bf16[2,4,256,128]{3,2,1,0:T(8,128)(2,1)S(1)} %get-tuple-element.51), channel_id=1, source_target_pairs={{2,6},{4,0},{6,10},{8,4},{10,14},{12,8},{14,18},{16,12},{18,22},{2... | collective-permute-start | bytes 1572872 | tf_op jit(solution)/shard_map/ppermute | solution.py:23
  100.6 0.3 collective-permute-done.12.refs_4_.refs_2_
  100.9 0.1 later.3
  100.9 6.5 %collective-permute-start.13 = (bf16[2,4,256,128]{3,2,1,0:T(8,128)(2,1)S(1)}, bf16[2,4,256,128]{3,2,1,0:T(8,128)(2,1)S(1)}, u32[]{:S(2)}, u32[]{:S(2)}) collective-permute-start(bf16[2,4,256,128]{3,2,1,0:T(8,128)(2,1)S(1)} %get-tuple-element.57), channel_id=1, source_target_pairs={{0,4},{4,8},{6,2},{8,12},{10,6},{12,16},{14,10},{16,20},{18,14},{2... | collective-permute-start | bytes 1572872 | tf_op jit(solution)/shard_map/ppermute | solution.py:23
  107.4 1.9 %collective-permute-start.14 = (bf16[2,4,128,128]{3,2,1,0:T(8,128)(2,1)S(1)}, bf16[2,4,128,128]{3,2,1,0:T(8,128)(2,1)S(1)}, u32[]{:S(2)}, u32[]{:S(2)}) collective-permute-start(bf16[2,4,128,128]{3,2,1,0:T(8,128)(2,1)S(1)} %get-tuple-element.58), channel_id=1, source_target_pairs={{0,8},{4,12},{8,16},{10,2},{12,20},{14,6},{16,24},{18,10},{20,28},... | collective-permute-start | bytes 786440 | tf_op jit(solution)/shard_map/ppermute | solution.py:23
  109.3 2.8 %collective-permute-start.15 = (bf16[2,4,64,128]{3,2,1,0:T(8,128)(2,1)S(1)}, bf16[2,4,64,128]{3,2,1,0:T(8,128)(2,1)S(1)}, u32[]{:S(2)}, u32[]{:S(2)}) collective-permute-start(bf16[2,4,64,128]{3,2,1,0:T(8,128)(2,1)S(1)} %get-tuple-element.59), channel_id=1, source_target_pairs={{0,16},{4,20},{8,24},{12,28},{16,32},{18,2},{20,36},{22,6},{24,40}... | collective-permute-start | bytes 393224 | tf_op jit(solution)/shard_map/ppermute | solution.py:23
  112.1 1.2 join.1
  113.3 1.3 %collective-permute-done.10.refs_0_ = bf16[2,4,256,128]{3,2,1,0:T(8,128)(2,1)S(1)} collective-permute-done((bf16[2,4,256,128]{3,2,1,0:T(8,128)(2,1)S(1)}, bf16[2,4,256,128]{3,2,1,0:T(8,128)(2,1)S(1)}, u32[]{:S(2)}, u32[]{:S(2)}) %collective-permute-start.10) | collective-permute-done | bytes 524320 | tf_op jit(solution)/shard_map/ppermute | solution.py:23
  114.7 16.4 %collective-permute-done.15.refs_5_ = bf16[2,4,64,128]{3,2,1,0:T(8,128)(2,1)S(1)} collective-permute-done((bf16[2,4,64,128]{3,2,1,0:T(8,128)(2,1)S(1)}, bf16[2,4,64,128]{3,2,1,0:T(8,128)(2,1)S(1)}, u32[]{:S(2)}, u32[]{:S(2)}) %collective-permute-start.15) | collective-permute-done | bytes 131104 | tf_op jit(solution)/shard_map/ppermute | solution.py:23
  131.1 2.0 %gather.1 = (bf16[2048,128]{1,0:T(8,128)(2,1)}, bf16[2048,128]{1,0:T(8,128)(2,1)}) custom-call(s32[1]{0:T(128)} %bitcast.place_ref, f32[2,4,512,128]{3,2,1,0:T(8,128)S(1)} %get-tuple-element.48.own, bf16[2,4,256,128]{3,2,1,0:T(8,128)(2,1)S(1)} %collective-permute-done.8.outer, bf16[2,4,256,128]{3,2,1,0:T(8,128)(2,1)S(1)} %collective-permute-done.9.refs_5_.inner, ...), custom_call_target="tpu_custom_call" | custom-call | bytes 8388608 | tf_op jit(solution)/shard_map/gather/pallas_call | solution.py:409
  (15 shorter events, 0.0 us)
Async XLA Ops:
  0.6 1.0 copy-start
  1.7 1.0 copy-start.1
  2.7 43.2 %copy-start.2 = (bf16[512,4,128]{2,1,0:T(4,128)(2,1)S(1)}, bf16[512,4,128]{2,1,0:T(4,128)(2,1)}, u32[]{:S(2)}) copy-start(bf16[512,4,128]{2,1,0:T(4,128)(2,1)} %param.4) | copy-start | bytes 1572868
  2.7 43.3 %copy-start.3 = (bf16[512,4,128]{2,1,0:T(4,128)(2,1)S(1)}, bf16[512,4,128]{2,1,0:T(4,128)(2,1)}, u32[]{:S(2)}) copy-start(bf16[512,4,128]{2,1,0:T(4,128)(2,1)} %param.7) | copy-start | bytes 1572868
  3.6 27.6 %collective-permute-start.1 = (bf16[2,4,256,128]{3,2,1,0:T(8,128)(2,1)S(1)}, bf16[2,4,256,128]{3,2,1,0:T(8,128)(2,1)S(1)}, u32[]{:S(2)}, u32[]{:S(2)}) collective-permute-start(bf16[2,4,256,128]{3,2,1,0:T(8,128)(2,1)S(1)} %get-tuple-element.37.inner), channel_id=1, source_target_pairs={{0,2},{2,0},{4,6},{6,4},{8,10},{10,8},{12,14},{14,12},{16,18},{18,... | collective-permute-start | bytes 1572872 | tf_op jit(solution)/shard_map/ppermute | solution.py:31
  6.2 25.0 %collective-permute-start.2 = (bf16[2,4,128,128]{3,2,1,0:T(8,128)(2,1)S(1)}, bf16[2,4,128,128]{3,2,1,0:T(8,128)(2,1)S(1)}, u32[]{:S(2)}, u32[]{:S(2)}) collective-permute-start(bf16[2,4,128,128]{3,2,1,0:T(8,128)(2,1)S(1)} %get-tuple-element.39.refs_1_), channel_id=1, source_target_pairs={{2,10},{6,14},{8,0},{10,18},{12,4},{14,22},{16,8},{18,26},{20,12},... | collective-permute-start | bytes 786440 | tf_op jit(solution)/shard_map/ppermute | solution.py:23
  11.1 20.1 %collective-permute-start.3 = (bf16[2,4,64,128]{3,2,1,0:T(8,128)(2,1)S(1)}, bf16[2,4,64,128]{3,2,1,0:T(8,128)(2,1)S(1)}, u32[]{:S(2)}, u32[]{:S(2)}) collective-permute-start(bf16[2,4,64,128]{3,2,1,0:T(8,128)(2,1)S(1)} %get-tuple-element.40.refs_2_), channel_id=1, source_target_pairs={{2,18},{6,22},{10,26},{14,30},{16,0},{18,34},{20,4},{22,38},{24,8}... | collective-permute-start | bytes 393224 | tf_op jit(solution)/shard_map/ppermute | solution.py:23
  19.9 27.0 %collective-permute-start = (bf16[2,4,256,128]{3,2,1,0:T(8,128)(2,1)S(1)}, bf16[2,4,256,128]{3,2,1,0:T(8,128)(2,1)S(1)}, u32[]{:S(2)}, u32[]{:S(2)}) collective-permute-start(bf16[2,4,256,128]{3,2,1,0:T(8,128)(2,1)S(1)} %get-tuple-element.36.outer), channel_id=1, source_target_pairs={{2,4},{4,2},{6,8},{8,6},{10,12},{12,10},{14,16},{16,14},{18,20},{2... | collective-permute-start | bytes 1572872 | tf_op jit(solution)/shard_map/ppermute | solution.py:31
  28.7 21.3 %collective-permute-start.7 = (bf16[2,4,256,128]{3,2,1,0:T(8,128)(2,1)S(1)}, bf16[2,4,256,128]{3,2,1,0:T(8,128)(2,1)S(1)}, u32[]{:S(2)}, u32[]{:S(2)}) collective-permute-start(bf16[2,4,256,128]{3,2,1,0:T(8,128)(2,1)S(1)} %get-tuple-element.38.refs_0_), channel_id=1, source_target_pairs={{2,6},{4,0},{6,10},{8,4},{10,14},{12,8},{14,18},{16,12},{18,22},{2... | collective-permute-start | bytes 1572872 | tf_op jit(solution)/shard_map/ppermute | solution.py:23
  31.3 29.5 %collective-permute-start.4 = (bf16[2,4,256,128]{3,2,1,0:T(8,128)(2,1)S(1)}, bf16[2,4,256,128]{3,2,1,0:T(8,128)(2,1)S(1)}, u32[]{:S(2)}, u32[]{:S(2)}) collective-permute-start(bf16[2,4,256,128]{3,2,1,0:T(8,128)(2,1)S(1)} %get-tuple-element.41), channel_id=1, source_target_pairs={{0,4},{4,8},{6,2},{8,12},{10,6},{12,16},{14,10},{16,20},{18,14},{2... | collective-permute-start | bytes 1572872 | tf_op jit(solution)/shard_map/ppermute | solution.py:23
  38.8 21.9 %collective-permute-start.5 = (bf16[2,4,128,128]{3,2,1,0:T(8,128)(2,1)S(1)}, bf16[2,4,128,128]{3,2,1,0:T(8,128)(2,1)S(1)}, u32[]{:S(2)}, u32[]{:S(2)}) collective-permute-start(bf16[2,4,128,128]{3,2,1,0:T(8,128)(2,1)S(1)} %get-tuple-element.42), channel_id=1, source_target_pairs={{0,8},{4,12},{8,16},{10,2},{12,20},{14,6},{16,24},{18,10},{20,28},... | collective-permute-start | bytes 786440 | tf_op jit(solution)/shard_map/ppermute | solution.py:23
  41.0 19.8 %collective-permute-start.6 = (bf16[2,4,64,128]{3,2,1,0:T(8,128)(2,1)S(1)}, bf16[2,4,64,128]{3,2,1,0:T(8,128)(2,1)S(1)}, u32[]{:S(2)}, u32[]{:S(2)}) collective-permute-start(bf16[2,4,64,128]{3,2,1,0:T(8,128)(2,1)S(1)} %get-tuple-element.43), channel_id=1, source_target_pairs={{0,16},{4,20},{8,24},{12,28},{16,32},{18,2},{20,36},{22,6},{24,40}... | collective-permute-start | bytes 393224 | tf_op jit(solution)/shard_map/ppermute | solution.py:23
  78.3 22.6 %collective-permute-start.9 = (bf16[2,4,256,128]{3,2,1,0:T(8,128)(2,1)S(1)}, bf16[2,4,256,128]{3,2,1,0:T(8,128)(2,1)S(1)}, u32[]{:S(2)}, u32[]{:S(2)}) collective-permute-start(bf16[2,4,256,128]{3,2,1,0:T(8,128)(2,1)S(1)} %get-tuple-element.50), channel_id=1, source_target_pairs={{0,2},{2,0},{4,6},{6,4},{8,10},{10,8},{12,14},{14,12},{16,18},{18,... | collective-permute-start | bytes 1572872 | tf_op jit(solution)/shard_map/ppermute | solution.py:31
  80.2 20.7 %collective-permute-start.11 = (bf16[2,4,128,128]{3,2,1,0:T(8,128)(2,1)S(1)}, bf16[2,4,128,128]{3,2,1,0:T(8,128)(2,1)S(1)}, u32[]{:S(2)}, u32[]{:S(2)}) collective-permute-start(bf16[2,4,128,128]{3,2,1,0:T(8,128)(2,1)S(1)} %get-tuple-element.52), channel_id=1, source_target_pairs={{2,10},{6,14},{8,0},{10,18},{12,4},{14,22},{16,8},{18,26},{20,12},... | collective-permute-start | bytes 786440 | tf_op jit(solution)/shard_map/ppermute | solution.py:23
  82.1 18.7 %collective-permute-start.12 = (bf16[2,4,64,128]{3,2,1,0:T(8,128)(2,1)S(1)}, bf16[2,4,64,128]{3,2,1,0:T(8,128)(2,1)S(1)}, u32[]{:S(2)}, u32[]{:S(2)}) collective-permute-start(bf16[2,4,64,128]{3,2,1,0:T(8,128)(2,1)S(1)} %get-tuple-element.53), channel_id=1, source_target_pairs={{2,18},{6,22},{10,26},{14,30},{16,0},{18,34},{20,4},{22,38},{24,8}... | collective-permute-start | bytes 393224 | tf_op jit(solution)/shard_map/ppermute | solution.py:23
  85.6 27.7 %collective-permute-start.8 = (bf16[2,4,256,128]{3,2,1,0:T(8,128)(2,1)S(1)}, bf16[2,4,256,128]{3,2,1,0:T(8,128)(2,1)S(1)}, u32[]{:S(2)}, u32[]{:S(2)}) collective-permute-start(bf16[2,4,256,128]{3,2,1,0:T(8,128)(2,1)S(1)} %get-tuple-element.49), channel_id=1, source_target_pairs={{2,4},{4,2},{6,8},{8,6},{10,12},{12,10},{14,16},{16,14},{18,20},{2... | collective-permute-start | bytes 1572872 | tf_op jit(solution)/shard_map/ppermute | solution.py:31
  96.1 18.6 %collective-permute-start.10 = (bf16[2,4,256,128]{3,2,1,0:T(8,128)(2,1)S(1)}, bf16[2,4,256,128]{3,2,1,0:T(8,128)(2,1)S(1)}, u32[]{:S(2)}, u32[]{:S(2)}) collective-permute-start(bf16[2,4,256,128]{3,2,1,0:T(8,128)(2,1)S(1)} %get-tuple-element.51), channel_id=1, source_target_pairs={{2,6},{4,0},{6,10},{8,4},{10,14},{12,8},{14,18},{16,12},{18,22},{2... | collective-permute-start | bytes 1572872 | tf_op jit(solution)/shard_map/ppermute | solution.py:23
  100.9 30.2 %collective-permute-start.13 = (bf16[2,4,256,128]{3,2,1,0:T(8,128)(2,1)S(1)}, bf16[2,4,256,128]{3,2,1,0:T(8,128)(2,1)S(1)}, u32[]{:S(2)}, u32[]{:S(2)}) collective-permute-start(bf16[2,4,256,128]{3,2,1,0:T(8,128)(2,1)S(1)} %get-tuple-element.57), channel_id=1, source_target_pairs={{0,4},{4,8},{6,2},{8,12},{10,6},{12,16},{14,10},{16,20},{18,14},{2... | collective-permute-start | bytes 1572872 | tf_op jit(solution)/shard_map/ppermute | solution.py:23
  107.4 23.7 %collective-permute-start.14 = (bf16[2,4,128,128]{3,2,1,0:T(8,128)(2,1)S(1)}, bf16[2,4,128,128]{3,2,1,0:T(8,128)(2,1)S(1)}, u32[]{:S(2)}, u32[]{:S(2)}) collective-permute-start(bf16[2,4,128,128]{3,2,1,0:T(8,128)(2,1)S(1)} %get-tuple-element.58), channel_id=1, source_target_pairs={{0,8},{4,12},{8,16},{10,2},{12,20},{14,6},{16,24},{18,10},{20,28},... | collective-permute-start | bytes 786440 | tf_op jit(solution)/shard_map/ppermute | solution.py:23
  109.3 21.8 %collective-permute-start.15 = (bf16[2,4,64,128]{3,2,1,0:T(8,128)(2,1)S(1)}, bf16[2,4,64,128]{3,2,1,0:T(8,128)(2,1)S(1)}, u32[]{:S(2)}, u32[]{:S(2)}) collective-permute-start(bf16[2,4,64,128]{3,2,1,0:T(8,128)(2,1)S(1)} %get-tuple-element.59), channel_id=1, source_target_pairs={{0,16},{4,20},{8,24},{12,28},{16,32},{18,2},{20,36},{22,6},{24,40}... | collective-permute-start | bytes 393224 | tf_op jit(solution)/shard_map/ppermute | solution.py:23

commit v6 on v5

--- a/solution.py
+++ b/solution.py
@@ -29,10 +29,6 @@
     if across:
         pairs = [(at, at + 1 if at % 2 else at - 1) for at in range(count)]
     return lax.ppermute(value, "seq", [(at, to) for at, to in pairs if 0 <= to < count])
-
-
-def nt(left, right):
-    return lax.dot_general(left, right, (((1,), (1,)), ((), ())), preferred_element_type=F32)
 
 
 def nn(left, right):
@@ -137,15 +133,18 @@
     return down, up, rims
 
 
-def split_qd_kernel(heads, place_ref, q_ref, d_ref, q_out, d_out, rep_out, wide, sums, spread):
+def split_qd_kernel(heads, place_ref, q_ref, d_ref, *refs):
+    q_out, d_out, rep_out, q_turn, d_turn, rep_turn, wide, sums, spread = refs
     span = q_out.shape[1]
     odd = lax.rem(place_ref[0], 2)
     turned(wide, d_ref, odd)
     for head in range(heads):
         d_out[head] = wide[pl.ds(head, span, stride=heads), :].astype(BF)
+        d_turn[head] = d_out[head].T
     turned(wide, q_ref, odd)
     for head in range(heads):
         q_out[head] = wide[pl.ds(head, span, stride=heads), :].astype(BF)
+        q_turn[head] = q_out[head].T
         total = pair_sums(wide, head, span // 2, heads)
         for level in range(LEVELS):
             factor = 2 ** (level + 1)
@@ -153,6 +152,7 @@
             for row in range(factor):
                 spread[pl.ds(row, span // factor, stride=factor), :] = mean
             rep_out[level, head] = spread[...].astype(BF)
+            rep_turn[level, head] = rep_out[level, head].T
             if level + 1 < LEVELS:
                 total = next_sums(sums, total)
 
@@ -164,6 +164,9 @@
             shape((heads, span, 128)),
             shape((heads, span, 128)),
             shape((LEVELS, heads, span, 128)),
+            shape((heads, 128, span)),
+            shape((heads, 128, span)),
+            shape((LEVELS, heads, 128, span)),
         ],
         in_specs=[SMEM_SPEC] + [VMEM_SPEC] * 2,
         scratch_shapes=[
@@ -184,7 +187,10 @@
     return result
 
 
-def attend_kernel(count, place_ref, q_ref, d_ref, rep_ref, outer, inner, rim_out, rim_in, *rest):
+def attend_kernel(
+    count, place_ref, q_ref, d_ref, rep_ref, q_turn, d_turn, rep_turn, outer, inner, *rest
+):
+    rim_out, rim_in, *rest = rest
     crossed_a, crossed_b = rest[:LEVELS], rest[LEVELS : 2 * LEVELS]
     att, gq, own, g_out, g_in = rest[2 * LEVELS : 2 * LEVELS + 5]
     rest = rest[2 * LEVELS + 5 :]
@@ -225,16 +231,16 @@
     met = [segments[:-1], segments[1:]]
     top = [None, None]
     for turn in turns:
-        d_blk = d_ref[0, cols[turn], :]
-        using = [q_ref[0, cols[turn], :]]
-        using += [rep_ref[level, 0, cols[turn], :] for level in range(LEVELS)]
+        d_blk = d_turn[0, :, cols[turn]]
+        using = [q_turn[0, :, cols[turn]]]
+        using += [rep_turn[level, 0, :, cols[turn]] for level in range(LEVELS)]
         for start, size, bias, level in met[turn]:
             here = pl.ds(start, size)
-            s = nt(keys[here, :], using[level])
+            s = nn(keys[here, :], using[level])
             scores[turn, here, :] = s
             high = jnp.max(folded(s, jnp.maximum), axis=0, keepdims=True) * scale2 + bias
             top[turn] = high if top[turn] is None else jnp.maximum(top[turn], high)
-            grads[turn, here, :] = nt(vals[here, :], d_blk)
+            grads[turn, here, :] = nn(vals[here, :], d_blk)
     inverse, delta = [None, None], [None, None]
     for turn in turns:
         total = jnp.zeros((8, block), F32)
@@ -302,7 +308,7 @@
                 ref[which, 0, pl.ds(offset, size), :] = value
 
 
-def attend(place, count, q, d, rep, outer, inner, rim_out, rim_in, crossed_a, crossed_b):
+def attend(place, count, q, d, rep, turned_qd, outer, inner, rim_out, rim_in, crossed_a, crossed_b):
     heads, block = inner.shape[1], inner.shape[2]
     span = 2 * block
     sizes = [span // 2 ** (level + 1) for level in range(LEVELS)]
@@ -322,6 +328,9 @@
             head_spec,
             head_spec,
             pl.BlockSpec((LEVELS, 1, span, 128), lambda h: (0, h, 0, 0)),
+            pl.BlockSpec((1, 128, span), lambda h: (h, 0, 0)),
+            pl.BlockSpec((1, 128, span), lambda h: (h, 0, 0)),
+            pl.BlockSpec((LEVELS, 1, 128, span), lambda h: (0, h, 0, 0)),
         ]
         + [pair(block)] * 4
         + [pair(size) for size in sizes] * 2,
@@ -352,7 +361,7 @@
         cost_estimate=pl.CostEstimate(
             flops=flops, bytes_accessed=8 * 2**20, transcendentals=heads * span * width
         ),
-    )(place, q, d, rep, outer, inner, rim_out, rim_in, *crossed_a, *crossed_b)
+    )(place, q, d, rep, *turned_qd, outer, inner, rim_out, rim_in, *crossed_a, *crossed_b)
 
 
 def join_kernel(heads, place_ref, att, gq, att_out, gq_out, wide):
@@ -429,9 +438,9 @@
     q2, k2, v2, d2 = (x.reshape(flat) for x in (query, key, value, dout))
     outer, inner, *coarse = split_kv(place, k2, v2, heads, span)
     crossed_b, crossed_a, rims = exchange(coarse, coarse, outer, inner)
-    qh, dh, rep = split_qd(place, q2, d2, heads, span)
+    qh, dh, rep, *turned_qd = split_qd(place, q2, d2, heads, span)
     att, gq, own, g_out, g_in, *grads = attend(
-        place, count, qh, dh, rep, outer, inner, *rims, crossed_a, crossed_b
+        place, count, qh, dh, rep, turned_qd, outer, inner, *rims, crossed_a, crossed_b
     )
     downs, ups, rims = exchange(grads[:LEVELS], grads[LEVELS:], g_out, g_in)
     attended, grad_query = join(place, att, gq)

time: 134 us -> 133 us (level)
  no operation moved by 1% of the time
where the time goes in v6:
time: 133 us; the launch traced here: 132 us
  starting transfers between devices  75.1 us (56%)
  waiting for transfers between devices  31.9 us (24%)
  Pallas kernels  22.6 us (17%)
  local copies, waits for them, and re-layouts  2.08 us (2%)
    ppermute x12, starting transfers between devices, crossed(): lax.ppermute(value, 'seq', [(at, to) for at, to in pairs if 0 <= to < cou...  51.3 us
    ppermute x12, waiting for transfers between devices, crossed(): lax.ppermute(value, 'seq', [(at, to) for at, to in pairs if 0 <= to < cou...  31.9 us
    ppermute x4, starting transfers between devices, swapped(): lax.ppermute(value, 'seq', [(at, to) for at, to in pairs if 0 <= to < cou...  23.8 us
    pallas_call x1, Pallas kernels, attend(): pl.pallas_call(functools.partial(attend_kernel, count), grid=(heads,), in...  16.8 us
  transfers between devices with their start and end apart: 16, of which 6 were waited for; matrix products, arithmetic and copies ran while one was open for 0% of the time, Pallas kernels for 2%

profile of v6, /device:TPU:25, one launch (start us, length us, event | category | flops | bytes accessed | tf_op | source)
XLA Modules:
  0.0 132.5 jit_solution(15657504400616273168)
XLA Ops:
  0.6 1.0 copy-done
  1.7 1.0 copy-done.1
  2.7 0.9 split_kv.1
  3.6 2.6 %collective-permute-start.1 = (bf16[2,4,256,128]{3,2,1,0:T(8,128)(2,1)S(1)}, bf16[2,4,256,128]{3,2,1,0:T(8,128)(2,1)S(1)}, u32[]{:S(2)}, u32[]{:S(2)}) collective-permute-start(bf16[2,4,256,128]{3,2,1,0:T(8,128)(2,1)S(1)} %get-tuple-element.43.inner), channel_id=1, source_target_pairs={{0,2},{2,0},{4,6},{6,4},{8,10},{10,8},{12,14},{14,12},{16,18},{18,... | collective-permute-start | bytes 1572872 | tf_op jit(solution)/shard_map/ppermute | solution.py:31
  6.2 4.9 %collective-permute-start.2 = (bf16[2,4,128,128]{3,2,1,0:T(8,128)(2,1)S(1)}, bf16[2,4,128,128]{3,2,1,0:T(8,128)(2,1)S(1)}, u32[]{:S(2)}, u32[]{:S(2)}) collective-permute-start(bf16[2,4,128,128]{3,2,1,0:T(8,128)(2,1)S(1)} %get-tuple-element.45.refs_1_), channel_id=1, source_target_pairs={{2,10},{6,14},{8,0},{10,18},{12,4},{14,22},{16,8},{18,26},{20,12},... | collective-permute-start | bytes 786440 | tf_op jit(solution)/shard_map/ppermute | solution.py:23
  11.1 8.8 %collective-permute-start.3 = (bf16[2,4,64,128]{3,2,1,0:T(8,128)(2,1)S(1)}, bf16[2,4,64,128]{3,2,1,0:T(8,128)(2,1)S(1)}, u32[]{:S(2)}, u32[]{:S(2)}) collective-permute-start(bf16[2,4,64,128]{3,2,1,0:T(8,128)(2,1)S(1)} %get-tuple-element.46.refs_2_), channel_id=1, source_target_pairs={{2,18},{6,22},{10,26},{14,30},{16,0},{18,34},{20,4},{22,38},{24,8}... | collective-permute-start | bytes 393224 | tf_op jit(solution)/shard_map/ppermute | solution.py:23
  19.9 8.8 %collective-permute-start = (bf16[2,4,256,128]{3,2,1,0:T(8,128)(2,1)S(1)}, bf16[2,4,256,128]{3,2,1,0:T(8,128)(2,1)S(1)}, u32[]{:S(2)}, u32[]{:S(2)}) collective-permute-start(bf16[2,4,256,128]{3,2,1,0:T(8,128)(2,1)S(1)} %get-tuple-element.42.outer), channel_id=1, source_target_pairs={{2,4},{4,2},{6,8},{8,6},{10,12},{12,10},{14,16},{16,14},{18,20},{2... | collective-permute-start | bytes 1572872 | tf_op jit(solution)/shard_map/ppermute | solution.py:31
  28.7 1.9 %collective-permute-start.7 = (bf16[2,4,256,128]{3,2,1,0:T(8,128)(2,1)S(1)}, bf16[2,4,256,128]{3,2,1,0:T(8,128)(2,1)S(1)}, u32[]{:S(2)}, u32[]{:S(2)}) collective-permute-start(bf16[2,4,256,128]{3,2,1,0:T(8,128)(2,1)S(1)} %get-tuple-element.44.refs_0_), channel_id=1, source_target_pairs={{2,6},{4,0},{6,10},{8,4},{10,14},{12,8},{14,18},{16,12},{18,22},{2... | collective-permute-start | bytes 1572872 | tf_op jit(solution)/shard_map/ppermute | solution.py:23
  30.6 0.6 collective-permute-done.3.refs_4_.rest_7_
  31.2 0.0 collective-permute-done.2.refs_3_.rest_6_
  31.2 0.1 later.2
  31.3 7.5 %collective-permute-start.4 = (bf16[2,4,256,128]{3,2,1,0:T(8,128)(2,1)S(1)}, bf16[2,4,256,128]{3,2,1,0:T(8,128)(2,1)S(1)}, u32[]{:S(2)}, u32[]{:S(2)}) collective-permute-start(bf16[2,4,256,128]{3,2,1,0:T(8,128)(2,1)S(1)} %get-tuple-element.47), channel_id=1, source_target_pairs={{0,4},{4,8},{6,2},{8,12},{10,6},{12,16},{14,10},{16,20},{18,14},{2... | collective-permute-start | bytes 1572872 | tf_op jit(solution)/shard_map/ppermute | solution.py:23
  38.8 2.2 %collective-permute-start.5 = (bf16[2,4,128,128]{3,2,1,0:T(8,128)(2,1)S(1)}, bf16[2,4,128,128]{3,2,1,0:T(8,128)(2,1)S(1)}, u32[]{:S(2)}, u32[]{:S(2)}) collective-permute-start(bf16[2,4,128,128]{3,2,1,0:T(8,128)(2,1)S(1)} %get-tuple-element.48), channel_id=1, source_target_pairs={{0,8},{4,12},{8,16},{10,2},{12,20},{14,6},{16,24},{18,10},{20,28},... | collective-permute-start | bytes 786440 | tf_op jit(solution)/shard_map/ppermute | solution.py:23
  41.0 5.0 %collective-permute-start.6 = (bf16[2,4,64,128]{3,2,1,0:T(8,128)(2,1)S(1)}, bf16[2,4,64,128]{3,2,1,0:T(8,128)(2,1)S(1)}, u32[]{:S(2)}, u32[]{:S(2)}) collective-permute-start(bf16[2,4,64,128]{3,2,1,0:T(8,128)(2,1)S(1)} %get-tuple-element.49), channel_id=1, source_target_pairs={{0,16},{4,20},{8,24},{12,28},{16,32},{18,2},{20,36},{22,6},{24,40}... | collective-permute-start | bytes 393224 | tf_op jit(solution)/shard_map/ppermute | solution.py:23
  46.0 1.6 %split_qd.1 = (bf16[4,512,128]{2,1,0:T(8,128)(2,1)S(1)}, bf16[4,512,128]{2,1,0:T(8,128)(2,1)S(1)}, bf16[3,4,512,128]{3,2,1,0:T(8,128)(2,1)S(1)}, bf16[4,128,512]...) custom-call(s32[1]{0:T(128)} %bitcast.place_ref, ...), custom_call_target="tpu_custom_call" | custom-call | bytes 8388608 | tf_op jit(solution)/shard_map/split_qd/pallas_call | solution.py:161
  47.6 2.4 %collective-permute-done.7.rest_5_ = bf16[2,4,256,128]{3,2,1,0:T(8,128)(2,1)S(1)} collective-permute-done((bf16[2,4,256,128]{3,2,1,0:T(8,128)(2,1)S(1)}, bf16[2,4,256,128]{3,2,1,0:T(8,128)(2,1)S(1)}, u32[]{:S(2)}, u32[]{:S(2)}) %collective-permute-start.7) | collective-permute-done | bytes 524320 | tf_op jit(solution)/shard_map/ppermute | solution.py:23
  50.0 10.8 %collective-permute-done.6.rest_4_ = bf16[2,4,64,128]{3,2,1,0:T(8,128)(2,1)S(1)} collective-permute-done((bf16[2,4,64,128]{3,2,1,0:T(8,128)(2,1)S(1)}, bf16[2,4,64,128]{3,2,1,0:T(8,128)(2,1)S(1)}, u32[]{:S(2)}, u32[]{:S(2)}) %collective-permute-start.6) | collective-permute-done | bytes 131104 | tf_op jit(solution)/shard_map/ppermute | solution.py:23
  60.8 16.8 %attend.1 = (bf16[4,512,128]{2,1,0:T(8,128)(2,1)S(1)}, bf16[4,512,128]{2,1,0:T(8,128)(2,1)S(1)}, f32[2,4,512,128]{3,2,1,0:T(8,128)S(1)}, bf16[2,4,256,128]{3,2,1...) custom-call(s32[1]{0:T(128)} %bitcast.place_ref, ...), custom_call_target="tpu_custom_call" | custom-call | flops 5234491392 | bytes 8388608 | tf_op jit(solution)/shard_map/attend/pallas_call | solution.py:323
  77.6 1.9 %collective-permute-start.9 = (bf16[2,4,256,128]{3,2,1,0:T(8,128)(2,1)S(1)}, bf16[2,4,256,128]{3,2,1,0:T(8,128)(2,1)S(1)}, u32[]{:S(2)}, u32[]{:S(2)}) collective-permute-start(bf16[2,4,256,128]{3,2,1,0:T(8,128)(2,1)S(1)} %get-tuple-element.56), channel_id=1, source_target_pairs={{0,2},{2,0},{4,6},{6,4},{8,10},{10,8},{12,14},{14,12},{16,18},{18,... | collective-permute-start | bytes 1572872 | tf_op jit(solution)/shard_map/ppermute | solution.py:31
  79.5 1.9 %collective-permute-start.11 = (bf16[2,4,128,128]{3,2,1,0:T(8,128)(2,1)S(1)}, bf16[2,4,128,128]{3,2,1,0:T(8,128)(2,1)S(1)}, u32[]{:S(2)}, u32[]{:S(2)}) collective-permute-start(bf16[2,4,128,128]{3,2,1,0:T(8,128)(2,1)S(1)} %get-tuple-element.58), channel_id=1, source_target_pairs={{2,10},{6,14},{8,0},{10,18},{12,4},{14,22},{16,8},{18,26},{20,12},... | collective-permute-start | bytes 786440 | tf_op jit(solution)/shard_map/ppermute | solution.py:23
  81.4 3.5 %collective-permute-start.12 = (bf16[2,4,64,128]{3,2,1,0:T(8,128)(2,1)S(1)}, bf16[2,4,64,128]{3,2,1,0:T(8,128)(2,1)S(1)}, u32[]{:S(2)}, u32[]{:S(2)}) collective-permute-start(bf16[2,4,64,128]{3,2,1,0:T(8,128)(2,1)S(1)} %get-tuple-element.59), channel_id=1, source_target_pairs={{2,18},{6,22},{10,26},{14,30},{16,0},{18,34},{20,4},{22,38},{24,8}... | collective-permute-start | bytes 393224 | tf_op jit(solution)/shard_map/ppermute | solution.py:23
  85.0 10.5 %collective-permute-start.8 = (bf16[2,4,256,128]{3,2,1,0:T(8,128)(2,1)S(1)}, bf16[2,4,256,128]{3,2,1,0:T(8,128)(2,1)S(1)}, u32[]{:S(2)}, u32[]{:S(2)}) collective-permute-start(bf16[2,4,256,128]{3,2,1,0:T(8,128)(2,1)S(1)} %get-tuple-element.55), channel_id=1, source_target_pairs={{2,4},{4,2},{6,8},{8,6},{10,12},{12,10},{14,16},{16,14},{18,20},{2... | collective-permute-start | bytes 1572872 | tf_op jit(solution)/shard_map/ppermute | solution.py:31
  95.5 4.4 %collective-permute-start.10 = (bf16[2,4,256,128]{3,2,1,0:T(8,128)(2,1)S(1)}, bf16[2,4,256,128]{3,2,1,0:T(8,128)(2,1)S(1)}, u32[]{:S(2)}, u32[]{:S(2)}) collective-permute-start(bf16[2,4,256,128]{3,2,1,0:T(8,128)(2,1)S(1)} %get-tuple-element.57), channel_id=1, source_target_pairs={{2,6},{4,0},{6,10},{8,4},{10,14},{12,8},{14,18},{16,12},{18,22},{2... | collective-permute-start | bytes 1572872 | tf_op jit(solution)/shard_map/ppermute | solution.py:23
  99.9 0.3 collective-permute-done.12.refs_4_.refs_2_
  100.2 0.1 later.3
  100.2 6.5 %collective-permute-start.13 = (bf16[2,4,256,128]{3,2,1,0:T(8,128)(2,1)S(1)}, bf16[2,4,256,128]{3,2,1,0:T(8,128)(2,1)S(1)}, u32[]{:S(2)}, u32[]{:S(2)}) collective-permute-start(bf16[2,4,256,128]{3,2,1,0:T(8,128)(2,1)S(1)} %get-tuple-element.63), channel_id=1, source_target_pairs={{0,4},{4,8},{6,2},{8,12},{10,6},{12,16},{14,10},{16,20},{18,14},{2... | collective-permute-start | bytes 1572872 | tf_op jit(solution)/shard_map/ppermute | solution.py:23
  106.8 1.9 %collective-permute-start.14 = (bf16[2,4,128,128]{3,2,1,0:T(8,128)(2,1)S(1)}, bf16[2,4,128,128]{3,2,1,0:T(8,128)(2,1)S(1)}, u32[]{:S(2)}, u32[]{:S(2)}) collective-permute-start(bf16[2,4,128,128]{3,2,1,0:T(8,128)(2,1)S(1)} %get-tuple-element.64), channel_id=1, source_target_pairs={{0,8},{4,12},{8,16},{10,2},{12,20},{14,6},{16,24},{18,10},{20,28},... | collective-permute-start | bytes 786440 | tf_op jit(solution)/shard_map/ppermute | solution.py:23
  108.7 2.8 %collective-permute-start.15 = (bf16[2,4,64,128]{3,2,1,0:T(8,128)(2,1)S(1)}, bf16[2,4,64,128]{3,2,1,0:T(8,128)(2,1)S(1)}, u32[]{:S(2)}, u32[]{:S(2)}) collective-permute-start(bf16[2,4,64,128]{3,2,1,0:T(8,128)(2,1)S(1)} %get-tuple-element.65), channel_id=1, source_target_pairs={{0,16},{4,20},{8,24},{12,28},{16,32},{18,2},{20,36},{22,6},{24,40}... | collective-permute-start | bytes 393224 | tf_op jit(solution)/shard_map/ppermute | solution.py:23
  111.4 1.2 join.1
  112.7 1.4 %collective-permute-done.10.refs_0_ = bf16[2,4,256,128]{3,2,1,0:T(8,128)(2,1)S(1)} collective-permute-done((bf16[2,4,256,128]{3,2,1,0:T(8,128)(2,1)S(1)}, bf16[2,4,256,128]{3,2,1,0:T(8,128)(2,1)S(1)}, u32[]{:S(2)}, u32[]{:S(2)}) %collective-permute-start.10) | collective-permute-done | bytes 524320 | tf_op jit(solution)/shard_map/ppermute | solution.py:23
  114.0 16.5 %collective-permute-done.15.refs_5_ = bf16[2,4,64,128]{3,2,1,0:T(8,128)(2,1)S(1)} collective-permute-done((bf16[2,4,64,128]{3,2,1,0:T(8,128)(2,1)S(1)}, bf16[2,4,64,128]{3,2,1,0:T(8,128)(2,1)S(1)}, u32[]{:S(2)}, u32[]{:S(2)}) %collective-permute-start.15) | collective-permute-done | bytes 131104 | tf_op jit(solution)/shard_map/ppermute | solution.py:23
  130.5 2.0 %gather.1 = (bf16[2048,128]{1,0:T(8,128)(2,1)}, bf16[2048,128]{1,0:T(8,128)(2,1)}) custom-call(s32[1]{0:T(128)} %bitcast.place_ref, f32[2,4,512,128]{3,2,1,0:T(8,128)S(1)} %get-tuple-element.54.own, bf16[2,4,256,128]{3,2,1,0:T(8,128)(2,1)S(1)} %collective-permute-done.8.outer, bf16[2,4,256,128]{3,2,1,0:T(8,128)(2,1)S(1)} %collective-permute-done.9.refs_5_.inner, ...), custom_call_target="tpu_custom_call" | custom-call | bytes 8388608 | tf_op jit(solution)/shard_map/gather/pallas_call | solution.py:418
  (15 shorter events, 0.0 us)
Async XLA Ops:
  0.6 1.0 copy-start
  1.7 1.0 copy-start.1
  2.7 43.2 %copy-start.2 = (bf16[512,4,128]{2,1,0:T(4,128)(2,1)S(1)}, bf16[512,4,128]{2,1,0:T(4,128)(2,1)}, u32[]{:S(2)}) copy-start(bf16[512,4,128]{2,1,0:T(4,128)(2,1)} %param.4) | copy-start | bytes 1572868
  2.7 43.3 %copy-start.3 = (bf16[512,4,128]{2,1,0:T(4,128)(2,1)S(1)}, bf16[512,4,128]{2,1,0:T(4,128)(2,1)}, u32[]{:S(2)}) copy-start(bf16[512,4,128]{2,1,0:T(4,128)(2,1)} %param.7) | copy-start | bytes 1572868
  3.6 27.6 %collective-permute-start.1 = (bf16[2,4,256,128]{3,2,1,0:T(8,128)(2,1)S(1)}, bf16[2,4,256,128]{3,2,1,0:T(8,128)(2,1)S(1)}, u32[]{:S(2)}, u32[]{:S(2)}) collective-permute-start(bf16[2,4,256,128]{3,2,1,0:T(8,128)(2,1)S(1)} %get-tuple-element.43.inner), channel_id=1, source_target_pairs={{0,2},{2,0},{4,6},{6,4},{8,10},{10,8},{12,14},{14,12},{16,18},{18,... | collective-permute-start | bytes 1572872 | tf_op jit(solution)/shard_map/ppermute | solution.py:31
  6.2 25.0 %collective-permute-start.2 = (bf16[2,4,128,128]{3,2,1,0:T(8,128)(2,1)S(1)}, bf16[2,4,128,128]{3,2,1,0:T(8,128)(2,1)S(1)}, u32[]{:S(2)}, u32[]{:S(2)}) collective-permute-start(bf16[2,4,128,128]{3,2,1,0:T(8,128)(2,1)S(1)} %get-tuple-element.45.refs_1_), channel_id=1, source_target_pairs={{2,10},{6,14},{8,0},{10,18},{12,4},{14,22},{16,8},{18,26},{20,12},... | collective-permute-start | bytes 786440 | tf_op jit(solution)/shard_map/ppermute | solution.py:23
  11.1 20.1 %collective-permute-start.3 = (bf16[2,4,64,128]{3,2,1,0:T(8,128)(2,1)S(1)}, bf16[2,4,64,128]{3,2,1,0:T(8,128)(2,1)S(1)}, u32[]{:S(2)}, u32[]{:S(2)}) collective-permute-start(bf16[2,4,64,128]{3,2,1,0:T(8,128)(2,1)S(1)} %get-tuple-element.46.refs_2_), channel_id=1, source_target_pairs={{2,18},{6,22},{10,26},{14,30},{16,0},{18,34},{20,4},{22,38},{24,8}... | collective-permute-start | bytes 393224 | tf_op jit(solution)/shard_map/ppermute | solution.py:23
  19.9 27.7 %collective-permute-start = (bf16[2,4,256,128]{3,2,1,0:T(8,128)(2,1)S(1)}, bf16[2,4,256,128]{3,2,1,0:T(8,128)(2,1)S(1)}, u32[]{:S(2)}, u32[]{:S(2)}) collective-permute-start(bf16[2,4,256,128]{3,2,1,0:T(8,128)(2,1)S(1)} %get-tuple-element.42.outer), channel_id=1, source_target_pairs={{2,4},{4,2},{6,8},{8,6},{10,12},{12,10},{14,16},{16,14},{18,20},{2... | collective-permute-start | bytes 1572872 | tf_op jit(solution)/shard_map/ppermute | solution.py:31
  28.7 21.3 %collective-permute-start.7 = (bf16[2,4,256,128]{3,2,1,0:T(8,128)(2,1)S(1)}, bf16[2,4,256,128]{3,2,1,0:T(8,128)(2,1)S(1)}, u32[]{:S(2)}, u32[]{:S(2)}) collective-permute-start(bf16[2,4,256,128]{3,2,1,0:T(8,128)(2,1)S(1)} %get-tuple-element.44.refs_0_), channel_id=1, source_target_pairs={{2,6},{4,0},{6,10},{8,4},{10,14},{12,8},{14,18},{16,12},{18,22},{2... | collective-permute-start | bytes 1572872 | tf_op jit(solution)/shard_map/ppermute | solution.py:23
  31.3 29.5 %collective-permute-start.4 = (bf16[2,4,256,128]{3,2,1,0:T(8,128)(2,1)S(1)}, bf16[2,4,256,128]{3,2,1,0:T(8,128)(2,1)S(1)}, u32[]{:S(2)}, u32[]{:S(2)}) collective-permute-start(bf16[2,4,256,128]{3,2,1,0:T(8,128)(2,1)S(1)} %get-tuple-element.47), channel_id=1, source_target_pairs={{0,4},{4,8},{6,2},{8,12},{10,6},{12,16},{14,10},{16,20},{18,14},{2... | collective-permute-start | bytes 1572872 | tf_op jit(solution)/shard_map/ppermute | solution.py:23
  38.8 21.9 %collective-permute-start.5 = (bf16[2,4,128,128]{3,2,1,0:T(8,128)(2,1)S(1)}, bf16[2,4,128,128]{3,2,1,0:T(8,128)(2,1)S(1)}, u32[]{:S(2)}, u32[]{:S(2)}) collective-permute-start(bf16[2,4,128,128]{3,2,1,0:T(8,128)(2,1)S(1)} %get-tuple-element.48), channel_id=1, source_target_pairs={{0,8},{4,12},{8,16},{10,2},{12,20},{14,6},{16,24},{18,10},{20,28},... | collective-permute-start | bytes 786440 | tf_op jit(solution)/shard_map/ppermute | solution.py:23
  41.0 19.8 %collective-permute-start.6 = (bf16[2,4,64,128]{3,2,1,0:T(8,128)(2,1)S(1)}, bf16[2,4,64,128]{3,2,1,0:T(8,128)(2,1)S(1)}, u32[]{:S(2)}, u32[]{:S(2)}) collective-permute-start(bf16[2,4,64,128]{3,2,1,0:T(8,128)(2,1)S(1)} %get-tuple-element.49), channel_id=1, source_target_pairs={{0,16},{4,20},{8,24},{12,28},{16,32},{18,2},{20,36},{22,6},{24,40}... | collective-permute-start | bytes 393224 | tf_op jit(solution)/shard_map/ppermute | solution.py:23
  77.6 22.6 %collective-permute-start.9 = (bf16[2,4,256,128]{3,2,1,0:T(8,128)(2,1)S(1)}, bf16[2,4,256,128]{3,2,1,0:T(8,128)(2,1)S(1)}, u32[]{:S(2)}, u32[]{:S(2)}) collective-permute-start(bf16[2,4,256,128]{3,2,1,0:T(8,128)(2,1)S(1)} %get-tuple-element.56), channel_id=1, source_target_pairs={{0,2},{2,0},{4,6},{6,4},{8,10},{10,8},{12,14},{14,12},{16,18},{18,... | collective-permute-start | bytes 1572872 | tf_op jit(solution)/shard_map/ppermute | solution.py:31
  79.5 20.7 %collective-permute-start.11 = (bf16[2,4,128,128]{3,2,1,0:T(8,128)(2,1)S(1)}, bf16[2,4,128,128]{3,2,1,0:T(8,128)(2,1)S(1)}, u32[]{:S(2)}, u32[]{:S(2)}) collective-permute-start(bf16[2,4,128,128]{3,2,1,0:T(8,128)(2,1)S(1)} %get-tuple-element.58), channel_id=1, source_target_pairs={{2,10},{6,14},{8,0},{10,18},{12,4},{14,22},{16,8},{18,26},{20,12},... | collective-permute-start | bytes 786440 | tf_op jit(solution)/shard_map/ppermute | solution.py:23
  81.4 18.7 %collective-permute-start.12 = (bf16[2,4,64,128]{3,2,1,0:T(8,128)(2,1)S(1)}, bf16[2,4,64,128]{3,2,1,0:T(8,128)(2,1)S(1)}, u32[]{:S(2)}, u32[]{:S(2)}) collective-permute-start(bf16[2,4,64,128]{3,2,1,0:T(8,128)(2,1)S(1)} %get-tuple-element.59), channel_id=1, source_target_pairs={{2,18},{6,22},{10,26},{14,30},{16,0},{18,34},{20,4},{22,38},{24,8}... | collective-permute-start | bytes 393224 | tf_op jit(solution)/shard_map/ppermute | solution.py:23
  85.0 27.7 %collective-permute-start.8 = (bf16[2,4,256,128]{3,2,1,0:T(8,128)(2,1)S(1)}, bf16[2,4,256,128]{3,2,1,0:T(8,128)(2,1)S(1)}, u32[]{:S(2)}, u32[]{:S(2)}) collective-permute-start(bf16[2,4,256,128]{3,2,1,0:T(8,128)(2,1)S(1)} %get-tuple-element.55), channel_id=1, source_target_pairs={{2,4},{4,2},{6,8},{8,6},{10,12},{12,10},{14,16},{16,14},{18,20},{2... | collective-permute-start | bytes 1572872 | tf_op jit(solution)/shard_map/ppermute | solution.py:31
  95.5 18.5 %collective-permute-start.10 = (bf16[2,4,256,128]{3,2,1,0:T(8,128)(2,1)S(1)}, bf16[2,4,256,128]{3,2,1,0:T(8,128)(2,1)S(1)}, u32[]{:S(2)}, u32[]{:S(2)}) collective-permute-start(bf16[2,4,256,128]{3,2,1,0:T(8,128)(2,1)S(1)} %get-tuple-element.57), channel_id=1, source_target_pairs={{2,6},{4,0},{6,10},{8,4},{10,14},{12,8},{14,18},{16,12},{18,22},{2... | collective-permute-start | bytes 1572872 | tf_op jit(solution)/shard_map/ppermute | solution.py:23
  100.2 30.2 %collective-permute-start.13 = (bf16[2,4,256,128]{3,2,1,0:T(8,128)(2,1)S(1)}, bf16[2,4,256,128]{3,2,1,0:T(8,128)(2,1)S(1)}, u32[]{:S(2)}, u32[]{:S(2)}) collective-permute-start(bf16[2,4,256,128]{3,2,1,0:T(8,128)(2,1)S(1)} %get-tuple-element.63), channel_id=1, source_target_pairs={{0,4},{4,8},{6,2},{8,12},{10,6},{12,16},{14,10},{16,20},{18,14},{2... | collective-permute-start | bytes 1572872 | tf_op jit(solution)/shard_map/ppermute | solution.py:23
  106.8 23.7 %collective-permute-start.14 = (bf16[2,4,128,128]{3,2,1,0:T(8,128)(2,1)S(1)}, bf16[2,4,128,128]{3,2,1,0:T(8,128)(2,1)S(1)}, u32[]{:S(2)}, u32[]{:S(2)}) collective-permute-start(bf16[2,4,128,128]{3,2,1,0:T(8,128)(2,1)S(1)} %get-tuple-element.64), channel_id=1, source_target_pairs={{0,8},{4,12},{8,16},{10,2},{12,20},{14,6},{16,24},{18,10},{20,28},... | collective-permute-start | bytes 786440 | tf_op jit(solution)/shard_map/ppermute | solution.py:23
  108.7 21.8 %collective-permute-start.15 = (bf16[2,4,64,128]{3,2,1,0:T(8,128)(2,1)S(1)}, bf16[2,4,64,128]{3,2,1,0:T(8,128)(2,1)S(1)}, u32[]{:S(2)}, u32[]{:S(2)}) collective-permute-start(bf16[2,4,64,128]{3,2,1,0:T(8,128)(2,1)S(1)} %get-tuple-element.65), channel_id=1, source_target_pairs={{0,16},{4,20},{8,24},{12,28},{16,32},{18,2},{20,36},{22,6},{24,40}... | collective-permute-start | bytes 393224 | tf_op jit(solution)/shard_map/ppermute | solution.py:23
